TPU v7x, 128 devices: a whole 4x4x4 slice. The times are simulated.
128 devices in a mesh: bx: 16 (over x, y), by: 8 (over z, core).
Axes of the slice: x: 4, y: 4, z: 4, core: 2. Of those that a mesh axis runs over, the one named last changes fastest.
Arguments:
- tracers: float32 [4, 12, 2048, 2048], P(None, None, 'bx', 'by'), may hold values from -6 to 6
- velocity: float32 [2, 12, 2048, 2048], P(None, None, 'bx', 'by'), may hold values from -0.2 to 0.2
- ocean: int32 [2048, 2048], P('bx', 'by'), may hold values 0 or 1
- thickness: float32 [12], replicated, may hold values from 0.5 to 2
- depth: float32 [2048, 2048], P('bx', 'by'), may hold values from 0.25 to 10, as said below
Outputs:
- new_tracers: float32 [4, 12, 2048, 2048], P(None, None, 'bx', 'by')
- surface_pressure: float32 [2048, 2048], P(('bx', 'by'))
Inputs may be any that keep to these rules, and one draw needn't show every extreme that they name: depth is positive.
All inputs are finite; a program needn't handle non-finite values. No bound on the sum of `ocean` on one device may be relied on, other than what follows from the above.
Results may differ from a plain program's by a relative error of at most 0.00002.
Values sent between devices are 32-bit elements; how exact they have to be, the bound alone decides.
No kernel may reach another device: no remote copies, remote signals or barrier semaphores. Data moves between devices by JAX's collectives and lax.ppermute only.
A program may use at most 128 MiB of HBM per device.

v0:
```python
import jax
import jax.numpy as jnp
from jax import lax
from jax.sharding import PartitionSpec as P

ITERS = 3


NEIGHBOURS = (
    (1, 0, 0.5),
    (-1, 0, 0.5),
    (0, 1, 0.5),
    (0, -1, 0.5),
    (1, 1, 0.125),
    (1, -1, 0.125),
    (-1, 1, 0.125),
    (-1, -1, 0.125),
)


def with_halo(block, sides, width):
    for axis, dim in sides:
        count = lax.axis_size(axis)
        forward = [(i, i + 1) for i in range(count - 1)]
        backward = [(target, source) for source, target in forward]
        low = lax.ppermute(
            lax.slice_in_dim(block, block.shape[dim] - width, None, axis=dim), axis, forward
        )
        high = lax.ppermute(lax.slice_in_dim(block, 0, width, axis=dim), axis, backward)
        block = jnp.concatenate([low, block, high], axis=dim)
    return block


def face_flux(speed, here, ahead, wet_here, wet_ahead):
    return (jnp.maximum(speed, 0.0) * here + jnp.minimum(speed, 0.0) * ahead) * (
        wet_here * wet_ahead
    )


def operate(padded_p, padded_h):
    rows = padded_p.shape[0] - 2
    cols = padded_p.shape[1] - 2
    center_p = padded_p[1 : rows + 1, 1 : cols + 1]
    center_h = padded_h[1 : rows + 1, 1 : cols + 1]
    result = 0.5 * center_p
    for step_a, step_b, weight in NEIGHBOURS:
        near_p = padded_p[1 + step_a : rows + 1 + step_a, 1 + step_b : cols + 1 + step_b]
        near_h = padded_h[1 + step_a : rows + 1 + step_a, 1 + step_b : cols + 1 + step_b]
        result = result + weight * (center_h + near_h) * (center_p - near_p)
    return result


def chebyshev(rhs, apply_fn, lam_max, keep):
    theta = (lam_max + 0.5) / 2.0
    delta = (lam_max - 0.5) / 2.0
    sigma = theta / delta
    rho = 1.0 / sigma
    resid = rhs
    direction = rhs / theta * keep
    solution = jnp.zeros_like(rhs)
    for step in range(ITERS):
        resid = resid - apply_fn(direction)
        solution = solution + direction
        rho_next = 1.0 / (2.0 * sigma - rho)
        direction = (rho_next * rho * direction + 2.0 * rho_next / delta * resid) * keep
        rho = rho_next
    return solution + direction


def shards(tracers, velocity, ocean, thickness, depth):
    count, levels, rows, cols = tracers.shape
    wet = ocean.astype(jnp.float32)
    coefficient = depth * (0.1 + 0.9 * wet)
    lam_max = 0.5 + 10.0 * lax.pmax(jnp.max(coefficient), ("bx", "by"))
    layers = count * levels
    stacked = jnp.concatenate(
        [tracers.reshape(layers, rows, cols), velocity.reshape(2 * levels, rows, cols), wet[None]],
        0,
    )
    padded = with_halo(stacked, (("bx", 1), ("by", 2)), 1)
    padded_t = padded[:layers].reshape(count, levels, rows + 2, cols + 2)
    speed_x = padded[layers : layers + levels]
    speed_y = padded[layers + levels : layers + 2 * levels]
    padded_w = padded[layers + 2 * levels]
    flux_x = face_flux(
        speed_x[:, 0 : rows + 1, 1 : cols + 1],
        padded_t[:, :, 0 : rows + 1, 1 : cols + 1],
        padded_t[:, :, 1 : rows + 2, 1 : cols + 1],
        padded_w[0 : rows + 1, 1 : cols + 1],
        padded_w[1 : rows + 2, 1 : cols + 1],
    )
    flux_y = face_flux(
        speed_y[:, 1 : rows + 1, 0 : cols + 1],
        padded_t[:, :, 1 : rows + 1, 0 : cols + 1],
        padded_t[:, :, 1 : rows + 1, 1 : cols + 2],
        padded_w[1 : rows + 1, 0 : cols + 1],
        padded_w[1 : rows + 1, 1 : cols + 2],
    )
    new_tracers = (
        tracers
        - (flux_x[:, :, 1:] - flux_x[:, :, :-1])
        - (flux_y[:, :, :, 1:] - flux_y[:, :, :, :-1])
    )
    forcing = wet * jnp.sum(
        thickness[:, None, None] * (0.2 * new_tracers[0] - 0.8 * new_tracers[1]), axis=0
    )
    strip = lax.all_to_all(
        jnp.stack([forcing, coefficient]), "by", split_axis=1, concat_axis=2, tiled=True
    )
    rhs = strip[0]
    padded_h = jnp.pad(with_halo(strip[1], ((("bx", "by"), 0),), 1), ((0, 0), (1, 1)))

    def apply_fn(direction):
        near = with_halo(direction, ((("bx", "by"), 0),), 1)
        return operate(jnp.pad(near, ((0, 0), (1, 1))), padded_h)

    surface_pressure = chebyshev(rhs, apply_fn, lam_max, 1.0)
    return (new_tracers, surface_pressure)


def solution(mesh):
    return jax.shard_map(
        shards,
        mesh=mesh,
        in_specs=(
            P(None, None, "bx", "by"),
            P(None, None, "bx", "by"),
            P("bx", "by"),
            P(),
            P("bx", "by"),
        ),
        out_specs=(P(None, None, "bx", "by"), P(("bx", "by"), None)),
        check_vma=False,
    )
```

profile of v0, /device:TPU:121, one launch (start us, length us, event | category | flops | bytes accessed | tf_op | source)
XLA Modules:
  0.0 243.8 jit_solution(16242690862136201487)
XLA Ops:
  0.7 1.1 convert_bitcast_fusion
  1.7 1.9 pad_maximum_fusion.21
  3.6 2.9 %collective-permute-start = (f32[73,1,256]{2,1,0:T(1,128)S(1)}, f32[73,1,256]{2,1,0:T(1,128)S(1)}, u32[]{:S(2)}, u32[]{:S(2)}) collective-permute-start(f32[73,1,256]{2,1,0:T(1,128)S(1)} %get-tuple-element.10), channel_id=1, source_target_pairs={{0,8},{8,16},{16,24},{24,32},{32,40},{40,48},{48,56},{56,64},{64,7... | collective-permute-start | bytes 224264 | tf_op jit(solution)/shard_map/ppermute | solution.py:26
  6.6 2.5 %collective-permute-start.1 = (f32[73,1,256]{2,1,0:T(1,128)S(1)}, f32[73,1,256]{2,1,0:T(1,128)S(1)}, u32[]{:S(2)}, u32[]{:S(2)}) collective-permute-start(f32[73,1,256]{2,1,0:T(1,128)S(1)} %get-tuple-element.11), channel_id=1, source_target_pairs={{8,0},{16,8},{24,16},{32,24},{40,32},{48,40},{56,48},{64,56},{72,6... | collective-permute-start | bytes 224264 | tf_op jit(solution)/shard_map/ppermute | solution.py:29
  9.1 4.7 %collective-permute-done.1 = f32[73,1,256]{2,1,0:T(1,128)S(1)} collective-permute-done((f32[73,1,256]{2,1,0:T(1,128)S(1)}, f32[73,1,256]{2,1,0:T(1,128)S(1)}, u32[]{:S(2)}, u32[]{:S(2)}) %collective-permute-start.1) | collective-permute-done | bytes 74784 | tf_op jit(solution)/shard_map/ppermute | solution.py:29
  13.8 8.6 %pad_maximum_fusion.1 = f32[73,130,256]{2,1,0:T(8,128)S(1)} fusion(f32[73,1,256]{2,1,0:T(1,128)S(1)} %collective-permute-done.1, f32[1,128,256]{2,1,0:T(8,128)S(1)} %convert_bitcast_fusion, f32[24,128,256]{2,1,0:T(8,128)S(1)} %bitcast.42, f32[48,128,256]{2,1,0:T(8,128)S(1)} %bitcast.31, f32[73,1,256]{2,1,0:T(1,128)S(1)} %collective-permute-done), kind=kLoop, calls=%fused_computation.1 | loop fusion | flops 9717760 | bytes 19435520 | tf_op jit(solution)/shard_map/concatenate | solution.py:30
  22.4 5.6 %fusion.84 = (f32[73,130,1]{2,1,0:T(8,128)}, f32[73,130,1]{2,1,0:T(8,128)}) fusion(f32[73,130,256]{2,1,0:T(8,128)S(1)} %pad_maximum_fusion.1), kind=kLoop, calls=%fused_computation.160 | loop fusion | bytes 151840 | tf_op jit(solution)/shard_map/slice | solution.py:27
  28.0 4.3 %copy.21 = f32[73,130,1]{0,2,1:T(1,128)} copy(f32[73,130,1]{2,1,0:T(8,128)} %get-tuple-element.8) | data formatting | bytes 75920 | tf_op jit(solution)/shard_map/slice | solution.py:27
  32.3 3.8 %copy.22 = f32[73,130,1]{0,2,1:T(1,128)S(1)} copy(f32[73,130,1]{2,1,0:T(8,128)} %get-tuple-element.9) | data formatting | bytes 75920 | tf_op jit(solution)/shard_map/slice | solution.py:29
  36.1 4.6 %collective-permute-start.3 = (f32[73,130,1]{0,2,1:T(1,128)S(1)}, f32[73,130,1]{0,2,1:T(1,128)}, u32[]{:S(2)}, u32[]{:S(2)}) collective-permute-start(f32[73,130,1]{0,2,1:T(1,128)S(1)} %copy.22), channel_id=1, source_target_pairs={{1,0},{2,1},{3,2},{4,3},{5,4},{6,5},{7,6},{9,8},{10,9},{11,10},{12... | collective-permute-start | bytes 113888 | tf_op jit(solution)/shard_map/ppermute | solution.py:29
  40.7 1.3 collective-permute-start.2
  42.0 1.4 broadcast_maximum_fusion.1
  43.4 1.3 broadcast_minimum_fusion.1
  44.7 4.3 %copy.23 = f32[73,130,1]{2,1,0:T(8,128)} copy(f32[73,130,1]{0,2,1:T(1,128)} %collective-permute-done.2) | data formatting | bytes 75920 | tf_op jit(solution)/shard_map/ppermute | solution.py:26
  49.0 4.3 %copy.24 = f32[73,130,1]{2,1,0:T(8,128)} copy(f32[73,130,1]{0,2,1:T(1,128)} %collective-permute-done.3) | data formatting | bytes 75920 | tf_op jit(solution)/shard_map/ppermute | solution.py:29
  53.3 1.2 maximum_bitcast_fusion
  54.8 0.7 slice-done.1
  55.6 1.0 copy-done.2
  56.5 1.4 copy-done.3
  58.0 0.7 broadcast_maximum_fusion
  58.7 0.2 broadcast_minimum_fusion
  58.9 0.5 slice-done.5
  59.5 21.8 %pad_maximum_fusion = f32[73,130,258]{2,1,0:T(8,128)} fusion(f32[73,130,1]{2,1,0:T(8,128)S(1)} %bitcast.47, f32[73,1,256]{2,1,0:T(1,128)S(1)} %collective-permute-done.1, f32[1,128,256]{2,1,0:T(8,128)S(1)} %convert_bitcast_fusion, f32[24,128,256]{2,1,0:T(8,128)S(1)} %bitcast.45, f32[48,128,256]{2,1,0:T(8,128)S(1)} %bitcast.35, ...), kind=kLoop, calls=%fused_computation | loop fusion | flops 14690520 | bytes 19587360 | tf_op jit(solution)/shard_map/concatenate | solution.py:30
  81.3 8.3 %slice.319 = f32[48,130,258]{2,1,0:T(8,128)} slice(f32[73,130,258]{2,1,0:T(8,128)} %pad_maximum_fusion), slice={[0:48], [0:130], [0:258]} | slice | bytes 12879360 | tf_op jit(solution)/shard_map/slice | solution.py:81
  89.6 12.5 %fusion.3 = f32[4,12,129,256]{3,2,1,0:T(8,128)} fusion(f32[4,12,130,258]{3,2,1,0:T(8,128)} %bitcast.36, f32[129,256]{1,0:T(8,128)S(1)} %slice_multiply_fusion.7, f32[12,129,256]{2,1,0:T(8,128)} %broadcast_minimum_fusion.1, f32[12,129,256]{2,1,0:T(8,128)} %get-tuple-element.4), kind=kLoop, calls=%fused_computation.8 | loop fusion | flops 6340608 | bytes 22324224 | tf_op jit(solution)/shard_map/mul | solution.py:35
  102.2 5.9 %fusion.1 = f32[4,12,128,257]{3,2,1,0:T(8,128)} fusion(f32[4,12,130,258]{3,2,1,0:T(8,128)S(1)} %bitcast.39, f32[128,257]{1,0:T(8,128)S(1)} %slice_multiply_fusion.6, f32[12,128,257]{2,1,0:T(8,128)S(1)} %broadcast_minimum_fusion, f32[12,128,257]{2,1,0:T(8,128)S(1)} %get-tuple-element.6), kind=kLoop, calls=%fused_computation.4 | loop fusion | flops 6316032 | bytes 22237696 | tf_op jit(solution)/shard_map/mul | solution.py:35
  108.1 11.2 %fusion.4 = f32[4,12,128,256]{3,2,1,0:T(8,128)S(1)} fusion(f32[4,12,128,257]{3,2,1,0:T(8,128)} %fusion.1, f32[4,12,128,256]{3,2,1,0:T(8,128)S(1)} %bitcast.33, f32[4,12,129,256]{3,2,1,0:T(8,128)} %fusion.3), kind=kLoop, calls=%fused_computation.11 | loop fusion | flops 6291456 | bytes 37748736 | tf_op jit(solution)/shard_map/sub | solution.py:100
  119.3 2.7 %copy-done.4 = f32[4,12,128,256]{3,2,1,0:T(8,128)} copy-done((f32[4,12,128,256]{3,2,1,0:T(8,128)}, f32[4,12,128,256]{3,2,1,0:T(8,128)S(1)}, u32[]{:S(2)}) %copy-start.4) | copy-done | bytes 6291480
  122.0 0.3 fusion.9
  122.3 0.6 fusion.81
  123.0 0.9 copy.26
  123.9 5.4 %all-to-all-start = ((f32[2,128,256]{2,0,1:T(2,128)}), f32[2,128,256]{2,0,1:T(2,128)S(1)}, u32[]{:S(2)}, u32[]{:S(2)}) async-start(f32[2,128,256]{2,0,1:T(2,128)} %copy.26), calls=%async_computation | async-start | bytes 524288 | tf_op jit(solution)/shard_map/all_to_all | solution.py:107
  129.4 62.9 %pmax.7 = f32[]{:T(128)} all-reduce(f32[]{:T(128)} %get-tuple-element.16), channel_id=1, replica_groups=mesh['bx'=16,'by'=8] {'bx','by'}, use_global_device_ids=true, to_apply=%region_2.0 | all-reduce | flops 1 | bytes 8 | tf_op jit(solution)/shard_map/pmax | solution.py:74
  193.7 0.2 fusion.86
  194.1 5.6 %collective-permute-start.7 = (f32[1,2048]{1,0:T(1,128)S(1)}, f32[1,2048]{1,0:T(1,128)S(1)}, u32[]{:S(2)}, u32[]{:S(2)}) collective-permute-start(f32[1,2048]{1,0:T(1,128)S(1)} %get-tuple-element.22), channel_id=1, source_target_pairs={{0,1},{1,2},{2,3},{3,4},{4,5},{5,6},{6,7},{7,8},{8,9},{9,10},{10,1... | collective-permute-start | bytes 24584 | tf_op jit(solution)/shard_map/ppermute | solution.py:26
  199.7 1.9 collective-permute-start.5
  201.8 1.9 collective-permute-start.4
  203.8 7.9 %collective-permute-start.6 = (f32[1,2048]{1,0:T(1,128)S(1)}, f32[1,2048]{1,0:T(1,128)S(1)}, u32[]{:S(2)}, u32[]{:S(2)}) collective-permute-start(f32[1,2048]{1,0:T(1,128)S(1)} %bitcast.60), channel_id=1, source_target_pairs={{0,1},{1,2},{2,3},{3,4},{4,5},{5,6},{6,7},{7,8},{8,9},{9,10},{10,1... | collective-permute-start | bytes 24584 | tf_op jit(solution)/shard_map/ppermute | solution.py:26
  211.8 0.6 collective-permute-done.6
  212.6 0.4 multiply_add_fusion.1
  213.0 8.4 %collective-permute-start.9 = (f32[1,2048]{1,0:T(1,128)S(1)}, f32[1,2048]{1,0:T(1,128)S(1)}, u32[]{:S(2)}, u32[]{:S(2)}) collective-permute-start(f32[1,2048]{1,0:T(1,128)S(1)} %get-tuple-element.20), channel_id=1, source_target_pairs={{0,1},{1,2},{2,3},{3,4},{4,5},{5,6},{6,7},{7,8},{8,9},{9,10},{10,1... | collective-permute-start | bytes 24584 | tf_op jit(solution)/shard_map/ppermute | solution.py:26
  221.4 1.9 collective-permute-start.8
  223.4 7.2 %collective-permute-done.8 = f32[1,2048]{1,0:T(1,128)S(1)} collective-permute-done((f32[1,2048]{1,0:T(1,128)S(1)}, f32[1,2048]{1,0:T(1,128)S(1)}, u32[]{:S(2)}, u32[]{:S(2)}) %collective-permute-start.8) | collective-permute-done | bytes 8224 | tf_op jit(solution)/shard_map/ppermute | solution.py:29
  230.7 0.4 multiply_add_fusion
  231.2 1.9 collective-permute-start.11
  233.1 2.4 collective-permute-start.10
  235.6 6.7 %collective-permute-done.10 = f32[1,2048]{1,0:T(1,128)S(1)} collective-permute-done((f32[1,2048]{1,0:T(1,128)S(1)}, f32[1,2048]{1,0:T(1,128)S(1)}, u32[]{:S(2)}, u32[]{:S(2)}) %collective-permute-start.10) | collective-permute-done | bytes 8224 | tf_op jit(solution)/shard_map/ppermute | solution.py:29
  242.5 1.3 fusion.16
  (53 shorter events, 1.4 us)
Async XLA Ops:
  0.6 13.1 %copy-start = (f32[4,12,128,256]{3,2,1,0:T(8,128)S(1)}, f32[4,12,128,256]{3,2,1,0:T(8,128)}, u32[]{:S(2)}) copy-start(f32[4,12,128,256]{3,2,1,0:T(8,128)} %param.5) | copy-start | bytes 18874372
  0.6 13.1 %copy-start.1 = (f32[2,12,128,256]{3,2,1,0:T(8,128)S(1)}, f32[2,12,128,256]{3,2,1,0:T(8,128)}, u32[]{:S(2)}) copy-start(f32[2,12,128,256]{3,2,1,0:T(8,128)} %param.6) | copy-start | bytes 9437188
  3.6 5.4 %collective-permute-start = (f32[73,1,256]{2,1,0:T(1,128)S(1)}, f32[73,1,256]{2,1,0:T(1,128)S(1)}, u32[]{:S(2)}, u32[]{:S(2)}) collective-permute-start(f32[73,1,256]{2,1,0:T(1,128)S(1)} %get-tuple-element.10), channel_id=1, source_target_pairs={{0,8},{8,16},{16,24},{24,32},{32,40},{40,48},{48,56},{56,64},{64,7... | collective-permute-start | bytes 224264 | tf_op jit(solution)/shard_map/ppermute | solution.py:26
  6.6 7.2 %collective-permute-start.1 = (f32[73,1,256]{2,1,0:T(1,128)S(1)}, f32[73,1,256]{2,1,0:T(1,128)S(1)}, u32[]{:S(2)}, u32[]{:S(2)}) collective-permute-start(f32[73,1,256]{2,1,0:T(1,128)S(1)} %get-tuple-element.11), channel_id=1, source_target_pairs={{8,0},{16,8},{24,16},{32,24},{40,32},{48,40},{56,48},{64,56},{72,6... | collective-permute-start | bytes 224264 | tf_op jit(solution)/shard_map/ppermute | solution.py:29
  36.1 12.9 %collective-permute-start.3 = (f32[73,130,1]{0,2,1:T(1,128)S(1)}, f32[73,130,1]{0,2,1:T(1,128)}, u32[]{:S(2)}, u32[]{:S(2)}) collective-permute-start(f32[73,130,1]{0,2,1:T(1,128)S(1)} %copy.22), channel_id=1, source_target_pairs={{1,0},{2,1},{3,2},{4,3},{5,4},{6,5},{7,6},{9,8},{10,9},{11,10},{12... | collective-permute-start | bytes 113888 | tf_op jit(solution)/shard_map/ppermute | solution.py:29
  40.7 4.0 %collective-permute-start.2 = (f32[73,130,1]{0,2,1:T(1,128)}, f32[73,130,1]{0,2,1:T(1,128)}, u32[]{:S(2)}, u32[]{:S(2)}) collective-permute-start(f32[73,130,1]{0,2,1:T(1,128)} %copy.21), channel_id=1, source_target_pairs={{0,1},{1,2},{2,3},{3,4},{4,5},{5,6},{6,7},{8,9},{9,10},{10,11},{11... | collective-permute-start | bytes 113888 | tf_op jit(solution)/shard_map/ppermute | solution.py:26
  49.0 5.8 %slice-start = ((s8[6291456]{0:T(1024)(128)(4,1)}), s8[2097152]{0:T(1024)(128)(4,1)S(1)}, s32[]{:S(2)}) async-start(s8[6291456]{0:T(1024)(128)(4,1)} %bitcast.32), calls=%async_computation.1 | async-start | bytes 4194304
  53.3 2.3 slice-start.1
  53.3 3.2 %copy-start.2 = (f32[2,12,128,256]{3,2,1,0:T(8,128)S(1)}, f32[2,12,128,256]{3,2,1,0:T(8,128)}, u32[]{:S(2)}) copy-start(f32[2,12,128,256]{3,2,1,0:T(8,128)} %param.6) | copy-start | bytes 9437188
  53.3 4.7 %copy-start.3 = (f32[73,130,1]{2,1,0:T(8,128)S(1)}, f32[73,130,1]{2,1,0:T(8,128)}, u32[]{:S(2)}) copy-start(f32[73,130,1]{2,1,0:T(8,128)} %copy.23) | copy-start | bytes 113884
  54.7 4.7 %slice-start.5 = ((s8[5083136]{0:T(1024)(128)(4,1)}), s8[4194304]{0:T(1024)(128)(4,1)S(1)}, s32[]{:S(2)}) async-start(s8[5083136]{0:T(1024)(128)(4,1)} %bitcast.46), calls=%async_computation.6 | async-start | bytes 8388608
  58.0 1.5 slice-start.6
  89.6 12.5 %slice-start.2 = ((s8[10027008]{0:T(1024)(128)(4,1)}), s8[4194304]{0:T(1024)(128)(4,1)S(1)}, s32[]{:S(2)}) async-start(s8[10027008]{0:T(1024)(128)(4,1)} %bitcast.37), calls=%async_computation.3 | async-start | bytes 8388608
  89.6 12.5 %slice-start.3 = ((s8[10027008]{0:T(1024)(128)(4,1)}), s8[4194304]{0:T(1024)(128)(4,1)S(1)}, s32[]{:S(2)}) async-start(s8[10027008]{0:T(1024)(128)(4,1)} %bitcast.37), calls=%async_computation.4 | async-start | bytes 8388608
  89.6 12.6 %slice-start.4 = ((s8[10027008]{0:T(1024)(128)(4,1)}), s8[1638400]{0:T(1024)(128)(4,1)S(1)}, s32[]{:S(2)}) async-start(s8[10027008]{0:T(1024)(128)(4,1)} %bitcast.37), calls=%async_computation.5 | async-start | bytes 3276800
  108.1 13.9 %copy-start.7 = (f32[12]{0:T(128)S(1)}, f32[12]{0:T(128)}, u32[]{:S(2)}) copy-start(f32[12]{0:T(128)} %param.8) | copy-start | bytes 148
  108.1 14.3 %copy-start.5 = (s32[128,256]{1,0:T(8,128)S(1)}, s32[128,256]{1,0:T(8,128)}, u32[]{:S(2)}) copy-start(s32[128,256]{1,0:T(8,128)} %param.7) | copy-start | bytes 393220
  108.1 14.3 %copy-start.6 = (f32[128,256]{1,0:T(8,128)S(1)}, f32[128,256]{1,0:T(8,128)}, u32[]{:S(2)}) copy-start(f32[128,256]{1,0:T(8,128)} %param.9) | copy-start | bytes 393220
  119.3 2.7 %copy-start.4 = (f32[4,12,128,256]{3,2,1,0:T(8,128)}, f32[4,12,128,256]{3,2,1,0:T(8,128)S(1)}, u32[]{:S(2)}) copy-start(f32[4,12,128,256]{3,2,1,0:T(8,128)S(1)} %fusion.4) | copy-start | bytes 18874372
  123.9 69.8 %all-to-all-start = ((f32[2,128,256]{2,0,1:T(2,128)}), f32[2,128,256]{2,0,1:T(2,128)S(1)}, u32[]{:S(2)}, u32[]{:S(2)}) async-start(f32[2,128,256]{2,0,1:T(2,128)} %copy.26), calls=%async_computation | async-start | bytes 524288 | tf_op jit(solution)/shard_map/all_to_all | solution.py:107
  194.1 17.5 %collective-permute-start.7 = (f32[1,2048]{1,0:T(1,128)S(1)}, f32[1,2048]{1,0:T(1,128)S(1)}, u32[]{:S(2)}, u32[]{:S(2)}) collective-permute-start(f32[1,2048]{1,0:T(1,128)S(1)} %get-tuple-element.22), channel_id=1, source_target_pairs={{0,1},{1,2},{2,3},{3,4},{4,5},{5,6},{6,7},{7,8},{8,9},{9,10},{10,1... | collective-permute-start | bytes 24584 | tf_op jit(solution)/shard_map/ppermute | solution.py:26
  199.7 11.9 %collective-permute-start.5 = (f32[1,2048]{1,0:T(1,128)S(1)}, f32[1,2048]{1,0:T(1,128)S(1)}, u32[]{:S(2)}, u32[]{:S(2)}) collective-permute-start(f32[1,2048]{1,0:T(1,128)S(1)} %get-tuple-element.23), channel_id=1, source_target_pairs={{1,0},{2,1},{3,2},{4,3},{5,4},{6,5},{7,6},{8,7},{9,8},{10,9},{11,1... | collective-permute-start | bytes 24584 | tf_op jit(solution)/shard_map/ppermute | solution.py:29
  201.8 10.0 %collective-permute-start.4 = (f32[1,2048]{1,0:T(1,128)S(1)}, f32[1,2048]{1,0:T(1,128)S(1)}, u32[]{:S(2)}, u32[]{:S(2)}) collective-permute-start(f32[1,2048]{1,0:T(1,128)S(1)} %bitcast.61), channel_id=1, source_target_pairs={{1,0},{2,1},{3,2},{4,3},{5,4},{6,5},{7,6},{8,7},{9,8},{10,9},{11,1... | collective-permute-start | bytes 24584 | tf_op jit(solution)/shard_map/ppermute | solution.py:29
  203.8 8.6 %collective-permute-start.6 = (f32[1,2048]{1,0:T(1,128)S(1)}, f32[1,2048]{1,0:T(1,128)S(1)}, u32[]{:S(2)}, u32[]{:S(2)}) collective-permute-start(f32[1,2048]{1,0:T(1,128)S(1)} %bitcast.60), channel_id=1, source_target_pairs={{0,1},{1,2},{2,3},{3,4},{4,5},{5,6},{6,7},{7,8},{8,9},{9,10},{10,1... | collective-permute-start | bytes 24584 | tf_op jit(solution)/shard_map/ppermute | solution.py:26
  213.0 10.4 %collective-permute-start.9 = (f32[1,2048]{1,0:T(1,128)S(1)}, f32[1,2048]{1,0:T(1,128)S(1)}, u32[]{:S(2)}, u32[]{:S(2)}) collective-permute-start(f32[1,2048]{1,0:T(1,128)S(1)} %get-tuple-element.20), channel_id=1, source_target_pairs={{0,1},{1,2},{2,3},{3,4},{4,5},{5,6},{6,7},{7,8},{8,9},{9,10},{10,1... | collective-permute-start | bytes 24584 | tf_op jit(solution)/shard_map/ppermute | solution.py:26
  221.4 9.2 %collective-permute-start.8 = (f32[1,2048]{1,0:T(1,128)S(1)}, f32[1,2048]{1,0:T(1,128)S(1)}, u32[]{:S(2)}, u32[]{:S(2)}) collective-permute-start(f32[1,2048]{1,0:T(1,128)S(1)} %get-tuple-element.21), channel_id=1, source_target_pairs={{1,0},{2,1},{3,2},{4,3},{5,4},{6,5},{7,6},{8,7},{9,8},{10,9},{11,1... | collective-permute-start | bytes 24584 | tf_op jit(solution)/shard_map/ppermute | solution.py:29
  231.2 4.4 %collective-permute-start.11 = (f32[1,2048]{1,0:T(1,128)S(1)}, f32[1,2048]{1,0:T(1,128)S(1)}, u32[]{:S(2)}, u32[]{:S(2)}) collective-permute-start(f32[1,2048]{1,0:T(1,128)S(1)} %get-tuple-element.18), channel_id=1, source_target_pairs={{0,1},{1,2},{2,3},{3,4},{4,5},{5,6},{6,7},{7,8},{8,9},{9,10},{10,1... | collective-permute-start | bytes 24584 | tf_op jit(solution)/shard_map/ppermute | solution.py:26
  233.1 9.2 %collective-permute-start.10 = (f32[1,2048]{1,0:T(1,128)S(1)}, f32[1,2048]{1,0:T(1,128)S(1)}, u32[]{:S(2)}, u32[]{:S(2)}) collective-permute-start(f32[1,2048]{1,0:T(1,128)S(1)} %get-tuple-element.19), channel_id=1, source_target_pairs={{1,0},{2,1},{3,2},{4,3},{5,4},{6,5},{7,6},{8,7},{9,8},{10,9},{11,1... | collective-permute-start | bytes 24584 | tf_op jit(solution)/shard_map/ppermute | solution.py:29
where the time goes:
time: 244 us
  other arithmetic  71.9 us (29%)
  blocking collectives  62.9 us (26%)
  starting transfers between devices  48.7 us (20%)
  local copies, waits for them, and re-layouts  38.5 us (16%)
  waiting for transfers between devices  19.2 us (8%)
  between operations  2.68 us (1%)
    pmax x1, blocking collectives, shards(): lam_max = 0.5 + 10.0 * lax.pmax(jnp.max(coefficient), ('bx', 'by'))  62.9 us
    concatenate x6, other arithmetic, with_halo(): block = jnp.concatenate([low, block, high], axis=dim)  31 us
    ppermute x6, starting transfers between devices, with_halo(): lax.ppermute(lax.slice_in_dim(block, block.shape[dim] - width, None, axis...  28 us
    ppermute x6, waiting for transfers between devices, with_halo(): lax.ppermute(lax.slice_in_dim(block, 0, width, axis=dim), axis, backward)  18.6 us
    mul x2, other arithmetic, face_flux(): (jnp.maximum(speed, 0.0) * here + jnp.minimum(speed, 0.0) * ahead) * (wet...  18.4 us
    ppermute x6, starting transfers between devices, with_halo(): lax.ppermute(lax.slice_in_dim(block, 0, width, axis=dim), axis, backward)  15.3 us
    sub x1, other arithmetic, shards(): tracers - (flux_x[:, :, 1:] - flux_x[:, :, :-1])  11.2 us
    slice x6, local copies, waits for them, and re-layouts, with_halo(): lax.slice_in_dim(block, block.shape[dim] - width, None, axis=dim)  9.93 us
  transfers between devices with their start and end apart: 13, of which 4 were waited for; matrix products, arithmetic and copies ran while one was open for 3% of the time, Pallas kernels for 0%

commit v1 on v0

v1 whole, which is shorter than its diff:
```python
import functools

import jax
import jax.numpy as jnp
from jax import lax
from jax.experimental import pallas as pl
from jax.experimental.pallas import tpu as pltpu
from jax.sharding import PartitionSpec as P

ITERS = 3
TRACERS = 4
LEVELS = 12
ROWS = 128
COLS = 256
TILES = ROWS // 8
LANE = 128
WET = 60
VMEM = pl.BlockSpec(memory_space=pltpu.VMEM)
SMEM = pl.BlockSpec(memory_space=pltpu.SMEM)


def lanes(shape):
    return lax.broadcasted_iota(jnp.int32, shape, len(shape) - 1)


def sublanes(shape):
    return lax.broadcasted_iota(jnp.int32, shape, len(shape) - 2)


def pack_kernel(t_ref, v_ref, ocean_ref, depth_ref, row_hi, row_lo, col_hi, col_lo, top, wet_out, coef_out):
    k = pl.program_id(0)
    lane = lanes((ROWS, LANE))

    @pl.when(k == 0)
    def _():
        wet = ocean_ref[...].astype(jnp.float32)
        coef = depth_ref[...] * (0.1 + 0.9 * wet)
        wet_out[...] = wet
        coef_out[...] = coef
        most = jnp.max(jnp.max(coef, axis=0, keepdims=True), axis=1, keepdims=True)
        top[...] = jnp.broadcast_to(most[None], top.shape)
        row_hi[...] = jnp.zeros(row_hi.shape, jnp.float32)
        row_lo[...] = jnp.zeros(row_lo.shape, jnp.float32)
        row_hi[pl.ds(WET, 1), :] = wet[ROWS - 1 : ROWS, :]
        row_lo[pl.ds(WET, 1), :] = wet[0:1, :]
        col_hi[...] = jnp.where(lane == WET, pltpu.roll(wet[:, LANE:], WET + 1, 1), 0.0)
        col_lo[...] = jnp.where(lane == WET, pltpu.roll(wet[:, :LANE], WET, 1), 0.0)

    hi = col_hi[...]
    lo = col_lo[...]
    for t in range(TRACERS):
        slot = t * LEVELS + k
        row_hi[pl.ds(slot, 1), :] = t_ref[t, 0, ROWS - 1 : ROWS, :]
        row_lo[pl.ds(slot, 1), :] = t_ref[t, 0, 0:1, :]
        hi = jnp.where(lane == slot, pltpu.roll(t_ref[t, 0, :, LANE:], slot + 1, 1), hi)
        lo = jnp.where(lane == slot, pltpu.roll(t_ref[t, 0, :, :LANE], slot, 1), lo)
    slot = TRACERS * LEVELS + k
    row_hi[pl.ds(slot, 1), :] = v_ref[0, 0, ROWS - 1 : ROWS, :]
    hi = jnp.where(lane == slot, pltpu.roll(v_ref[1, 0, :, LANE:], slot + 1, 1), hi)
    col_hi[...] = hi
    col_lo[...] = lo


def pack(tracers, velocity, ocean, depth):
    whole = lambda *shape: pl.BlockSpec(shape, lambda k: (0,) * len(shape))
    f32 = lambda *shape: jax.ShapeDtypeStruct(shape, jnp.float32)
    shapes = ((64, COLS), (64, COLS), (ROWS, LANE), (ROWS, LANE), (16, 8, LANE), (ROWS, COLS), (ROWS, COLS))
    return pl.pallas_call(
        pack_kernel,
        grid=(LEVELS,),
        in_specs=[
            pl.BlockSpec((TRACERS, 1, ROWS, COLS), lambda k: (0, k, 0, 0)),
            pl.BlockSpec((2, 1, ROWS, COLS), lambda k: (0, k, 0, 0)),
            whole(ROWS, COLS),
            whole(ROWS, COLS),
        ],
        out_specs=[whole(*s) for s in shapes],
        out_shape=[f32(*s) for s in shapes],
        cost_estimate=pl.CostEstimate(flops=4_000_000, bytes_accessed=9_400_000, transcendentals=0),
        name="pack_edges",
    )(tracers, velocity, ocean, depth)


def sided(x, edge_lo, edge_hi):
    lane = lanes((8, LANE))
    a, b = x[:, :LANE], x[:, LANE:]
    ra, rb = pltpu.roll(a, 1, 1), pltpu.roll(b, 1, 1)
    sa, sb = pltpu.roll(a, LANE - 1, 1), pltpu.roll(b, LANE - 1, 1)
    behind = jnp.concatenate([jnp.where(lane == 0, edge_lo, ra), jnp.where(lane == 0, ra, rb)], 1)
    ahead = jnp.concatenate([jnp.where(lane == LANE - 1, sb, sa), jnp.where(lane == LANE - 1, edge_hi, sb)], 1)
    return behind, ahead


def below(load, edge, r):
    if r:
        return load(8 * r - 1)
    return jnp.where(sublanes((8, COLS)) == 0, edge, pltpu.roll(load(0), 1, 0))


def above(load, edge, r):
    if r < TILES - 1:
        return load(8 * r + 1)
    return jnp.where(sublanes((8, COLS)) == 7, edge, pltpu.roll(load(8 * r), 7, 0))


def advect_kernel(first, *refs):
    if first == 0:
        (thick, t_ref, v_ref, wet_ref, row_lo, row_hi, col_lo, col_hi, coef_ref, tops_ref, out_ref, send_ref, w_e, w_w, w_n, w_s, total) = refs
    else:
        (t_ref, v_ref, wet_ref, row_lo, row_hi, col_lo, col_hi, _, out_ref, w_e, w_w, w_n, w_s) = refs
    k = pl.program_id(0)

    @pl.when(k == 0)
    def _():
        load = lambda at: wet_ref[at : at + 8, :]
        for r in range(TILES):
            rows = pl.ds(8 * r, 8)
            here = load(8 * r)
            w_e[rows, :] = here * above(load, row_hi[WET : WET + 1, :], r)
            w_w[rows, :] = here * below(load, row_lo[WET : WET + 1, :], r)
            edge_lo = pltpu.roll(col_lo[rows, :], LANE - WET, 1)
            edge_hi = pltpu.roll(col_hi[rows, :], LANE - 1 - WET, 1)
            behind, ahead = sided(here, edge_lo, edge_hi)
            w_n[rows, :] = here * ahead
            w_s[rows, :] = here * behind
        if first == 0:
            total[...] = jnp.zeros(total.shape, jnp.float32)

    speed_slot = TRACERS * LEVELS + k
    before_u = row_lo[pl.ds(speed_slot, 1), :]
    for r in range(TILES):
        rows = pl.ds(8 * r, 8)
        load_u = lambda at: v_ref[0, 0, at : at + 8, :]
        u = load_u(8 * r)
        u_behind = below(load_u, before_u, r)
        v = v_ref[1, 0, rows, :]
        lo_tile = col_lo[rows, :]
        hi_tile = col_hi[rows, :]
        v_edge = pltpu.roll(lo_tile, LANE - speed_slot, 1)
        lane = lanes((8, LANE))
        va, vb = pltpu.roll(v[:, :LANE], 1, 1), pltpu.roll(v[:, LANE:], 1, 1)
        v_behind = jnp.concatenate([jnp.where(lane == 0, v_edge, va), jnp.where(lane == 0, va, vb)], 1)
        we, ww, wn, ws = w_e[rows, :], w_w[rows, :], w_n[rows, :], w_s[rows, :]
        ahead_x = jnp.minimum(u, 0.0) * we
        behind_x = jnp.maximum(u_behind, 0.0) * ww
        ahead_y = jnp.minimum(v, 0.0) * wn
        behind_y = jnp.maximum(v_behind, 0.0) * ws
        center = (1.0 - (jnp.maximum(u, 0.0) * we - jnp.minimum(u_behind, 0.0) * ww)) - (
            jnp.maximum(v, 0.0) * wn - jnp.minimum(v_behind, 0.0) * ws
        )
        new = []
        for t in range(2):
            load = lambda at: t_ref[t, 0, at : at + 8, :]
            slot = (first + t) * LEVELS + k
            c = load(8 * r)
            c_below = below(load, row_lo[pl.ds(slot, 1), :], r)
            c_above = above(load, row_hi[pl.ds(slot, 1), :], r)
            edge_lo = pltpu.roll(lo_tile, LANE - slot, 1)
            edge_hi = pltpu.roll(hi_tile, LANE - 1 - slot, 1)
            c_behind, c_ahead = sided(c, edge_lo, edge_hi)
            value = center * c - (ahead_x * c_above - behind_x * c_below) - (ahead_y * c_ahead - behind_y * c_behind)
            out_ref[t, 0, rows, :] = value
            new.append(value)
        if first == 0:
            total[rows, :] = total[rows, :] + thick[k] * (0.2 * new[0] - 0.8 * new[1])

    if first == 0:

        @pl.when(k == LEVELS - 1)
        def _():
            most = jnp.max(tops_ref[...], axis=0)
            for j in range(8):
                rows = pl.ds(16 * j, 16)
                send_ref[j, 0:16, :] = total[rows, :] * wet_ref[rows, :]
                send_ref[j, 16:32, :] = coef_ref[rows, :]
                send_ref[j, 32:40, :LANE] = most
                send_ref[j, 32:40, LANE:] = most


def advect(first, tracers, velocity, wet, row_lo, row_hi, col_lo, col_hi, extra):
    whole = lambda *shape: pl.BlockSpec(shape, lambda k: (0,) * len(shape))
    half = first // 2
    ins = [
        pl.BlockSpec((2, 1, ROWS, COLS), lambda k: (half, k, 0, 0)),
        pl.BlockSpec((2, 1, ROWS, COLS), lambda k: (0, k, 0, 0)),
        whole(ROWS, COLS),
        whole(64, COLS),
        whole(64, COLS),
        whole(ROWS, LANE),
        whole(ROWS, LANE),
    ]
    operands = [tracers, velocity, wet, row_lo, row_hi, col_lo, col_hi]
    out_specs = [pl.BlockSpec((2, 1, ROWS, COLS), lambda k: (half, k, 0, 0))]
    out_shape = [jax.ShapeDtypeStruct((TRACERS, LEVELS, ROWS, COLS), jnp.float32)]
    scratch = [pltpu.VMEM((ROWS, COLS), jnp.float32)] * 4
    aliases = {}
    if first == 0:
        thickness, coef, tops = extra
        ins = [SMEM] + ins + [whole(ROWS, COLS), whole(16, 8, LANE)]
        operands = [thickness] + operands + [coef, tops]
        out_specs.append(whole(8, 40, COLS))
        out_shape.append(jax.ShapeDtypeStruct((8, 40, COLS), jnp.float32))
        scratch.append(pltpu.VMEM((ROWS, COLS), jnp.float32))
    else:
        aliases = {len(operands): 0}
        ins = ins + [pl.BlockSpec(memory_space=pl.ANY)]
        operands = operands + [extra]
    return pl.pallas_call(
        functools.partial(advect_kernel, first),
        grid=(LEVELS,),
        in_specs=ins,
        out_specs=out_specs,
        out_shape=out_shape,
        scratch_shapes=scratch,
        input_output_aliases=aliases,
        cost_estimate=pl.CostEstimate(flops=24_000_000, bytes_accessed=9_400_000, transcendentals=0),
        name="advect_forcing" if first == 0 else "advect_rest",
    )(*operands)


def strip_kernel(got_ref, strip_ref, down_ref, up_ref):
    for j in range(8):
        cols = pl.ds(j * COLS, COLS)
        strip_ref[0, :, cols] = got_ref[j, 0:16, :]
        strip_ref[1, :, cols] = got_ref[j, 16:32, :]
        down_ref[0:4, cols] = got_ref[j, 0:4, :]
        down_ref[4:8, cols] = got_ref[j, 16:20, :]
        up_ref[0:4, cols] = got_ref[j, 12:16, :]
        up_ref[4:8, cols] = got_ref[j, 28:32, :]


def strips(got):
    f32 = lambda *shape: jax.ShapeDtypeStruct(shape, jnp.float32)
    return pl.pallas_call(
        strip_kernel,
        in_specs=[VMEM],
        out_specs=[VMEM] * 3,
        out_shape=[f32(2, 16, 8 * COLS), f32(8, 8 * COLS), f32(8, 8 * COLS)],
        cost_estimate=pl.CostEstimate(flops=1000, bytes_accessed=600_000, transcendentals=0),
        name="strip_rows",
    )(got)


WIDE = 8 * COLS
EXT = 24
NEAR = ((1, 0, 0.5), (-1, 0, 0.5), (0, 1, 0.5), (0, -1, 0.5), (1, 1, 0.125), (1, -1, 0.125), (-1, 1, 0.125), (-1, -1, 0.125))


def moved(x, rows, cols):
    if cols:
        lane = lanes(x.shape)
        x = pltpu.roll(x, (-cols) % x.shape[1], 1)
        x = jnp.where(lane == (x.shape[1] - 1 if cols > 0 else 0), 0.0, x)
    if rows:
        x = pltpu.roll(x, (-rows) % x.shape[0], 0)
    return x


def solve_kernel(got_ref, strip_ref, before_ref, after_ref, out_ref, h_ref, p_ref, weight):
    h_ref[0:4, :] = before_ref[4:8, :]
    h_ref[4:20, :] = strip_ref[1]
    h_ref[20:24, :] = after_ref[4:8, :]
    p_ref[0:4, :] = before_ref[0:4, :]
    p_ref[4:20, :] = strip_ref[0]
    p_ref[20:24, :] = after_ref[0:4, :]
    most = jnp.max(got_ref[:, 32:40, 0:LANE], axis=0)[0:1, 0:1]
    lam_max = 0.5 + 10.0 * most
    theta = (lam_max + 0.5) / 2.0
    delta = (lam_max - 0.5) / 2.0
    sigma = theta / delta
    rho = 1.0 / sigma
    h = h_ref[...]
    sides = {c: moved(h, 0, c) for c in (-1, 0, 1)}
    for n, (a, b, w) in enumerate(NEAR):
        weight[n] = w * (h + moved(sides[b], a, 0))
    inside = h > 0.0
    resid = p_ref[...]
    direction = resid / theta
    answer = jnp.zeros_like(resid)
    for _ in range(ITERS):
        sides = {c: moved(direction, 0, c) for c in (-1, 0, 1)}
        applied = 0.5 * direction
        for n, (a, b, w) in enumerate(NEAR):
            applied = applied + weight[n] * (direction - moved(sides[b], a, 0))
        resid = jnp.where(inside, resid - applied, 0.0)
        answer = answer + direction
        rho_next = 1.0 / (2.0 * sigma - rho)
        direction = rho_next * rho * direction + (2.0 * rho_next / delta) * resid
        rho = rho_next
    out_ref[...] = (answer + direction)[4:20, :]


def solve(got, strip, before, after):
    return pl.pallas_call(
        solve_kernel,
        in_specs=[VMEM] * 4,
        out_specs=VMEM,
        out_shape=jax.ShapeDtypeStruct((16, WIDE), jnp.float32),
        scratch_shapes=[
            pltpu.VMEM((EXT, WIDE), jnp.float32),
            pltpu.VMEM((EXT, WIDE), jnp.float32),
            pltpu.VMEM((8, EXT, WIDE), jnp.float32),
        ],
        cost_estimate=pl.CostEstimate(flops=6_000_000, bytes_accessed=600_000, transcendentals=0),
        name="chebyshev",
    )(got, strip, before, after)


def send(x, axes, count, step):
    pairs = [(i, i + step) for i in range(count) if 0 <= i + step < count]
    return lax.ppermute(x, axes, pairs)


def shards(tracers, velocity, ocean, thickness, depth):
    nx, ny = lax.axis_size("bx"), lax.axis_size("by")
    row_hi, row_lo, col_hi, col_lo, top, wet, coef = pack(tracers, velocity, ocean, depth)
    before_row = send(row_hi, "bx", nx, 1)
    after_row = send(row_lo, "bx", nx, -1)
    before_col = send(col_hi, "by", ny, 1)
    after_col = send(col_lo, "by", ny, -1)
    tops = lax.all_to_all(top, "bx", split_axis=0, concat_axis=0, tiled=True)
    halos = (wet, before_row, after_row, before_col, after_col)
    part, parcels = advect(0, tracers, velocity, *halos, (thickness, coef, tops))
    got = lax.all_to_all(parcels, "by", split_axis=0, concat_axis=0, tiled=True)
    new_tracers = advect(2, tracers, velocity, *halos, part)[0]
    strip, down, up = strips(got)
    both = ("bx", "by")
    before = send(up, both, nx * ny, 1)
    after = send(down, both, nx * ny, -1)
    return new_tracers, solve(got, strip, before, after)


def solution(mesh):
    return jax.shard_map(
        shards,
        mesh=mesh,
        in_specs=(
            P(None, None, "bx", "by"),
            P(None, None, "bx", "by"),
            P("bx", "by"),
            P(),
            P("bx", "by"),
        ),
        out_specs=(P(None, None, "bx", "by"), P(("bx", "by"), None)),
        check_vma=False,
    )
```

time: 244 us -> 87.5 us (0.36)
  the two profiles are of different devices: /device:TPU:121 before, /device:TPU:2 now
where the time goes in v1:
time: 87.5 us; the launch traced here: 86.4 us
  Pallas kernels  35.7 us (41%)
  blocking collectives  28.4 us (32%)
  starting transfers between devices  20.3 us (23%)
  local copies, waits for them, and re-layouts  1.28 us (1%)
    pallas_call x2, Pallas kernels, advect(): pl.pallas_call(functools.partial(advect_kernel, first), grid=(LEVELS,), i...  21.2 us
    ppermute x6, starting transfers between devices, send(): return lax.ppermute(x, axes, pairs)  20.3 us
    all_to_all x1, blocking collectives, shards(): got = lax.all_to_all(parcels, 'by', split_axis=0, concat_axis=0, tiled=True)  16.6 us
    all_to_all x1, blocking collectives, shards(): tops = lax.all_to_all(top, 'bx', split_axis=0, concat_axis=0, tiled=True)  11.7 us
    pallas_call x1, Pallas kernels, pack(): pl.pallas_call(pack_kernel, grid=(LEVELS,), in_specs=[pl.BlockSpec((TRACE...  9.62 us
    pallas_call x1, Pallas kernels, solve(): pl.pallas_call(solve_kernel, in_specs=[VMEM] * 4, out_specs=VMEM, out_sha...  3.11 us
    pallas_call x1, Pallas kernels, strips(): pl.pallas_call(strip_kernel, in_specs=[VMEM], out_specs=[VMEM] * 3, out_s...  1.75 us
  transfers between devices with their start and end apart: 6, of which 0 were waited for; matrix products, arithmetic and copies ran while one was open for 0% of the time, Pallas kernels for 12%

profile of v1, /device:TPU:2, one launch (start us, length us, event | category | flops | bytes accessed | tf_op | source)
XLA Modules:
  0.0 86.4 jit_solution(11246855347656411556)
XLA Ops:
  0.6 9.6 %pack_edges.1 = (f32[64,256]{1,0:T(8,128)}, f32[64,256]{1,0:T(8,128)}, f32[128,128]{1,0:T(8,128)}, f32[128,128]{1,0:T(8,128)}, f32[16,8,128]{2,1,0:T(8,128)}, /*index=5*/f32[128,256]{1,0:T(8,128)}, f32[128,256]{1,0:T(8,128)}) custom-call(f32[4,12,128,256]{3,2,1,0:T(8,128)} %refs_0_.3, f32[2,12,128,256]{3,2,1,0:T(8,128)} %refs_1_.3, s32[128,256]{1,0:T(8,128)} %ocean_ref.1, ...), custom_call_target="tpu_custom_call" | custom-call | flops 4000000 | bytes 9400000 | tf_op jit(solution)/shard_map/pack_edges/pallas_call | solution.py:68
  10.3 3.5 %collective-permute-start = (f32[64,256]{1,0:T(8,128)}, f32[64,256]{1,0:T(8,128)S(1)}, u32[]{:S(2)}, u32[]{:S(2)}) collective-permute-start(f32[64,256]{1,0:T(8,128)} %get-tuple-element.15), channel_id=1, source_target_pairs={{0,8},{8,16},{16,24},{24,32},{32,40},{40,48},{48,56},{56,64},{64,7... | collective-permute-start | bytes 196616 | tf_op jit(solution)/shard_map/ppermute | solution.py:311
  13.7 4.5 %collective-permute-start.1 = (f32[64,256]{1,0:T(8,128)}, f32[64,256]{1,0:T(8,128)S(1)}, u32[]{:S(2)}, u32[]{:S(2)}) collective-permute-start(f32[64,256]{1,0:T(8,128)} %get-tuple-element.16), channel_id=1, source_target_pairs={{8,0},{16,8},{24,16},{32,24},{40,32},{48,40},{56,48},{64,56},{72,6... | collective-permute-start | bytes 196616 | tf_op jit(solution)/shard_map/ppermute | solution.py:311
  18.2 1.3 %collective-permute-start.2 = (f32[128,128]{1,0:T(8,128)}, f32[128,128]{1,0:T(8,128)S(1)}, u32[]{:S(2)}, u32[]{:S(2)}) collective-permute-start(f32[128,128]{1,0:T(8,128)} %get-tuple-element.17), channel_id=1, source_target_pairs={{0,1},{1,2},{2,3},{3,4},{4,5},{5,6},{6,7},{8,9},{9,10},{10,11},{11... | collective-permute-start | bytes 196616 | tf_op jit(solution)/shard_map/ppermute | solution.py:311
  19.5 1.3 %collective-permute-start.3 = (f32[128,128]{1,0:T(8,128)}, f32[128,128]{1,0:T(8,128)S(1)}, u32[]{:S(2)}, u32[]{:S(2)}) collective-permute-start(f32[128,128]{1,0:T(8,128)} %get-tuple-element.18), channel_id=1, source_target_pairs={{1,0},{2,1},{3,2},{4,3},{5,4},{6,5},{7,6},{9,8},{10,9},{11,10},{12... | collective-permute-start | bytes 196616 | tf_op jit(solution)/shard_map/ppermute | solution.py:311
  20.8 11.7 %all_to_all.10.refs_9_ = f32[16,8,128]{2,1,0:T(8,128)} all-to-all(f32[16,8,128]{2,1,0:T(8,128)} %get-tuple-element.20), channel_id=1, replica_groups=mesh['bx'=16,'by'=8] {'bx'}, dimensions={0} | all-to-all | bytes 131072 | tf_op jit(solution)/shard_map/all_to_all | solution.py:321
  32.6 0.0 collective-permute-done.refs_4_.refs_3_
  32.6 0.0 copy-start
  32.6 0.0 collective-permute-done.1.refs_5_.refs_4_
  32.6 0.0 copy-start.1
  32.6 0.0 collective-permute-done.2.refs_6_.refs_5_
  32.6 0.0 copy-start.2
  32.6 0.0 collective-permute-done.3.refs_7_.refs_6_
  32.6 0.0 copy-start.3
  32.6 0.6 copy-done
  33.2 0.0 copy-done.1
  33.2 0.0 copy-done.2
  33.2 0.0 copy-done.3
  33.3 10.7 %advect_forcing.1 = (f32[4,12,128,256]{3,2,1,0:T(8,128)}, f32[8,40,256]{2,1,0:T(8,128)}) custom-call(f32[12]{0:T(128)} %refs_0_.2, f32[4,12,128,256]{3,2,1,0:T(8,128)} %refs_0_.3, f32[2,12,128,256]{3,2,1,0:T(8,128)} %refs_1_.3, f32[128,256]{1,0:T(8,128)} %get-tuple-element.14.refs_3_.refs_2_, f32[64,256]{1,0:T(8,128)} %copy-done, f32[64,256]{1,0:T(8,128)} %copy-done.1, ...), custom_call_target="tpu_custom_call" | custom-call | flops 24000000 | bytes 9400000 | tf_op jit(solution)/shard_map/advect_forcing/pallas_call | solution.py:208
  44.0 16.6 %all_to_all.11.got_ref = f32[8,40,256]{2,1,0:T(8,128)} all-to-all(f32[8,40,256]{2,1,0:T(8,128)} %get-tuple-element.22), channel_id=1, replica_groups=mesh['bx'=16,'by'=8] {'by'}, dimensions={0} | all-to-all | bytes 655360 | tf_op jit(solution)/shard_map/all_to_all | solution.py:324
  60.7 1.8 %strip_rows.1 = (f32[2,16,2048]{2,1,0:T(8,128)}, f32[8,2048]{1,0:T(8,128)}, f32[8,2048]{1,0:T(8,128)}) custom-call(f32[8,40,256]{2,1,0:T(8,128)} %all_to_all.11.got_ref), custom_call_target="tpu_custom_call" | custom-call | flops 1000 | bytes 600000 | tf_op jit(solution)/shard_map/strip_rows/pallas_call | solution.py:234
  62.4 1.9 %collective-permute-start.4 = (f32[8,2048]{1,0:T(8,128)}, f32[8,2048]{1,0:T(8,128)S(1)}, u32[]{:S(2)}, u32[]{:S(2)}) collective-permute-start(f32[8,2048]{1,0:T(8,128)} %get-tuple-element.24), channel_id=1, source_target_pairs={{0,1},{1,2},{2,3},{3,4},{4,5},{5,6},{6,7},{7,8},{8,9},{9,10},{10,1... | collective-permute-start | bytes 196616 | tf_op jit(solution)/shard_map/ppermute | solution.py:311
  64.3 7.9 %collective-permute-start.5 = (f32[8,2048]{1,0:T(8,128)}, f32[8,2048]{1,0:T(8,128)S(1)}, u32[]{:S(2)}, u32[]{:S(2)}) collective-permute-start(f32[8,2048]{1,0:T(8,128)} %get-tuple-element.25), channel_id=1, source_target_pairs={{1,0},{2,1},{3,2},{4,3},{5,4},{6,5},{7,6},{8,7},{9,8},{10,9},{11,1... | collective-permute-start | bytes 196616 | tf_op jit(solution)/shard_map/ppermute | solution.py:311
  72.2 10.4 %advect_rest.1 = f32[4,12,128,256]{3,2,1,0:T(8,128)} custom-call(f32[4,12,128,256]{3,2,1,0:T(8,128)} %refs_0_.3, f32[2,12,128,256]{3,2,1,0:T(8,128)} %refs_1_.3, f32[128,256]{1,0:T(8,128)} %get-tuple-element.14.refs_3_.refs_2_, f32[64,256]{1,0:T(8,128)} %copy-done, f32[64,256]{1,0:T(8,128)} %copy-done.1, ...), custom_call_target="tpu_custom_call", output_to_operand_aliasing={{}: (7, {})} | custom-call | flops 24000000 | bytes 9400000 | tf_op jit(solution)/shard_map/advect_rest/pallas_call | solution.py:208
  82.6 0.0 collective-permute-done.4.before_ref
  82.6 0.0 copy-start.4
  82.6 0.0 collective-permute-done.5.after_ref
  82.6 0.0 copy-start.5
  82.6 0.6 copy-done.4
  83.2 0.0 copy-done.5
  83.3 3.1 %chebyshev.1 = f32[16,2048]{1,0:T(8,128)} custom-call(f32[8,40,256]{2,1,0:T(8,128)} %all_to_all.11.got_ref, f32[2,16,2048]{2,1,0:T(8,128)} %get-tuple-element.23.strip_ref, f32[8,2048]{1,0:T(8,128)} %copy-done.4, f32[8,2048]{1,0:T(8,128)} %copy-done.5), custom_call_target="tpu_custom_call" | custom-call | flops 6000000 | bytes 600000 | tf_op jit(solution)/shard_map/chebyshev/pallas_call | solution.py:294
Async XLA Ops:
  10.3 22.3 %collective-permute-start = (f32[64,256]{1,0:T(8,128)}, f32[64,256]{1,0:T(8,128)S(1)}, u32[]{:S(2)}, u32[]{:S(2)}) collective-permute-start(f32[64,256]{1,0:T(8,128)} %get-tuple-element.15), channel_id=1, source_target_pairs={{0,8},{8,16},{16,24},{24,32},{32,40},{40,48},{48,56},{56,64},{64,7... | collective-permute-start | bytes 196616 | tf_op jit(solution)/shard_map/ppermute | solution.py:311
  13.7 18.8 %collective-permute-start.1 = (f32[64,256]{1,0:T(8,128)}, f32[64,256]{1,0:T(8,128)S(1)}, u32[]{:S(2)}, u32[]{:S(2)}) collective-permute-start(f32[64,256]{1,0:T(8,128)} %get-tuple-element.16), channel_id=1, source_target_pairs={{8,0},{16,8},{24,16},{32,24},{40,32},{48,40},{56,48},{64,56},{72,6... | collective-permute-start | bytes 196616 | tf_op jit(solution)/shard_map/ppermute | solution.py:311
  18.2 14.4 %collective-permute-start.2 = (f32[128,128]{1,0:T(8,128)}, f32[128,128]{1,0:T(8,128)S(1)}, u32[]{:S(2)}, u32[]{:S(2)}) collective-permute-start(f32[128,128]{1,0:T(8,128)} %get-tuple-element.17), channel_id=1, source_target_pairs={{0,1},{1,2},{2,3},{3,4},{4,5},{5,6},{6,7},{8,9},{9,10},{10,11},{11... | collective-permute-start | bytes 196616 | tf_op jit(solution)/shard_map/ppermute | solution.py:311
  19.5 13.1 %collective-permute-start.3 = (f32[128,128]{1,0:T(8,128)}, f32[128,128]{1,0:T(8,128)S(1)}, u32[]{:S(2)}, u32[]{:S(2)}) collective-permute-start(f32[128,128]{1,0:T(8,128)} %get-tuple-element.18), channel_id=1, source_target_pairs={{1,0},{2,1},{3,2},{4,3},{5,4},{6,5},{7,6},{9,8},{10,9},{11,10},{12... | collective-permute-start | bytes 196616 | tf_op jit(solution)/shard_map/ppermute | solution.py:311
  32.6 0.6 copy-start
  32.6 0.6 copy-start.1
  32.6 0.7 copy-start.2
  32.6 0.7 copy-start.3
  62.4 20.2 %collective-permute-start.4 = (f32[8,2048]{1,0:T(8,128)}, f32[8,2048]{1,0:T(8,128)S(1)}, u32[]{:S(2)}, u32[]{:S(2)}) collective-permute-start(f32[8,2048]{1,0:T(8,128)} %get-tuple-element.24), channel_id=1, source_target_pairs={{0,1},{1,2},{2,3},{3,4},{4,5},{5,6},{6,7},{7,8},{8,9},{9,10},{10,1... | collective-permute-start | bytes 196616 | tf_op jit(solution)/shard_map/ppermute | solution.py:311
  64.3 18.3 %collective-permute-start.5 = (f32[8,2048]{1,0:T(8,128)}, f32[8,2048]{1,0:T(8,128)S(1)}, u32[]{:S(2)}, u32[]{:S(2)}) collective-permute-start(f32[8,2048]{1,0:T(8,128)} %get-tuple-element.25), channel_id=1, source_target_pairs={{1,0},{2,1},{3,2},{4,3},{5,4},{6,5},{7,6},{8,7},{9,8},{10,9},{11,1... | collective-permute-start | bytes 196616 | tf_op jit(solution)/shard_map/ppermute | solution.py:311
  82.6 0.6 copy-start.4
  82.6 0.6 copy-start.5

commit v2 on v1

v2 whole, which is shorter than its diff:
```python
import functools

import jax
import jax.numpy as jnp
from jax import lax
from jax.experimental import pallas as pl
from jax.experimental.pallas import tpu as pltpu
from jax.sharding import PartitionSpec as P

ITERS = 3
TRACERS = 4
LEVELS = 12
ROWS = 128
COLS = 256
TILES = ROWS // 8
LANE = 128
WIDE = 8 * COLS
EXT = 24
CHUNK = 32

SPEED, WET, PART, COEF, EDGE, MESSAGE = 48, 60, 64, 68, 72, 80
ANY = pl.BlockSpec(memory_space=pl.ANY)
VMEM = pl.BlockSpec(memory_space=pltpu.VMEM)
SMEM = pl.BlockSpec(memory_space=pltpu.SMEM)


def f32(*shape):
    return jax.ShapeDtypeStruct(shape, jnp.float32)


def lanes(shape):
    return lax.broadcasted_iota(jnp.int32, shape, len(shape) - 1)


def sublanes(shape):
    return lax.broadcasted_iota(jnp.int32, shape, len(shape) - 2)


def coefficient(depth, wet):
    return depth * (0.1 + 0.9 * wet)


def positive(x):
    return jnp.maximum(x, 0.0)


def negative(x):
    return jnp.minimum(x, 0.0)


def edge_forcing(q, u, v, wet, thick):
    shape = (8, COLS)
    row, col = sublanes(shape), lanes(shape)
    total = jnp.zeros(shape, jnp.float32)
    flux_x = jnp.zeros(shape, jnp.float32)
    flux_y = jnp.zeros(shape, jnp.float32)
    for k in range(LEVELS):
        depth = thick[k]
        total = total + depth * q[k]
        flux_x = flux_x + depth * (positive(u[k]) * q[k] + negative(u[k]) * pltpu.roll(q[k], 7, 0))
        flux_y = flux_y + depth * (positive(v[k]) * q[k] + negative(v[k]) * pltpu.roll(q[k], COLS - 1, 1))
    flux_x = flux_x * jnp.where(row == 7, 0.0, wet * pltpu.roll(wet, 7, 0))
    flux_y = flux_y * jnp.where(col == COLS - 1, 0.0, wet * pltpu.roll(wet, COLS - 1, 1))
    return wet * (total - (flux_x - pltpu.roll(flux_x, 1, 0)) - (flux_y - pltpu.roll(flux_y, 1, 1)))


def edge_terms(q, v, wet, thick):
    lane = lanes((8, LANE))
    last, first = wet[:, LANE:], wet[:, :LANE]
    upwind = jnp.zeros((8, LANE), jnp.float32)
    terms = jnp.where(lane == 28, pltpu.roll(first, 28, 1), 0.0)
    for k in range(LEVELS):
        depth = thick[k]
        speed = v[k][:, LANE:]
        upwind = upwind + depth * positive(speed) * q[k][:, LANE:]
        terms = jnp.where(lane == k, pltpu.roll(depth * negative(speed) * last, k + 1, 1), terms)
        terms = jnp.where(lane == 16 + k, pltpu.roll(q[k][:, :LANE] * first, 16 + k, 1), terms)
    return jnp.where(lane == LEVELS, pltpu.roll(upwind * last, LEVELS + 1, 1), terms)


def pack_kernel(thick, t_hbm, v_hbm, ocean_hbm, depth_hbm, row_hi, row_lo, col_hi, col_lo, top,
                t_ref, u_top, u_low, v_top, v_low, v_last, ocean_ref, depth_ref, sems):
    def chunk_copy(c):
        rows = pl.ds(pl.multiple_of(c * CHUNK, CHUNK), CHUNK)
        return pltpu.make_async_copy(t_hbm.at[:, :, rows, :], t_ref.at[:, :, rows, :], sems.at[c])

    chunks = ROWS // CHUNK
    small = [
        pltpu.make_async_copy(ocean_hbm, ocean_ref, sems.at[chunks]),
        pltpu.make_async_copy(depth_hbm, depth_ref, sems.at[chunks + 1]),
        pltpu.make_async_copy(v_hbm.at[1, :, :, LANE:], v_last, sems.at[chunks + 2]),
    ]
    tiles = [
        pltpu.make_async_copy(v_hbm.at[0, :, 0:8, :], u_top, sems.at[chunks + 3]),
        pltpu.make_async_copy(v_hbm.at[0, :, ROWS - 8 :, :], u_low, sems.at[chunks + 4]),
        pltpu.make_async_copy(v_hbm.at[1, :, 0:8, :], v_top, sems.at[chunks + 5]),
        pltpu.make_async_copy(v_hbm.at[1, :, ROWS - 8 :, :], v_low, sems.at[chunks + 6]),
    ]
    for copy in small:
        copy.start()
    for c in range(chunks):
        chunk_copy(c).start()
    for copy in tiles:
        copy.start()
    for copy in small:
        copy.wait()
    wet = ocean_ref[...].astype(jnp.float32)
    coef = coefficient(depth_ref[...], wet)
    most = jnp.max(jnp.max(coef, axis=0, keepdims=True), axis=1, keepdims=True)
    top[...] = jnp.broadcast_to(most[None], top.shape)

    def gather(c, _):
        chunk_copy(c).wait()
        lane = lanes((CHUNK, LANE))
        rows = pl.ds(pl.multiple_of(c * CHUNK, CHUNK), CHUNK)
        ocean = ocean_ref[rows, :].astype(jnp.float32)
        hi = jnp.where(lane == 2 * WET, pltpu.roll(ocean[:, LANE:], (2 * WET + 1) % LANE, 1), 0.0)
        lo = jnp.where(lane == 2 * WET - 1, pltpu.roll(ocean[:, :LANE], 2 * WET - 1, 1), 0.0)
        for k in range(LEVELS):
            for t in range(TRACERS):
                s = t * LEVELS + k
                hi = jnp.where(lane == 2 * s, pltpu.roll(t_ref[t, k, rows, LANE:], 2 * s + 1, 1), hi)
                place = (2 * s - 1) % LANE
                lo = jnp.where(lane == place, pltpu.roll(t_ref[t, k, rows, :LANE], place, 1), lo)
            s = SPEED + k
            hi = jnp.where(lane == 2 * s, pltpu.roll(v_last[k, rows, :], 2 * s + 1, 1), hi)
        col_hi[rows, :] = hi
        col_lo[rows, :] = lo
        return 0

    lax.fori_loop(0, chunks, gather, 0)
    for copy in tiles:
        copy.wait()
    for t in range(TRACERS):
        for k in range(LEVELS):
            s = t * LEVELS + k
            row_hi[s : s + 1, :] = t_ref[t, k, ROWS - 1 : ROWS, :]
            row_lo[s : s + 1, :] = t_ref[t, k, 0:1, :]
    for k in range(LEVELS):
        row_hi[SPEED + k : SPEED + k + 1, :] = u_low[k, 7:8, :]
    row_lo[SPEED:WET, :] = jnp.zeros((WET - SPEED, COLS), jnp.float32)
    for row, message, u, v, keep in ((0, row_lo, u_top, v_top, 0), (ROWS - 8, row_hi, u_low, v_low, 4)):
        rows = slice(row, row + 8)
        here = ocean_ref[rows, :].astype(jnp.float32)
        q = [0.2 * t_ref[0, k, rows, :] - 0.8 * t_ref[1, k, rows, :] for k in range(LEVELS)]
        speed_x = [u[k] for k in range(LEVELS)]
        speed_y = [v[k] for k in range(LEVELS)]
        message[WET:PART, :] = jnp.broadcast_to(here[7:8, :] if keep else here[0:1, :], (PART - WET, COLS))
        message[PART:COEF, :] = edge_forcing(q, speed_x, speed_y, here, thick)[keep : keep + 4, :]
        message[COEF:EDGE, :] = coefficient(depth_ref[rows, :], here)[keep : keep + 4, :]
        message[EDGE:MESSAGE, :LANE] = edge_terms(q, speed_y, here, thick)
        message[EDGE:MESSAGE, LANE:] = jnp.zeros((8, LANE), jnp.float32)


def pack(thickness, tracers, velocity, ocean, depth):
    tile = (LEVELS, 8, COLS)
    return pl.pallas_call(
        pack_kernel,
        in_specs=[SMEM, ANY, ANY, ANY, ANY],
        out_specs=[VMEM] * 5,
        out_shape=[f32(MESSAGE, COLS), f32(MESSAGE, COLS), f32(ROWS, LANE), f32(ROWS, LANE), f32(16, 8, LANE)],
        scratch_shapes=[
            pltpu.VMEM((TRACERS, LEVELS, ROWS, COLS), jnp.float32),
            pltpu.VMEM(tile, jnp.float32),
            pltpu.VMEM(tile, jnp.float32),
            pltpu.VMEM(tile, jnp.float32),
            pltpu.VMEM(tile, jnp.float32),
            pltpu.VMEM((LEVELS, ROWS, LANE), jnp.float32),
            pltpu.VMEM((ROWS, COLS), jnp.int32),
            pltpu.VMEM((ROWS, COLS), jnp.float32),
            pltpu.SemaphoreType.DMA((ROWS // CHUNK + 7,)),
        ],
        compiler_params=pltpu.CompilerParams(vmem_limit_bytes=14 * 2**20),
        cost_estimate=pl.CostEstimate(flops=4_000_000, bytes_accessed=7_400_000, transcendentals=0),
        name="pack_edges",
    )(thickness, tracers, velocity, ocean, depth)


def sided(x, edge):
    lane = lanes((8, LANE))
    a, b = x[:, :LANE], x[:, LANE:]
    ra, rb = pltpu.roll(a, 1, 1), pltpu.roll(b, 1, 1)
    sa, sb = pltpu.roll(a, LANE - 1, 1), pltpu.roll(b, LANE - 1, 1)
    behind = jnp.concatenate([jnp.where(lane == 0, edge, ra), jnp.where(lane == 0, ra, rb)], 1)
    ahead = jnp.concatenate([jnp.where(lane == LANE - 1, sb, sa), jnp.where(lane == LANE - 1, edge, sb)], 1)
    return behind, ahead


def below(load, edge, r):
    if r:
        return load(8 * r - 1)
    return jnp.where(sublanes((8, COLS)) == 0, edge, pltpu.roll(load(0), 1, 0))


def above(load, edge, r):
    if r < TILES - 1:
        return load(8 * r + 1)
    return jnp.where(sublanes((8, COLS)) == 7, edge, pltpu.roll(load(8 * r), 7, 0))


def advect_kernel(first, *refs):
    if first == 0:
        (thick, t_hbm, v_hbm, ocean_hbm, row_lo_hbm, row_hi_hbm, col_lo_hbm, col_hi_hbm, depth_hbm, tops_hbm, out_hbm, send_ref,
         t_ref, v_ref, out_ref, ocean_ref, row_lo, row_hi, col_lo, col_hi, w_e, w_w, w_n, w_s, edges, sems, small_sems,
         depth_ref, tops, total, flux, ext) = refs
    else:
        (t_hbm, v_hbm, ocean_hbm, row_lo_hbm, row_hi_hbm, col_lo_hbm, col_hi_hbm, _, out_hbm,
         t_ref, v_ref, out_ref, ocean_ref, row_lo, row_hi, col_lo, col_hi, w_e, w_w, w_n, w_s, edges, sems, small_sems) = refs
    small = [(ocean_hbm, ocean_ref), (row_lo_hbm, row_lo), (row_hi_hbm, row_hi), (col_lo_hbm, col_lo), (col_hi_hbm, col_hi)]
    if first == 0:
        small += [(depth_hbm, depth_ref), (tops_hbm, tops)]
    small = [pltpu.make_async_copy(a, b, small_sems.at[i]) for i, (a, b) in enumerate(small)]

    def tracers_in(k):
        return pltpu.make_async_copy(t_hbm.at[first : first + 2, k], t_ref.at[:, k], sems.at[0, k])

    def velocity_in(k):
        return pltpu.make_async_copy(v_hbm.at[:, k], v_ref.at[:, k], sems.at[1, k])

    def tracers_out(k):
        return pltpu.make_async_copy(out_ref.at[:, k], out_hbm.at[first : first + 2, k], sems.at[2, k])

    for copy in small:
        copy.start()
    for k in range(LEVELS):
        tracers_in(k).start()
        velocity_in(k).start()
    for copy in small:
        copy.wait()
    even = lanes((8, LANE)) % 2 == 0
    load_wet = lambda at: ocean_ref[at : at + 8, :].astype(jnp.float32)
    for r in range(TILES):
        rows = pl.ds(8 * r, 8)
        edge = jnp.where(even, col_lo[rows, :], col_hi[rows, :])
        edges[rows, :] = edge
        here = load_wet(8 * r)
        w_e[rows, :] = here * above(load_wet, row_hi[WET : WET + 1, :], r)
        w_w[rows, :] = here * below(load_wet, row_lo[WET : WET + 1, :], r)
        behind, ahead = sided(here, pltpu.roll(edge, LANE - 2 * WET, 1))
        w_n[rows, :] = here * ahead
        w_s[rows, :] = here * behind
        if first == 0:
            total[rows, :] = jnp.zeros((8, COLS), jnp.float32)
    if first == 0:
        flux[...] = jnp.zeros((8, COLS), jnp.float32)

    def level(k, _):
        tracers_in(k).wait()
        velocity_in(k).wait()
        before_u = row_lo[pl.ds(SPEED + k, 1), :]
        for r in range(TILES):
            rows = pl.ds(8 * r, 8)
            load_u = lambda at: v_ref[0, k, at : at + 8, :]
            u = load_u(8 * r)
            u_behind = below(load_u, before_u, r)
            v = v_ref[1, k, rows, :]
            edge_tile = edges[rows, :]
            lane = lanes((8, LANE))
            va, vb = pltpu.roll(v[:, :LANE], 1, 1), pltpu.roll(v[:, LANE:], 1, 1)
            v_edge = pltpu.roll(edge_tile, LANE - 2 * (SPEED + k), 1)
            v_behind = jnp.concatenate([jnp.where(lane == 0, v_edge, va), jnp.where(lane == 0, va, vb)], 1)
            we, ww, wn, ws = w_e[rows, :], w_w[rows, :], w_n[rows, :], w_s[rows, :]
            ahead_x = negative(u) * we
            behind_x = positive(u_behind) * ww
            ahead_y = negative(v) * wn
            behind_y = positive(v_behind) * ws
            center = (1.0 - (positive(u) * we - negative(u_behind) * ww)) - (positive(v) * wn - negative(v_behind) * ws)
            new = []
            for t in range(2):
                load = lambda at: t_ref[t, k, at : at + 8, :]
                slot = (first + t) * LEVELS + k
                c = load(8 * r)
                c_below = below(load, row_lo[pl.ds(slot, 1), :], r)
                c_above = above(load, row_hi[pl.ds(slot, 1), :], r)
                c_behind, c_ahead = sided(c, pltpu.roll(edge_tile, LANE - 2 * slot, 1))
                value = center * c - (ahead_x * c_above - behind_x * c_below) - (ahead_y * c_ahead - behind_y * c_behind)
                out_ref[t, k, rows, :] = value
                new.append(value)
            if first == 0:
                total[rows, :] = total[rows, :] + thick[k] * (0.2 * new[0] - 0.8 * new[1])
        if first == 0:
            mixed = lambda a, b: 0.2 * a - 0.8 * b
            q_before = mixed(row_lo[pl.ds(k, 1), :], row_lo[pl.ds(LEVELS + k, 1), :])
            q_after = mixed(row_hi[pl.ds(k, 1), :], row_hi[pl.ds(LEVELS + k, 1), :])
            q_first = mixed(t_ref[0, k, 0:1, :], t_ref[1, k, 0:1, :])
            q_last = mixed(t_ref[0, k, ROWS - 1 : ROWS, :], t_ref[1, k, ROWS - 1 : ROWS, :])
            u_last = v_ref[0, k, ROWS - 1 : ROWS, :]
            flux[0:1, :] = flux[0:1, :] + thick[k] * (positive(before_u) * q_before + negative(before_u) * q_first)
            flux[1:2, :] = flux[1:2, :] + thick[k] * (positive(u_last) * q_last + negative(u_last) * q_after)
        tracers_out(k).start()
        return 0

    lax.fori_loop(0, LEVELS, level, 0)

    if first == 0:
        row = sublanes((4, COLS))
        wet_first = load_wet(0)[0:1, :]
        wet_last = load_wet(ROWS - 8)[7:8, :]
        flux_lo = flux[0:1, :] * (row_lo[WET : WET + 1, :] * wet_first)
        flux_hi = flux[1:2, :] * (row_hi[WET : WET + 1, :] * wet_last)
        ext[0, 0:4, :] = row_lo[PART:COEF, :] - jnp.where(row == 3, flux_lo, 0.0)
        ext[0, ROWS + 4 :, :] = row_hi[PART:COEF, :] + jnp.where(row == 0, flux_hi, 0.0)
        ext[1, 0:4, :] = row_lo[COEF:EDGE, :]
        ext[1, ROWS + 4 :, :] = row_hi[COEF:EDGE, :]
        for r in range(TILES):
            rows = pl.ds(8 * r, 8)
            here = load_wet(8 * r)
            ext[0, 8 * r + 4 : 8 * r + 12, :] = total[rows, :] * here
            ext[1, 8 * r + 4 : 8 * r + 12, :] = coefficient(depth_ref[rows, :], here)
        most = jnp.max(tops[...], axis=0)
        tile = sublanes((8, LANE))
        for j in range(8):
            send_ref[j, 0:EXT, :] = ext[0, 16 * j : 16 * j + EXT, :]
            send_ref[j, EXT : 2 * EXT, :] = ext[1, 16 * j : 16 * j + EXT, :]
            edge = jnp.zeros((8, LANE), jnp.float32)
            if j == 0:
                edge = jnp.where((tile >= 1) & (tile <= 3), pltpu.roll(row_lo[EDGE:MESSAGE, :LANE], 4, 0), 0.0)
            if j == 7:
                edge = jnp.where((tile >= 4) & (tile <= 6), pltpu.roll(row_hi[EDGE:MESSAGE, :LANE], 4, 0), 0.0)
            send_ref[j, 2 * EXT : 2 * EXT + 8, :LANE] = edge
            send_ref[j, 2 * EXT : 2 * EXT + 8, LANE:] = most
    for k in range(LEVELS):
        tracers_out(k).wait()


def advect(first, tracers, velocity, ocean, row_lo, row_hi, col_lo, col_hi, extra):
    ins = [ANY] * 7
    operands = [tracers, velocity, ocean, row_lo, row_hi, col_lo, col_hi]
    out_specs = [ANY]
    out_shape = [f32(TRACERS, LEVELS, ROWS, COLS)]
    block = pltpu.VMEM((ROWS, COLS), jnp.float32)
    scratch = [
        pltpu.VMEM((2, LEVELS, ROWS, COLS), jnp.float32),
        pltpu.VMEM((2, LEVELS, ROWS, COLS), jnp.float32),
        pltpu.VMEM((2, LEVELS, ROWS, COLS), jnp.float32),
        pltpu.VMEM((ROWS, COLS), jnp.int32),
        pltpu.VMEM((MESSAGE, COLS), jnp.float32),
        pltpu.VMEM((MESSAGE, COLS), jnp.float32),
        pltpu.VMEM((ROWS, LANE), jnp.float32),
        pltpu.VMEM((ROWS, LANE), jnp.float32),
        block,
        block,
        block,
        block,
        pltpu.VMEM((ROWS, LANE), jnp.float32),
        pltpu.SemaphoreType.DMA((3, LEVELS)),
        pltpu.SemaphoreType.DMA((7,)),
    ]
    aliases = {}
    if first == 0:
        thickness, depth, tops = extra
        ins = [SMEM] + ins + [ANY, ANY]
        operands = [thickness] + operands + [depth, tops]
        out_specs.append(VMEM)
        out_shape.append(f32(8, 2 * EXT + 8, COLS))
        scratch += [
            block,
            pltpu.VMEM((16, 8, LANE), jnp.float32),
            block,
            pltpu.VMEM((8, COLS), jnp.float32),
            pltpu.VMEM((2, ROWS + 8, COLS), jnp.float32),
        ]
    else:
        aliases = {len(operands): 0}
        ins = ins + [ANY]
        operands = operands + [extra]
    return pl.pallas_call(
        functools.partial(advect_kernel, first),
        in_specs=ins,
        out_specs=out_specs,
        out_shape=out_shape,
        scratch_shapes=scratch,
        input_output_aliases=aliases,
        compiler_params=pltpu.CompilerParams(vmem_limit_bytes=16 * 2**20),
        cost_estimate=pl.CostEstimate(flops=24_000_000, bytes_accessed=9_400_000, transcendentals=0),
        name="advect_forcing" if first == 0 else "advect_rest",
    )(*operands)


NEAR = ((1, 0, 0.5), (-1, 0, 0.5), (0, 1, 0.5), (0, -1, 0.5), (1, 1, 0.125), (1, -1, 0.125), (-1, 1, 0.125), (-1, -1, 0.125))


def moved(x, rows, cols):
    if cols:
        lane = lanes(x.shape)
        x = pltpu.roll(x, (-cols) % x.shape[1], 1)
        x = jnp.where(lane == (x.shape[1] - 1 if cols > 0 else 0), 0.0, x)
    if rows:
        x = pltpu.roll(x, (-rows) % x.shape[0], 0)
    return x


def solve_kernel(got_ref, out_ref, h_ref, f_ref, weight):
    for j in range(8):
        cols = pl.ds(j * COLS, COLS)
        f_ref[:, cols] = got_ref[j, 0:EXT, :]
        h_ref[:, cols] = got_ref[j, EXT : 2 * EXT, :]
    lane, tile = lanes((8, LANE)), sublanes((8, LANE))
    edge_rows = pl.ds(2 * EXT, 8)
    for j in range(7):
        pairs = got_ref[j, edge_rows, :LANE] * pltpu.roll(got_ref[j + 1, edge_rows, :LANE], LANE - 16, 1)
        flux = jnp.sum(jnp.where(lane <= LEVELS, pairs, 0.0), axis=1, keepdims=True)
        for rows, there in ((pl.ds(0, 8), tile < 4), (pl.ds(16, 8), tile >= 4)):
            last = pl.ds((j + 1) * COLS - LANE, LANE)
            after = pl.ds((j + 1) * COLS, LANE)
            f_ref[rows, last] = f_ref[rows, last] - jnp.where(there & (lane == LANE - 1), flux, 0.0)
            f_ref[rows, after] = f_ref[rows, after] + jnp.where(there & (lane == 0), flux, 0.0)
    most = jnp.max(got_ref[:, 2 * EXT : 2 * EXT + 8, LANE:], axis=0)[0:1, 0:1]
    lam_max = 0.5 + 10.0 * most
    theta = (lam_max + 0.5) / 2.0
    delta = (lam_max - 0.5) / 2.0
    sigma = theta / delta
    rho = 1.0 / sigma
    h = h_ref[...]
    sides = {c: moved(h, 0, c) for c in (-1, 0, 1)}
    for n, (a, b, w) in enumerate(NEAR):
        weight[n] = w * (h + moved(sides[b], a, 0))
    inside = h > 0.0
    resid = f_ref[...]
    direction = resid / theta
    answer = jnp.zeros_like(resid)
    for _ in range(ITERS):
        sides = {c: moved(direction, 0, c) for c in (-1, 0, 1)}
        applied = 0.5 * direction
        for n, (a, b, w) in enumerate(NEAR):
            applied = applied + weight[n] * (direction - moved(sides[b], a, 0))
        resid = jnp.where(inside, resid - applied, 0.0)
        answer = answer + direction
        rho_next = 1.0 / (2.0 * sigma - rho)
        direction = rho_next * rho * direction + (2.0 * rho_next / delta) * resid
        rho = rho_next
    out_ref[...] = (answer + direction)[4:20, :]


def solve(got):
    return pl.pallas_call(
        solve_kernel,
        in_specs=[VMEM],
        out_specs=VMEM,
        out_shape=f32(16, WIDE),
        scratch_shapes=[
            pltpu.VMEM((EXT, WIDE), jnp.float32),
            pltpu.VMEM((EXT, WIDE), jnp.float32),
            pltpu.VMEM((8, EXT, WIDE), jnp.float32),
        ],
        compiler_params=pltpu.CompilerParams(vmem_limit_bytes=12 * 2**20),
        cost_estimate=pl.CostEstimate(flops=6_000_000, bytes_accessed=600_000, transcendentals=0),
        name="chebyshev",
    )(got)


def send(x, axis, step):
    count = lax.axis_size(axis)
    pairs = [(i, i + step) for i in range(count) if 0 <= i + step < count]
    return lax.ppermute(x, axis, pairs)


def shards(tracers, velocity, ocean, thickness, depth):
    row_hi, row_lo, col_hi, col_lo, top = pack(thickness, tracers, velocity, ocean, depth)
    halos = (send(row_hi, "bx", 1), send(row_lo, "bx", -1), send(col_hi, "by", 1), send(col_lo, "by", -1))
    tops = lax.all_to_all(top, "bx", split_axis=0, concat_axis=0, tiled=True)
    part, parcels = advect(0, tracers, velocity, ocean, *halos, (thickness, depth, tops))
    got = lax.all_to_all(parcels, "by", split_axis=0, concat_axis=0, tiled=True)
    new_tracers = advect(2, tracers, velocity, ocean, *halos, part)[0]
    return new_tracers, solve(got)


def solution(mesh):
    return jax.shard_map(
        shards,
        mesh=mesh,
        in_specs=(
            P(None, None, "bx", "by"),
            P(None, None, "bx", "by"),
            P("bx", "by"),
            P(),
            P("bx", "by"),
        ),
        out_specs=(P(None, None, "bx", "by"), P(("bx", "by"), None)),
        check_vma=False,
    )
```

time: 87.5 us -> 66.1 us (0.76)
  the two profiles are of different devices: /device:TPU:2 before, /device:TPU:1 now
where the time goes in v2:
time: 66.1 us; the launch traced here: 65.6 us
  Pallas kernels  20.2 us (31%)
  starting transfers between devices  18.8 us (28%)
  blocking collectives  14.1 us (21%)
  local copies, waits for them, and re-layouts  11.5 us (17%)
  between operations  0.79 us (1%)
    all_to_all x1, blocking collectives, shards(): tops = lax.all_to_all(top, 'bx', split_axis=0, concat_axis=0, tiled=True)  14.1 us
    pallas_call x2, Pallas kernels, advect(): pl.pallas_call(functools.partial(advect_kernel, first), in_specs=ins, out...  12.7 us
    ppermute x4, starting transfers between devices, send(): return lax.ppermute(x, axis, pairs)  11.9 us
    unnamed x26, local copies, waits for them, and re-layouts  11.5 us
    all_to_all x1, starting transfers between devices, shards(): got = lax.all_to_all(parcels, 'by', split_axis=0, concat_axis=0, tiled=True)  6.95 us
    pallas_call x1, Pallas kernels, pack(): pl.pallas_call(pack_kernel, in_specs=[SMEM, ANY, ANY, ANY, ANY], out_spec...  4.38 us
    pallas_call x1, Pallas kernels, solve(): pl.pallas_call(solve_kernel, in_specs=[VMEM], out_specs=VMEM, out_shape=f...  3.11 us
  transfers between devices with their start and end apart: 5, of which 0 were waited for; matrix products, arithmetic and copies ran while one was open for 0% of the time, Pallas kernels for 9%

profile of v2, /device:TPU:1, one launch (start us, length us, event | category | flops | bytes accessed | tf_op | source)
XLA Modules:
  0.0 65.6 jit_solution(2329633790799407064)
XLA Ops:
  0.6 0.0 copy-start
  0.6 2.8 %copy-done = f32[4,12,128,256]{3,2,1,0:T(8,128)S(1)} copy-done((f32[4,12,128,256]{3,2,1,0:T(8,128)S(1)}, f32[4,12,128,256]{3,2,1,0:T(8,128)}, u32[]{:S(2)}) %copy-start) | copy-done | bytes 6291480
  3.4 0.0 copy-start.3
  3.4 1.9 %copy-done.3 = f32[2,12,128,256]{3,2,1,0:T(8,128)S(1)} copy-done((f32[2,12,128,256]{3,2,1,0:T(8,128)S(1)}, f32[2,12,128,256]{3,2,1,0:T(8,128)}, u32[]{:S(2)}) %copy-start.3) | copy-done | bytes 3145752
  5.3 0.0 copy-start.5
  5.3 0.9 %copy-done.5 = s32[128,256]{1,0:T(8,128)S(1)} copy-done((s32[128,256]{1,0:T(8,128)S(1)}, s32[128,256]{1,0:T(8,128)}, u32[]{:S(2)}) %copy-start.5) | copy-done | bytes 131096
  6.2 0.0 copy-start.7
  6.2 0.9 %copy-done.7 = f32[128,256]{1,0:T(8,128)S(1)} copy-done((f32[128,256]{1,0:T(8,128)S(1)}, f32[128,256]{1,0:T(8,128)}, u32[]{:S(2)}) %copy-start.7) | copy-done | bytes 131096
  7.1 0.0 copy-start.11
  7.1 0.7 copy-done.11
  7.8 0.0 copy-start.1
  7.8 0.0 copy-start.12
  7.8 4.4 %pack_edges.1 = (f32[80,256]{1,0:T(8,128)S(1)}, f32[80,256]{1,0:T(8,128)S(1)}, f32[128,128]{1,0:T(8,128)S(1)}, f32[128,128]{1,0:T(8,128)S(1)}, f32[16,8,128]{2,1,0:T(8,128)S(1)}) custom-call(f32[12]{0:T(128)S(1)} %copy-done.11, f32[4,12,128,256]{3,2,1,0:T(8,128)S(1)} %copy-done, f32[2,12,128,256]{3,2,1,0:T(8,128)S(1)} %copy-done.3, ...), custom_call_target="tpu_custom_call" | custom-call | flops 4000000 | bytes 7400000 | tf_op jit(solution)/shard_map/pack_edges/pallas_call | solution.py:157
  12.2 0.0 copy-start.4
  12.2 0.0 copy-start.6
  12.2 4.3 %collective-permute-start = (f32[80,256]{1,0:T(8,128)S(1)}, f32[80,256]{1,0:T(8,128)S(1)}, u32[]{:S(2)}, u32[]{:S(2)}) collective-permute-start(f32[80,256]{1,0:T(8,128)S(1)} %get-tuple-element.9), channel_id=1, source_target_pairs={{0,8},{8,16},{16,24},{24,32},{32,40},{40,48},{48,56},{56,64},{64,7... | collective-permute-start | bytes 245768 | tf_op jit(solution)/shard_map/ppermute | solution.py:455
  16.5 1.3 %collective-permute-start.1 = (f32[80,256]{1,0:T(8,128)S(1)}, f32[80,256]{1,0:T(8,128)S(1)}, u32[]{:S(2)}, u32[]{:S(2)}) collective-permute-start(f32[80,256]{1,0:T(8,128)S(1)} %get-tuple-element.10), channel_id=1, source_target_pairs={{8,0},{16,8},{24,16},{32,24},{40,32},{48,40},{56,48},{64,56},{72,6... | collective-permute-start | bytes 245768 | tf_op jit(solution)/shard_map/ppermute | solution.py:455
  17.8 4.4 %collective-permute-start.2 = (f32[128,128]{1,0:T(8,128)S(1)}, f32[128,128]{1,0:T(8,128)S(1)}, u32[]{:S(2)}, u32[]{:S(2)}) collective-permute-start(f32[128,128]{1,0:T(8,128)S(1)} %get-tuple-element.11), channel_id=1, source_target_pairs={{0,1},{1,2},{2,3},{3,4},{4,5},{5,6},{6,7},{8,9},{9,10},{10,11},{11... | collective-permute-start | bytes 196616 | tf_op jit(solution)/shard_map/ppermute | solution.py:455
  22.2 1.9 %collective-permute-start.3 = (f32[128,128]{1,0:T(8,128)S(1)}, f32[128,128]{1,0:T(8,128)S(1)}, u32[]{:S(2)}, u32[]{:S(2)}) collective-permute-start(f32[128,128]{1,0:T(8,128)S(1)} %get-tuple-element.12), channel_id=1, source_target_pairs={{1,0},{2,1},{3,2},{4,3},{5,4},{6,5},{7,6},{9,8},{10,9},{11,10},{12... | collective-permute-start | bytes 196616 | tf_op jit(solution)/shard_map/ppermute | solution.py:455
  24.1 14.1 %all_to_all.10.refs_9_ = f32[16,8,128]{2,1,0:T(8,128)S(1)} all-to-all(f32[16,8,128]{2,1,0:T(8,128)S(1)} %get-tuple-element.13), channel_id=1, replica_groups=mesh['bx'=16,'by'=8] {'bx'}, dimensions={0} | all-to-all | bytes 131072 | tf_op jit(solution)/shard_map/all_to_all | solution.py:461
  38.3 0.0 collective-permute-done.2.refs_6_.refs_5_
  38.3 0.0 collective-permute-done.3.refs_7_.refs_6_
  38.3 0.0 copy-start.9
  38.3 0.0 collective-permute-done.refs_4_.refs_3_
  38.3 0.0 collective-permute-done.1.refs_5_.refs_4_
  38.3 0.0 copy-done.1
  38.3 0.0 copy-done.12
  38.3 7.0 %advect_forcing.1 = (f32[4,12,128,256]{3,2,1,0:T(8,128)}, f32[8,56,256]{2,1,0:T(8,128)S(1)}) custom-call(f32[12]{0:T(128)S(1)} %copy-done.12, f32[4,12,128,256]{3,2,1,0:T(8,128)S(1)} %copy-done.1, f32[2,12,128,256]{3,2,1,0:T(8,128)S(1)} %copy-done.3, s32[128,256]{1,0:T(8,128)S(1)} %copy-done.5, f32[80,256]{1,0:T(8,128)S(1)} %collective-permute-done.refs_4_.refs_3_, ...), custom_call_target="tpu_custom_call" | custom-call | flops 24000000 | bytes 9400000 | tf_op jit(solution)/shard_map/advect_forcing/pallas_call | solution.py:367
  45.3 0.0 copy-done.9
  45.3 0.0 copy-start.8
  45.3 0.8 %copy-done.8 = f32[8,56,256]{2,1,0:T(8,128)} copy-done((f32[8,56,256]{2,1,0:T(8,128)}, f32[8,56,256]{2,1,0:T(8,128)S(1)}, u32[]{:S(2)}) %copy-start.8) | copy-done | bytes 458776
  46.1 6.9 %all-to-all-start.1 = ((f32[8,56,256]{2,1,0:T(8,128)}), f32[8,56,256]{2,1,0:T(8,128)}, u32[]{:S(2)}, u32[]{:S(2)}) async-start(f32[8,56,256]{2,1,0:T(8,128)} %copy-done.8), calls=%async_computation.1 | async-start | bytes 917504 | tf_op jit(solution)/shard_map/all_to_all | solution.py:463
  53.0 0.0 copy-done.4
  53.0 0.0 copy-done.6
  53.0 0.0 copy-start.2
  53.0 2.8 %copy-done.2 = f32[4,12,128,256]{3,2,1,0:T(8,128)S(1)} copy-done((f32[4,12,128,256]{3,2,1,0:T(8,128)S(1)}, f32[4,12,128,256]{3,2,1,0:T(8,128)}, u32[]{:S(2)}) %copy-start.2) | copy-done | bytes 6291480
  55.8 0.0 copy-start.10
  55.8 0.8 %copy-done.10 = f32[128,128]{1,0:T(8,128)S(1)} copy-done((f32[128,128]{1,0:T(8,128)S(1)}, f32[128,128]{1,0:T(8,128)}, u32[]{:S(2)}) %copy-start.10) | copy-done | bytes 65560
  56.6 5.8 %advect_rest.1 = f32[4,12,128,256]{3,2,1,0:T(8,128)} custom-call(f32[4,12,128,256]{3,2,1,0:T(8,128)S(1)} %copy-done.2, f32[2,12,128,256]{3,2,1,0:T(8,128)S(1)} %copy-done.4, s32[128,256]{1,0:T(8,128)S(1)} %copy-done.6, f32[80,256]{1,0:T(8,128)S(1)} %collective-permute-done.refs_4_.refs_3_, ...), custom_call_target="tpu_custom_call", output_to_operand_aliasing={{}: (7, {})} | custom-call | flops 24000000 | bytes 9400000 | tf_op jit(solution)/shard_map/advect_rest/pallas_call | solution.py:367
  62.4 0.0 all-to-all-done.1.got_ref
  62.5 3.1 %chebyshev.1 = f32[16,2048]{1,0:T(8,128)} custom-call(f32[8,56,256]{2,1,0:T(8,128)} %all-to-all-done.1.got_ref), custom_call_target="tpu_custom_call" | custom-call | flops 6000000 | bytes 600000 | tf_op jit(solution)/shard_map/chebyshev/pallas_call | solution.py:436
Async XLA Ops:
  0.6 2.8 %copy-start = (f32[4,12,128,256]{3,2,1,0:T(8,128)S(1)}, f32[4,12,128,256]{3,2,1,0:T(8,128)}, u32[]{:S(2)}) copy-start(f32[4,12,128,256]{3,2,1,0:T(8,128)} %refs_0_.3) | copy-start | bytes 18874372
  3.4 1.9 %copy-start.3 = (f32[2,12,128,256]{3,2,1,0:T(8,128)S(1)}, f32[2,12,128,256]{3,2,1,0:T(8,128)}, u32[]{:S(2)}) copy-start(f32[2,12,128,256]{3,2,1,0:T(8,128)} %refs_1_.3) | copy-start | bytes 9437188
  5.3 0.9 %copy-start.5 = (s32[128,256]{1,0:T(8,128)S(1)}, s32[128,256]{1,0:T(8,128)}, u32[]{:S(2)}) copy-start(s32[128,256]{1,0:T(8,128)} %refs_2_.3) | copy-start | bytes 393220
  6.2 0.9 %copy-start.7 = (f32[128,256]{1,0:T(8,128)S(1)}, f32[128,256]{1,0:T(8,128)}, u32[]{:S(2)}) copy-start(f32[128,256]{1,0:T(8,128)} %refs_8_.1) | copy-start | bytes 393220
  7.1 0.7 copy-start.11
  7.8 30.5 %copy-start.1 = (f32[4,12,128,256]{3,2,1,0:T(8,128)S(1)}, f32[4,12,128,256]{3,2,1,0:T(8,128)}, u32[]{:S(2)}) copy-start(f32[4,12,128,256]{3,2,1,0:T(8,128)} %refs_0_.3) | copy-start | bytes 18874372
  7.8 30.5 %copy-start.12 = (f32[12]{0:T(128)S(1)}, f32[12]{0:T(128)}, u32[]{:S(2)}) copy-start(f32[12]{0:T(128)} %refs_0_.2) | copy-start | bytes 148
  12.2 40.8 %copy-start.4 = (f32[2,12,128,256]{3,2,1,0:T(8,128)S(1)}, f32[2,12,128,256]{3,2,1,0:T(8,128)}, u32[]{:S(2)}) copy-start(f32[2,12,128,256]{3,2,1,0:T(8,128)} %refs_1_.3) | copy-start | bytes 9437188
  12.2 40.8 %copy-start.6 = (s32[128,256]{1,0:T(8,128)S(1)}, s32[128,256]{1,0:T(8,128)}, u32[]{:S(2)}) copy-start(s32[128,256]{1,0:T(8,128)} %refs_2_.3) | copy-start | bytes 393220
  12.2 26.1 %collective-permute-start = (f32[80,256]{1,0:T(8,128)S(1)}, f32[80,256]{1,0:T(8,128)S(1)}, u32[]{:S(2)}, u32[]{:S(2)}) collective-permute-start(f32[80,256]{1,0:T(8,128)S(1)} %get-tuple-element.9), channel_id=1, source_target_pairs={{0,8},{8,16},{16,24},{24,32},{32,40},{40,48},{48,56},{56,64},{64,7... | collective-permute-start | bytes 245768 | tf_op jit(solution)/shard_map/ppermute | solution.py:455
  16.5 21.8 %collective-permute-start.1 = (f32[80,256]{1,0:T(8,128)S(1)}, f32[80,256]{1,0:T(8,128)S(1)}, u32[]{:S(2)}, u32[]{:S(2)}) collective-permute-start(f32[80,256]{1,0:T(8,128)S(1)} %get-tuple-element.10), channel_id=1, source_target_pairs={{8,0},{16,8},{24,16},{32,24},{40,32},{48,40},{56,48},{64,56},{72,6... | collective-permute-start | bytes 245768 | tf_op jit(solution)/shard_map/ppermute | solution.py:455
  17.8 20.5 %collective-permute-start.2 = (f32[128,128]{1,0:T(8,128)S(1)}, f32[128,128]{1,0:T(8,128)S(1)}, u32[]{:S(2)}, u32[]{:S(2)}) collective-permute-start(f32[128,128]{1,0:T(8,128)S(1)} %get-tuple-element.11), channel_id=1, source_target_pairs={{0,1},{1,2},{2,3},{3,4},{4,5},{5,6},{6,7},{8,9},{9,10},{10,11},{11... | collective-permute-start | bytes 196616 | tf_op jit(solution)/shard_map/ppermute | solution.py:455
  22.2 16.1 %collective-permute-start.3 = (f32[128,128]{1,0:T(8,128)S(1)}, f32[128,128]{1,0:T(8,128)S(1)}, u32[]{:S(2)}, u32[]{:S(2)}) collective-permute-start(f32[128,128]{1,0:T(8,128)S(1)} %get-tuple-element.12), channel_id=1, source_target_pairs={{1,0},{2,1},{3,2},{4,3},{5,4},{6,5},{7,6},{9,8},{10,9},{11,10},{12... | collective-permute-start | bytes 196616 | tf_op jit(solution)/shard_map/ppermute | solution.py:455
  38.3 7.0 %copy-start.9 = (f32[128,128]{1,0:T(8,128)}, f32[128,128]{1,0:T(8,128)S(1)}, u32[]{:S(2)}) copy-start(f32[128,128]{1,0:T(8,128)S(1)} %collective-permute-done.3.refs_7_.refs_6_) | copy-start | bytes 196612
  45.3 0.8 %copy-start.8 = (f32[8,56,256]{2,1,0:T(8,128)}, f32[8,56,256]{2,1,0:T(8,128)S(1)}, u32[]{:S(2)}) copy-start(f32[8,56,256]{2,1,0:T(8,128)S(1)} %get-tuple-element.15) | copy-start | bytes 1376260
  46.1 16.4 %all-to-all-start.1 = ((f32[8,56,256]{2,1,0:T(8,128)}), f32[8,56,256]{2,1,0:T(8,128)}, u32[]{:S(2)}, u32[]{:S(2)}) async-start(f32[8,56,256]{2,1,0:T(8,128)} %copy-done.8), calls=%async_computation.1 | async-start | bytes 917504 | tf_op jit(solution)/shard_map/all_to_all | solution.py:463
  53.0 2.8 %copy-start.2 = (f32[4,12,128,256]{3,2,1,0:T(8,128)S(1)}, f32[4,12,128,256]{3,2,1,0:T(8,128)}, u32[]{:S(2)}) copy-start(f32[4,12,128,256]{3,2,1,0:T(8,128)} %refs_0_.3) | copy-start | bytes 18874372
  55.8 0.8 %copy-start.10 = (f32[128,128]{1,0:T(8,128)S(1)}, f32[128,128]{1,0:T(8,128)}, u32[]{:S(2)}) copy-start(f32[128,128]{1,0:T(8,128)} %copy-done.9) | copy-start | bytes 196612

commit v3 on v2

--- a/solution.py
+++ b/solution.py
@@ -20,8 +20,8 @@
 
 SPEED, WET, PART, COEF, EDGE, MESSAGE = 48, 60, 64, 68, 72, 80
 ANY = pl.BlockSpec(memory_space=pl.ANY)
+HBM = pl.BlockSpec(memory_space=pltpu.HBM)
 VMEM = pl.BlockSpec(memory_space=pltpu.VMEM)
-SMEM = pl.BlockSpec(memory_space=pltpu.SMEM)
 
 
 def f32(*shape):
@@ -78,8 +78,12 @@
     return jnp.where(lane == LEVELS, pltpu.roll(upwind * last, LEVELS + 1, 1), terms)
 
 
-def pack_kernel(thick, t_hbm, v_hbm, ocean_hbm, depth_hbm, row_hi, row_lo, col_hi, col_lo, top,
-                t_ref, u_top, u_low, v_top, v_low, v_last, ocean_ref, depth_ref, sems):
+def pack_kernel(thick_hbm, t_hbm, v_hbm, ocean_hbm, depth_hbm, row_even, row_odd, col_even, col_odd, top,
+                t_ref, u_top, u_low, v_top, v_low, v_last, ocean_ref, depth_ref, thick, row_both, col_both, sems):
+    odd_x, odd_y = lax.axis_index("bx") % 2, lax.axis_index("by") % 2
+    row_hi, row_lo = row_both.at[0], row_both.at[1]
+    col_hi, col_lo = col_both.at[0], col_both.at[1]
+
     def chunk_copy(c):
         rows = pl.ds(pl.multiple_of(c * CHUNK, CHUNK), CHUNK)
         return pltpu.make_async_copy(t_hbm.at[:, :, rows, :], t_ref.at[:, :, rows, :], sems.at[c])
@@ -89,6 +93,7 @@
         pltpu.make_async_copy(ocean_hbm, ocean_ref, sems.at[chunks]),
         pltpu.make_async_copy(depth_hbm, depth_ref, sems.at[chunks + 1]),
         pltpu.make_async_copy(v_hbm.at[1, :, :, LANE:], v_last, sems.at[chunks + 2]),
+        pltpu.make_async_copy(thick_hbm, thick, sems.at[chunks + 7]),
     ]
     tiles = [
         pltpu.make_async_copy(v_hbm.at[0, :, 0:8, :], u_top, sems.at[chunks + 3]),
@@ -150,13 +155,17 @@
         message[COEF:EDGE, :] = coefficient(depth_ref[rows, :], here)[keep : keep + 4, :]
         message[EDGE:MESSAGE, :LANE] = edge_terms(q, speed_y, here, thick)
         message[EDGE:MESSAGE, LANE:] = jnp.zeros((8, LANE), jnp.float32)
+    row_even[...] = row_both[odd_x]
+    row_odd[...] = row_both[1 - odd_x]
+    col_even[...] = col_both[odd_y]
+    col_odd[...] = col_both[1 - odd_y]
 
 
 def pack(thickness, tracers, velocity, ocean, depth):
     tile = (LEVELS, 8, COLS)
     return pl.pallas_call(
         pack_kernel,
-        in_specs=[SMEM, ANY, ANY, ANY, ANY],
+        in_specs=[HBM] * 5,
         out_specs=[VMEM] * 5,
         out_shape=[f32(MESSAGE, COLS), f32(MESSAGE, COLS), f32(ROWS, LANE), f32(ROWS, LANE), f32(16, 8, LANE)],
         scratch_shapes=[
@@ -168,28 +177,27 @@
             pltpu.VMEM((LEVELS, ROWS, LANE), jnp.float32),
             pltpu.VMEM((ROWS, COLS), jnp.int32),
             pltpu.VMEM((ROWS, COLS), jnp.float32),
-            pltpu.SemaphoreType.DMA((ROWS // CHUNK + 7,)),
+            pltpu.SMEM((LEVELS,), jnp.float32),
+            pltpu.VMEM((2, MESSAGE, COLS), jnp.float32),
+            pltpu.VMEM((2, ROWS, LANE), jnp.float32),
+            pltpu.SemaphoreType.DMA((ROWS // CHUNK + 8,)),
         ],
-        compiler_params=pltpu.CompilerParams(vmem_limit_bytes=14 * 2**20),
+        compiler_params=pltpu.CompilerParams(vmem_limit_bytes=60 * 2**20),
         cost_estimate=pl.CostEstimate(flops=4_000_000, bytes_accessed=7_400_000, transcendentals=0),
         name="pack_edges",
     )(thickness, tracers, velocity, ocean, depth)
 
 
-def sided(x, edge):
-    lane = lanes((8, LANE))
-    a, b = x[:, :LANE], x[:, LANE:]
-    ra, rb = pltpu.roll(a, 1, 1), pltpu.roll(b, 1, 1)
-    sa, sb = pltpu.roll(a, LANE - 1, 1), pltpu.roll(b, LANE - 1, 1)
-    behind = jnp.concatenate([jnp.where(lane == 0, edge, ra), jnp.where(lane == 0, ra, rb)], 1)
-    ahead = jnp.concatenate([jnp.where(lane == LANE - 1, sb, sa), jnp.where(lane == LANE - 1, edge, sb)], 1)
-    return behind, ahead
-
-
-def below(load, edge, r):
-    if r:
-        return load(8 * r - 1)
-    return jnp.where(sublanes((8, COLS)) == 0, edge, pltpu.roll(load(0), 1, 0))
+def ahead_y(x, edge):
+    last = lanes((8, LANE)) == LANE - 1
+    a, b = pltpu.roll(x[:, :LANE], LANE - 1, 1), pltpu.roll(x[:, LANE:], LANE - 1, 1)
+    return jnp.concatenate([jnp.where(last, b, a), jnp.where(last, edge, b)], 1)
+
+
+def behind_y(x, edge):
+    first = lanes((8, LANE)) == 0
+    a, b = pltpu.roll(x[:, :LANE], 1, 1), pltpu.roll(x[:, LANE:], 1, 1)
+    return jnp.concatenate([jnp.where(first, edge, a), jnp.where(first, a, b)], 1)
 
 
 def above(load, edge, r):
@@ -198,17 +206,29 @@
     return jnp.where(sublanes((8, COLS)) == 7, edge, pltpu.roll(load(8 * r), 7, 0))
 
 
+def upwind(speed, here, ahead):
+    return speed * jnp.where(speed > 0.0, here, ahead)
+
+
 def advect_kernel(first, *refs):
     if first == 0:
-        (thick, t_hbm, v_hbm, ocean_hbm, row_lo_hbm, row_hi_hbm, col_lo_hbm, col_hi_hbm, depth_hbm, tops_hbm, out_hbm, send_ref,
-         t_ref, v_ref, out_ref, ocean_ref, row_lo, row_hi, col_lo, col_hi, w_e, w_w, w_n, w_s, edges, sems, small_sems,
-         depth_ref, tops, total, flux, ext) = refs
+        (thick_hbm, t_hbm, v_hbm, ocean_hbm, row_even, row_odd, col_even, col_odd, depth_hbm, tops_hbm, out_hbm, send_ref,
+         t_ref, v_ref, out_ref, ocean_ref, rows_in, cols_in, w_x, w_y, before_y, edges, flux_x, sems, small_sems,
+         depth_ref, tops, total, flux, ext, thick) = refs
     else:
-        (t_hbm, v_hbm, ocean_hbm, row_lo_hbm, row_hi_hbm, col_lo_hbm, col_hi_hbm, _, out_hbm,
-         t_ref, v_ref, out_ref, ocean_ref, row_lo, row_hi, col_lo, col_hi, w_e, w_w, w_n, w_s, edges, sems, small_sems) = refs
-    small = [(ocean_hbm, ocean_ref), (row_lo_hbm, row_lo), (row_hi_hbm, row_hi), (col_lo_hbm, col_lo), (col_hi_hbm, col_hi)]
+        (t_hbm, v_hbm, ocean_hbm, row_even, row_odd, col_even, col_odd, _, out_hbm,
+         t_ref, v_ref, out_ref, ocean_ref, rows_in, cols_in, w_x, w_y, before_y, edges, flux_x, sems, small_sems) = refs
+    odd_x, odd_y = lax.axis_index("bx") % 2, lax.axis_index("by") % 2
+    row_lo, row_hi = rows_in.at[0], rows_in.at[1]
+    small = [
+        (ocean_hbm, ocean_ref),
+        (row_even, rows_in.at[1 - odd_x]),
+        (row_odd, rows_in.at[odd_x]),
+        (col_even, cols_in.at[1 - odd_y]),
+        (col_odd, cols_in.at[odd_y]),
+    ]
     if first == 0:
-        small += [(depth_hbm, depth_ref), (tops_hbm, tops)]
+        small += [(depth_hbm, depth_ref), (tops_hbm, tops), (thick_hbm, thick)]
     small = [pltpu.make_async_copy(a, b, small_sems.at[i]) for i, (a, b) in enumerate(small)]
 
     def tracers_in(k):
@@ -231,62 +251,51 @@
     load_wet = lambda at: ocean_ref[at : at + 8, :].astype(jnp.float32)
     for r in range(TILES):
         rows = pl.ds(8 * r, 8)
-        edge = jnp.where(even, col_lo[rows, :], col_hi[rows, :])
+        edge = jnp.where(even, cols_in[0, rows, :], cols_in[1, rows, :])
         edges[rows, :] = edge
         here = load_wet(8 * r)
-        w_e[rows, :] = here * above(load_wet, row_hi[WET : WET + 1, :], r)
-        w_w[rows, :] = here * below(load_wet, row_lo[WET : WET + 1, :], r)
-        behind, ahead = sided(here, pltpu.roll(edge, LANE - 2 * WET, 1))
-        w_n[rows, :] = here * ahead
-        w_s[rows, :] = here * behind
+        wet_edge = pltpu.roll(edge, LANE - 2 * WET, 1)
+        w_x[rows, :] = here * above(load_wet, row_hi[WET : WET + 1, :], r)
+        w_y[rows, :] = here * ahead_y(here, wet_edge)
+        before_y[rows, :] = here[:, :LANE] * wet_edge
         if first == 0:
             total[rows, :] = jnp.zeros((8, COLS), jnp.float32)
+    w_before = load_wet(0)[0:1, :] * row_lo[WET : WET + 1, :]
     if first == 0:
         flux[...] = jnp.zeros((8, COLS), jnp.float32)
 
     def level(k, _):
         tracers_in(k).wait()
         velocity_in(k).wait()
-        before_u = row_lo[pl.ds(SPEED + k, 1), :]
+        u_before = row_lo[pl.ds(SPEED + k, 1), :] * w_before
+        for t in range(2):
+            flux_x[t, 7:8, :] = upwind(u_before, row_lo[pl.ds((first + t) * LEVELS + k, 1), :], t_ref[t, k, 0:1, :])
         for r in range(TILES):
             rows = pl.ds(8 * r, 8)
-            load_u = lambda at: v_ref[0, k, at : at + 8, :]
-            u = load_u(8 * r)
-            u_behind = below(load_u, before_u, r)
-            v = v_ref[1, k, rows, :]
             edge_tile = edges[rows, :]
-            lane = lanes((8, LANE))
-            va, vb = pltpu.roll(v[:, :LANE], 1, 1), pltpu.roll(v[:, LANE:], 1, 1)
-            v_edge = pltpu.roll(edge_tile, LANE - 2 * (SPEED + k), 1)
-            v_behind = jnp.concatenate([jnp.where(lane == 0, v_edge, va), jnp.where(lane == 0, va, vb)], 1)
-            we, ww, wn, ws = w_e[rows, :], w_w[rows, :], w_n[rows, :], w_s[rows, :]
-            ahead_x = negative(u) * we
-            behind_x = positive(u_behind) * ww
-            ahead_y = negative(v) * wn
-            behind_y = positive(v_behind) * ws
-            center = (1.0 - (positive(u) * we - negative(u_behind) * ww)) - (positive(v) * wn - negative(v_behind) * ws)
+            u = v_ref[0, k, rows, :] * w_x[rows, :]
+            v = v_ref[1, k, rows, :] * w_y[rows, :]
+            v_before = pltpu.roll(edge_tile, LANE - 2 * (SPEED + k), 1) * before_y[rows, :]
             new = []
             for t in range(2):
                 load = lambda at: t_ref[t, k, at : at + 8, :]
                 slot = (first + t) * LEVELS + k
                 c = load(8 * r)
-                c_below = below(load, row_lo[pl.ds(slot, 1), :], r)
-                c_above = above(load, row_hi[pl.ds(slot, 1), :], r)
-                c_behind, c_ahead = sided(c, pltpu.roll(edge_tile, LANE - 2 * slot, 1))
-                value = center * c - (ahead_x * c_above - behind_x * c_below) - (ahead_y * c_ahead - behind_y * c_behind)
+                c_edge = pltpu.roll(edge_tile, LANE - 2 * slot, 1)
+                here_x = upwind(u, c, above(load, row_hi[pl.ds(slot, 1), :], r))
+                flux_x[t, 8 * r + 8 : 8 * r + 16, :] = here_x
+                here_y = upwind(v, c, ahead_y(c, c_edge))
+                past_y = behind_y(here_y, upwind(v_before, c_edge, c[:, :LANE]))
+                past_x = flux_x[t, 8 * r + 7 : 8 * r + 15, :]
+                value = (c - (here_x - past_x)) - (here_y - past_y)
                 out_ref[t, k, rows, :] = value
                 new.append(value)
             if first == 0:
-                total[rows, :] = total[rows, :] + thick[k] * (0.2 * new[0] - 0.8 * new[1])
+                total[rows, :] = total[rows, :] + ((0.2 * thick[k]) * new[0] - (0.8 * thick[k]) * new[1])
         if first == 0:
-            mixed = lambda a, b: 0.2 * a - 0.8 * b
-            q_before = mixed(row_lo[pl.ds(k, 1), :], row_lo[pl.ds(LEVELS + k, 1), :])
-            q_after = mixed(row_hi[pl.ds(k, 1), :], row_hi[pl.ds(LEVELS + k, 1), :])
-            q_first = mixed(t_ref[0, k, 0:1, :], t_ref[1, k, 0:1, :])
-            q_last = mixed(t_ref[0, k, ROWS - 1 : ROWS, :], t_ref[1, k, ROWS - 1 : ROWS, :])
-            u_last = v_ref[0, k, ROWS - 1 : ROWS, :]
-            flux[0:1, :] = flux[0:1, :] + thick[k] * (positive(before_u) * q_before + negative(before_u) * q_first)
-            flux[1:2, :] = flux[1:2, :] + thick[k] * (positive(u_last) * q_last + negative(u_last) * q_after)
+            mixed = lambda row: thick[k] * (0.2 * flux_x[0, row : row + 1, :] - 0.8 * flux_x[1, row : row + 1, :])
+            flux[0:1, :] = flux[0:1, :] + mixed(7)
+            flux[1:2, :] = flux[1:2, :] + mixed(ROWS + 7)
         tracers_out(k).start()
         return 0
 
@@ -294,12 +303,8 @@
 
     if first == 0:
         row = sublanes((4, COLS))
-        wet_first = load_wet(0)[0:1, :]
-        wet_last = load_wet(ROWS - 8)[7:8, :]
-        flux_lo = flux[0:1, :] * (row_lo[WET : WET + 1, :] * wet_first)
-        flux_hi = flux[1:2, :] * (row_hi[WET : WET + 1, :] * wet_last)
-        ext[0, 0:4, :] = row_lo[PART:COEF, :] - jnp.where(row == 3, flux_lo, 0.0)
-        ext[0, ROWS + 4 :, :] = row_hi[PART:COEF, :] + jnp.where(row == 0, flux_hi, 0.0)
+        ext[0, 0:4, :] = row_lo[PART:COEF, :] - jnp.where(row == 3, flux[0:1, :], 0.0)
+        ext[0, ROWS + 4 :, :] = row_hi[PART:COEF, :] + jnp.where(row == 0, flux[1:2, :], 0.0)
         ext[1, 0:4, :] = row_lo[COEF:EDGE, :]
         ext[1, ROWS + 4 :, :] = row_hi[COEF:EDGE, :]
         for r in range(TILES):
@@ -323,33 +328,32 @@
         tracers_out(k).wait()
 
 
-def advect(first, tracers, velocity, ocean, row_lo, row_hi, col_lo, col_hi, extra):
-    ins = [ANY] * 7
-    operands = [tracers, velocity, ocean, row_lo, row_hi, col_lo, col_hi]
-    out_specs = [ANY]
+def advect(first, tracers, velocity, ocean, row_even, row_odd, col_even, col_odd, extra):
+    ins = [HBM] * 3 + [ANY] * 4
+    operands = [tracers, velocity, ocean, row_even, row_odd, col_even, col_odd]
+    out_specs = [HBM]
     out_shape = [f32(TRACERS, LEVELS, ROWS, COLS)]
     block = pltpu.VMEM((ROWS, COLS), jnp.float32)
+    narrow = pltpu.VMEM((ROWS, LANE), jnp.float32)
     scratch = [
         pltpu.VMEM((2, LEVELS, ROWS, COLS), jnp.float32),
         pltpu.VMEM((2, LEVELS, ROWS, COLS), jnp.float32),
         pltpu.VMEM((2, LEVELS, ROWS, COLS), jnp.float32),
         pltpu.VMEM((ROWS, COLS), jnp.int32),
-        pltpu.VMEM((MESSAGE, COLS), jnp.float32),
-        pltpu.VMEM((MESSAGE, COLS), jnp.float32),
-        pltpu.VMEM((ROWS, LANE), jnp.float32),
-        pltpu.VMEM((ROWS, LANE), jnp.float32),
+        pltpu.VMEM((2, MESSAGE, COLS), jnp.float32),
+        pltpu.VMEM((2, ROWS, LANE), jnp.float32),
         block,
         block,
-        block,
-        block,
-        pltpu.VMEM((ROWS, LANE), jnp.float32),
+        narrow,
+        narrow,
+        pltpu.VMEM((2, ROWS + 8, COLS), jnp.float32),
         pltpu.SemaphoreType.DMA((3, LEVELS)),
-        pltpu.SemaphoreType.DMA((7,)),
+        pltpu.SemaphoreType.DMA((8,)),
     ]
     aliases = {}
     if first == 0:
         thickness, depth, tops = extra
-        ins = [SMEM] + ins + [ANY, ANY]
+        ins = [HBM] + ins + [HBM, ANY]
         operands = [thickness] + operands + [depth, tops]
         out_specs.append(VMEM)
         out_shape.append(f32(8, 2 * EXT + 8, COLS))
@@ -359,10 +363,11 @@
             block,
             pltpu.VMEM((8, COLS), jnp.float32),
             pltpu.VMEM((2, ROWS + 8, COLS), jnp.float32),
+            pltpu.SMEM((LEVELS,), jnp.float32),
         ]
     else:
         aliases = {len(operands): 0}
-        ins = ins + [ANY]
+        ins = ins + [HBM]
         operands = operands + [extra]
     return pl.pallas_call(
         functools.partial(advect_kernel, first),
@@ -371,7 +376,7 @@
         out_shape=out_shape,
         scratch_shapes=scratch,
         input_output_aliases=aliases,
-        compiler_params=pltpu.CompilerParams(vmem_limit_bytes=16 * 2**20),
+        compiler_params=pltpu.CompilerParams(vmem_limit_bytes=58 * 2**20),
         cost_estimate=pl.CostEstimate(flops=24_000_000, bytes_accessed=9_400_000, transcendentals=0),
         name="advect_forcing" if first == 0 else "advect_rest",
     )(*operands)
@@ -390,22 +395,27 @@
     return x
 
 
-def solve_kernel(got_ref, out_ref, h_ref, f_ref, weight):
+def solve_kernel(got, out_ref, h_ref, f_ref, misc, weight, sems):
+    copies = []
     for j in range(8):
         cols = pl.ds(j * COLS, COLS)
-        f_ref[:, cols] = got_ref[j, 0:EXT, :]
-        h_ref[:, cols] = got_ref[j, EXT : 2 * EXT, :]
+        copies.append(pltpu.make_async_copy(got.at[j, 0:EXT, :], f_ref.at[:, cols], sems.at[0, j]))
+        copies.append(pltpu.make_async_copy(got.at[j, EXT : 2 * EXT, :], h_ref.at[:, cols], sems.at[1, j]))
+        copies.append(pltpu.make_async_copy(got.at[j, 2 * EXT :, :], misc.at[j], sems.at[2, j]))
+    for copy in copies:
+        copy.start()
+    for copy in copies:
+        copy.wait()
     lane, tile = lanes((8, LANE)), sublanes((8, LANE))
-    edge_rows = pl.ds(2 * EXT, 8)
     for j in range(7):
-        pairs = got_ref[j, edge_rows, :LANE] * pltpu.roll(got_ref[j + 1, edge_rows, :LANE], LANE - 16, 1)
+        pairs = misc[j, :, :LANE] * pltpu.roll(misc[j + 1, :, :LANE], LANE - 16, 1)
         flux = jnp.sum(jnp.where(lane <= LEVELS, pairs, 0.0), axis=1, keepdims=True)
         for rows, there in ((pl.ds(0, 8), tile < 4), (pl.ds(16, 8), tile >= 4)):
             last = pl.ds((j + 1) * COLS - LANE, LANE)
             after = pl.ds((j + 1) * COLS, LANE)
             f_ref[rows, last] = f_ref[rows, last] - jnp.where(there & (lane == LANE - 1), flux, 0.0)
             f_ref[rows, after] = f_ref[rows, after] + jnp.where(there & (lane == 0), flux, 0.0)
-    most = jnp.max(got_ref[:, 2 * EXT : 2 * EXT + 8, LANE:], axis=0)[0:1, 0:1]
+    most = jnp.max(misc[:, :, LANE:], axis=0)[0:1, 0:1]
     lam_max = 0.5 + 10.0 * most
     theta = (lam_max + 0.5) / 2.0
     delta = (lam_max - 0.5) / 2.0
@@ -435,13 +445,15 @@
 def solve(got):
     return pl.pallas_call(
         solve_kernel,
-        in_specs=[VMEM],
+        in_specs=[ANY],
         out_specs=VMEM,
         out_shape=f32(16, WIDE),
         scratch_shapes=[
             pltpu.VMEM((EXT, WIDE), jnp.float32),
             pltpu.VMEM((EXT, WIDE), jnp.float32),
+            pltpu.VMEM((8, 8, COLS), jnp.float32),
             pltpu.VMEM((8, EXT, WIDE), jnp.float32),
+            pltpu.SemaphoreType.DMA((3, 8)),
         ],
         compiler_params=pltpu.CompilerParams(vmem_limit_bytes=12 * 2**20),
         cost_estimate=pl.CostEstimate(flops=6_000_000, bytes_accessed=600_000, transcendentals=0),
@@ -449,15 +461,17 @@
     )(got)
 
 
-def send(x, axis, step):
+def exchange(x, axis, odd):
     count = lax.axis_size(axis)
-    pairs = [(i, i + step) for i in range(count) if 0 <= i + step < count]
+    pairs = []
+    for i in range(odd, count - 1, 2):
+        pairs += [(i, i + 1), (i + 1, i)]
     return lax.ppermute(x, axis, pairs)
 
 
 def shards(tracers, velocity, ocean, thickness, depth):
-    row_hi, row_lo, col_hi, col_lo, top = pack(thickness, tracers, velocity, ocean, depth)
-    halos = (send(row_hi, "bx", 1), send(row_lo, "bx", -1), send(col_hi, "by", 1), send(col_lo, "by", -1))
+    row_even, row_odd, col_even, col_odd, top = pack(thickness, tracers, velocity, ocean, depth)
+    halos = (exchange(row_even, "bx", 0), exchange(row_odd, "bx", 1), exchange(col_even, "by", 0), exchange(col_odd, "by", 1))
     tops = lax.all_to_all(top, "bx", split_axis=0, concat_axis=0, tiled=True)
     part, parcels = advect(0, tracers, velocity, ocean, *halos, (thickness, depth, tops))
     got = lax.all_to_all(parcels, "by", split_axis=0, concat_axis=0, tiled=True)

time: 66.1 us -> 65 us (0.983)
  Pallas kernels: 20.2 us -> 34.4 us
  local copies, waits for them, and re-layouts: 11.5 us -> 1.25 us
  starting transfers between devices: 18.8 us -> 13.1 us
  blocking collectives: 14.1 us -> 15.3 us
    pallas_call x2, Pallas kernels: 12.7 us -> 26.7 us  [advect(): pl.pallas_call(functools.partial(advect_kernel, first), in_specs=ins, out...]
    unnamed x26 -> x8, local copies, waits for them, and re-layouts: 11.5 us -> 1.25 us
    ppermute x4, starting transfers between devices: 11.9 us -> 7.34 us  [exchange(): return lax.ppermute(x, axis, pairs)]
    all_to_all x1, starting transfers between devices: 6.95 us -> 5.72 us  [shards(): got = lax.all_to_all(parcels, 'by', split_axis=0, concat_axis=0, tiled=True)]
    all_to_all x1, blocking collectives: 14.1 us -> 15.3 us  [shards(): tops = lax.all_to_all(top, 'bx', split_axis=0, concat_axis=0, tiled=True)]
  transfers between devices with their start and end apart: 5 -> 5, of which waited for: 0 -> 0; matrix products, arithmetic and copies ran while one was open for 0% -> 0% of each run, Pallas kernels for 9% -> 20%
where the time goes in v3:
time: 65 us; the launch traced here: 64.8 us
  Pallas kernels  34.4 us (53%)
  blocking collectives  15.3 us (24%)
  starting transfers between devices  13.1 us (20%)
  local copies, waits for them, and re-layouts  1.25 us (2%)
  between operations  0.72 us (1%)
    pallas_call x2, Pallas kernels, advect(): pl.pallas_call(functools.partial(advect_kernel, first), in_specs=ins, out...  26.7 us
    all_to_all x1, blocking collectives, shards(): tops = lax.all_to_all(top, 'bx', split_axis=0, concat_axis=0, tiled=True)  15.3 us
    ppermute x4, starting transfers between devices, exchange(): return lax.ppermute(x, axis, pairs)  7.34 us
    all_to_all x1, starting transfers between devices, shards(): got = lax.all_to_all(parcels, 'by', split_axis=0, concat_axis=0, tiled=True)  5.72 us
    pallas_call x1, Pallas kernels, pack(): pl.pallas_call(pack_kernel, in_specs=[HBM] * 5, out_specs=[VMEM] * 5, out...  5.03 us
    pallas_call x1, Pallas kernels, solve(): pl.pallas_call(solve_kernel, in_specs=[ANY], out_specs=VMEM, out_shape=f3...  2.64 us
  transfers between devices with their start and end apart: 5, of which 0 were waited for; matrix products, arithmetic and copies ran while one was open for 0% of the time, Pallas kernels for 20%

profile of v3, /device:TPU:1, one launch (start us, length us, event | category | flops | bytes accessed | tf_op | source)
XLA Modules:
  0.0 64.8 jit_solution(17607586030324770006)
XLA Ops:
  0.6 5.0 %pack_edges.1 = (f32[80,256]{1,0:T(8,128)}, f32[80,256]{1,0:T(8,128)}, f32[128,128]{1,0:T(8,128)}, f32[128,128]{1,0:T(8,128)}, f32[16,8,128]{2,1,0:T(8,128)}) custom-call(f32[12]{0:T(128)} %refs_0_.2, f32[4,12,128,256]{3,2,1,0:T(8,128)} %refs_0_.3, f32[2,12,128,256]{3,2,1,0:T(8,128)} %refs_1_.3, s32[128,256]{1,0:T(8,128)} %refs_2_.3, f32[128,256]{1,0:T(8,128)} %refs_8_.1), custom_call_target="tpu_custom_call" | custom-call | flops 4000000 | bytes 7400000 | tf_op jit(solution)/shard_map/pack_edges/pallas_call | solution.py:166
  5.7 2.2 %collective-permute-start = (f32[80,256]{1,0:T(8,128)}, f32[80,256]{1,0:T(8,128)S(1)}, u32[]{:S(2)}, u32[]{:S(2)}) collective-permute-start(f32[80,256]{1,0:T(8,128)} %get-tuple-element.9), channel_id=1, source_target_pairs={{0,8},{8,0},{16,24},{24,16},{32,40},{40,32},{48,56},{56,48},{64,72... | collective-permute-start | bytes 245768 | tf_op jit(solution)/shard_map/ppermute | solution.py:469
  7.9 0.7 %collective-permute-start.1 = (f32[80,256]{1,0:T(8,128)}, f32[80,256]{1,0:T(8,128)S(1)}, u32[]{:S(2)}, u32[]{:S(2)}) collective-permute-start(f32[80,256]{1,0:T(8,128)} %get-tuple-element.10), channel_id=1, source_target_pairs={{8,16},{16,8},{24,32},{32,24},{40,48},{48,40},{56,64},{64,56},{72,... | collective-permute-start | bytes 245768 | tf_op jit(solution)/shard_map/ppermute | solution.py:469
  8.5 1.0 %collective-permute-start.2 = (f32[128,128]{1,0:T(8,128)}, f32[128,128]{1,0:T(8,128)S(1)}, u32[]{:S(2)}, u32[]{:S(2)}) collective-permute-start(f32[128,128]{1,0:T(8,128)} %get-tuple-element.11), channel_id=1, source_target_pairs={{0,1},{1,0},{2,3},{3,2},{4,5},{5,4},{6,7},{7,6},{8,9},{9,8},{10,11... | collective-permute-start | bytes 196616 | tf_op jit(solution)/shard_map/ppermute | solution.py:469
  9.6 3.4 %collective-permute-start.3 = (f32[128,128]{1,0:T(8,128)}, f32[128,128]{1,0:T(8,128)S(1)}, u32[]{:S(2)}, u32[]{:S(2)}) collective-permute-start(f32[128,128]{1,0:T(8,128)} %get-tuple-element.12), channel_id=1, source_target_pairs={{1,2},{2,1},{3,4},{4,3},{5,6},{6,5},{9,10},{10,9},{11,12},{12,11},... | collective-permute-start | bytes 196616 | tf_op jit(solution)/shard_map/ppermute | solution.py:469
  13.0 15.3 %all_to_all.10.refs_9_ = f32[16,8,128]{2,1,0:T(8,128)} all-to-all(f32[16,8,128]{2,1,0:T(8,128)} %get-tuple-element.13), channel_id=1, replica_groups=mesh['bx'=16,'by'=8] {'bx'}, dimensions={0} | all-to-all | bytes 131072 | tf_op jit(solution)/shard_map/all_to_all | solution.py:475
  28.3 0.0 collective-permute-done.2.refs_6_.refs_5_
  28.3 0.0 copy-start.2
  28.3 0.0 collective-permute-done.3.refs_7_.refs_6_
  28.3 0.0 copy-start.3
  28.3 0.0 collective-permute-done.refs_4_.refs_3_
  28.4 0.0 copy-start
  28.4 0.0 collective-permute-done.1.refs_5_.refs_4_
  28.4 0.6 copy-done.2
  29.0 0.0 copy-done.3
  29.0 0.0 copy-done
  29.0 0.0 copy-start.1
  29.0 0.6 copy-done.1
  29.6 13.8 %advect_forcing.1 = (f32[4,12,128,256]{3,2,1,0:T(8,128)}, f32[8,56,256]{2,1,0:T(8,128)}) custom-call(f32[12]{0:T(128)} %refs_0_.2, f32[4,12,128,256]{3,2,1,0:T(8,128)} %refs_0_.3, f32[2,12,128,256]{3,2,1,0:T(8,128)} %refs_1_.3, s32[128,256]{1,0:T(8,128)} %refs_2_.3, f32[80,256]{1,0:T(8,128)} %copy-done, f32[80,256]{1,0:T(8,128)} %copy-done.1, ...), custom_call_target="tpu_custom_call" | custom-call | flops 24000000 | bytes 9400000 | tf_op jit(solution)/shard_map/advect_forcing/pallas_call | solution.py:372
  43.4 5.7 %all-to-all-start.1 = ((f32[8,56,256]{2,1,0:T(8,128)}), f32[8,56,256]{2,1,0:T(8,128)S(1)}, u32[]{:S(2)}, u32[]{:S(2)}) async-start(f32[8,56,256]{2,1,0:T(8,128)} %get-tuple-element.15), calls=%async_computation.1 | async-start | bytes 917504 | tf_op jit(solution)/shard_map/all_to_all | solution.py:477
  49.1 13.0 %advect_rest.1 = f32[4,12,128,256]{3,2,1,0:T(8,128)} custom-call(f32[4,12,128,256]{3,2,1,0:T(8,128)} %refs_0_.3, f32[2,12,128,256]{3,2,1,0:T(8,128)} %refs_1_.3, s32[128,256]{1,0:T(8,128)} %refs_2_.3, f32[80,256]{1,0:T(8,128)} %copy-done, f32[80,256]{1,0:T(8,128)} %copy-done.1, f32[128,128]{1,0:T(8,128)} %copy-done.2, ...), custom_call_target="tpu_custom_call", output_to_operand_aliasing={{}: (7, {})} | custom-call | flops 24000000 | bytes 9400000 | tf_op jit(solution)/shard_map/advect_rest/pallas_call | solution.py:372
  62.1 0.0 all-to-all-done.1.got
  62.1 2.6 %chebyshev.1 = f32[16,2048]{1,0:T(8,128)} custom-call(f32[8,56,256]{2,1,0:T(8,128)S(1)} %all-to-all-done.1.got), custom_call_target="tpu_custom_call" | custom-call | flops 6000000 | bytes 600000 | tf_op jit(solution)/shard_map/chebyshev/pallas_call | solution.py:446
Async XLA Ops:
  5.7 22.7 %collective-permute-start = (f32[80,256]{1,0:T(8,128)}, f32[80,256]{1,0:T(8,128)S(1)}, u32[]{:S(2)}, u32[]{:S(2)}) collective-permute-start(f32[80,256]{1,0:T(8,128)} %get-tuple-element.9), channel_id=1, source_target_pairs={{0,8},{8,0},{16,24},{24,16},{32,40},{40,32},{48,56},{56,48},{64,72... | collective-permute-start | bytes 245768 | tf_op jit(solution)/shard_map/ppermute | solution.py:469
  7.9 20.5 %collective-permute-start.1 = (f32[80,256]{1,0:T(8,128)}, f32[80,256]{1,0:T(8,128)S(1)}, u32[]{:S(2)}, u32[]{:S(2)}) collective-permute-start(f32[80,256]{1,0:T(8,128)} %get-tuple-element.10), channel_id=1, source_target_pairs={{8,16},{16,8},{24,32},{32,24},{40,48},{48,40},{56,64},{64,56},{72,... | collective-permute-start | bytes 245768 | tf_op jit(solution)/shard_map/ppermute | solution.py:469
  8.5 19.8 %collective-permute-start.2 = (f32[128,128]{1,0:T(8,128)}, f32[128,128]{1,0:T(8,128)S(1)}, u32[]{:S(2)}, u32[]{:S(2)}) collective-permute-start(f32[128,128]{1,0:T(8,128)} %get-tuple-element.11), channel_id=1, source_target_pairs={{0,1},{1,0},{2,3},{3,2},{4,5},{5,4},{6,7},{7,6},{8,9},{9,8},{10,11... | collective-permute-start | bytes 196616 | tf_op jit(solution)/shard_map/ppermute | solution.py:469
  9.6 18.8 %collective-permute-start.3 = (f32[128,128]{1,0:T(8,128)}, f32[128,128]{1,0:T(8,128)S(1)}, u32[]{:S(2)}, u32[]{:S(2)}) collective-permute-start(f32[128,128]{1,0:T(8,128)} %get-tuple-element.12), channel_id=1, source_target_pairs={{1,2},{2,1},{3,4},{4,3},{5,6},{6,5},{9,10},{10,9},{11,12},{12,11},... | collective-permute-start | bytes 196616 | tf_op jit(solution)/shard_map/ppermute | solution.py:469
  28.3 0.6 copy-start.2
  28.3 0.7 %copy-start.3 = (f32[128,128]{1,0:T(8,128)}, f32[128,128]{1,0:T(8,128)S(1)}, u32[]{:S(2)}) copy-start(f32[128,128]{1,0:T(8,128)S(1)} %collective-permute-done.3.refs_7_.refs_6_) | copy-start | bytes 196612
  28.4 0.7 %copy-start = (f32[80,256]{1,0:T(8,128)}, f32[80,256]{1,0:T(8,128)S(1)}, u32[]{:S(2)}) copy-start(f32[80,256]{1,0:T(8,128)S(1)} %collective-permute-done.refs_4_.refs_3_) | copy-start | bytes 245764
  29.0 0.6 copy-start.1
  43.4 18.7 %all-to-all-start.1 = ((f32[8,56,256]{2,1,0:T(8,128)}), f32[8,56,256]{2,1,0:T(8,128)S(1)}, u32[]{:S(2)}, u32[]{:S(2)}) async-start(f32[8,56,256]{2,1,0:T(8,128)} %get-tuple-element.15), calls=%async_computation.1 | async-start | bytes 917504 | tf_op jit(solution)/shard_map/all_to_all | solution.py:477

commit v4 on v3

--- a/solution.py
+++ b/solution.py
@@ -212,12 +212,12 @@
 
 def advect_kernel(first, *refs):
     if first == 0:
-        (thick_hbm, t_hbm, v_hbm, ocean_hbm, row_even, row_odd, col_even, col_odd, depth_hbm, tops_hbm, out_hbm, send_ref,
-         t_ref, v_ref, out_ref, ocean_ref, rows_in, cols_in, w_x, w_y, before_y, edges, flux_x, sems, small_sems,
-         depth_ref, tops, total, flux, ext, thick) = refs
+        (thick_hbm, t_hbm, v_hbm, ocean_hbm, row_even, row_odd, col_even, col_odd, depth_hbm, out_hbm, send_ref,
+         t_ref, v_ref, out_ref, ocean_ref, rows_in, cols_in, w_x, w_y, before_y, edges, sems, small_sems,
+         depth_ref, total, flux, ext, thick) = refs
     else:
         (t_hbm, v_hbm, ocean_hbm, row_even, row_odd, col_even, col_odd, _, out_hbm,
-         t_ref, v_ref, out_ref, ocean_ref, rows_in, cols_in, w_x, w_y, before_y, edges, flux_x, sems, small_sems) = refs
+         t_ref, v_ref, out_ref, ocean_ref, rows_in, cols_in, w_x, w_y, before_y, edges, sems, small_sems) = refs
     odd_x, odd_y = lax.axis_index("bx") % 2, lax.axis_index("by") % 2
     row_lo, row_hi = rows_in.at[0], rows_in.at[1]
     small = [
@@ -228,7 +228,7 @@
         (col_odd, cols_in.at[odd_y]),
     ]
     if first == 0:
-        small += [(depth_hbm, depth_ref), (tops_hbm, tops), (thick_hbm, thick)]
+        small += [(depth_hbm, depth_ref), (thick_hbm, thick)]
     small = [pltpu.make_async_copy(a, b, small_sems.at[i]) for i, (a, b) in enumerate(small)]
 
     def tracers_in(k):
@@ -252,7 +252,9 @@
     for r in range(TILES):
         rows = pl.ds(8 * r, 8)
         edge = jnp.where(even, cols_in[0, rows, :], cols_in[1, rows, :])
-        edges[rows, :] = edge
+        for k in range(LEVELS):
+            for i, slot in enumerate((first * LEVELS + k, (first + 1) * LEVELS + k, SPEED + k)):
+                edges[i, k, rows, :] = pltpu.roll(edge, (LANE - 2 * slot) % LANE, 1)
         here = load_wet(8 * r)
         wet_edge = pltpu.roll(edge, LANE - 2 * WET, 1)
         w_x[rows, :] = here * above(load_wet, row_hi[WET : WET + 1, :], r)
@@ -268,34 +270,35 @@
         tracers_in(k).wait()
         velocity_in(k).wait()
         u_before = row_lo[pl.ds(SPEED + k, 1), :] * w_before
-        for t in range(2):
-            flux_x[t, 7:8, :] = upwind(u_before, row_lo[pl.ds((first + t) * LEVELS + k, 1), :], t_ref[t, k, 0:1, :])
+        into_x = [upwind(u_before, row_lo[pl.ds((first + t) * LEVELS + k, 1), :], t_ref[t, k, 0:1, :]) for t in range(2)]
+        carry, out_x = list(into_x), [None, None]
         for r in range(TILES):
             rows = pl.ds(8 * r, 8)
-            edge_tile = edges[rows, :]
             u = v_ref[0, k, rows, :] * w_x[rows, :]
             v = v_ref[1, k, rows, :] * w_y[rows, :]
-            v_before = pltpu.roll(edge_tile, LANE - 2 * (SPEED + k), 1) * before_y[rows, :]
+            v_before = edges[2, k, rows, :] * before_y[rows, :]
             new = []
             for t in range(2):
                 load = lambda at: t_ref[t, k, at : at + 8, :]
                 slot = (first + t) * LEVELS + k
                 c = load(8 * r)
-                c_edge = pltpu.roll(edge_tile, LANE - 2 * slot, 1)
+                c_edge = edges[t, k, rows, :]
                 here_x = upwind(u, c, above(load, row_hi[pl.ds(slot, 1), :], r))
-                flux_x[t, 8 * r + 8 : 8 * r + 16, :] = here_x
+                turned = pltpu.roll(here_x, 1, 0)
+                past_x = jnp.where(sublanes((8, COLS)) == 0, carry[t], turned)
+                carry[t] = turned
+                if r == TILES - 1:
+                    out_x[t] = here_x[7:8, :]
                 here_y = upwind(v, c, ahead_y(c, c_edge))
                 past_y = behind_y(here_y, upwind(v_before, c_edge, c[:, :LANE]))
-                past_x = flux_x[t, 8 * r + 7 : 8 * r + 15, :]
                 value = (c - (here_x - past_x)) - (here_y - past_y)
                 out_ref[t, k, rows, :] = value
                 new.append(value)
             if first == 0:
                 total[rows, :] = total[rows, :] + ((0.2 * thick[k]) * new[0] - (0.8 * thick[k]) * new[1])
         if first == 0:
-            mixed = lambda row: thick[k] * (0.2 * flux_x[0, row : row + 1, :] - 0.8 * flux_x[1, row : row + 1, :])
-            flux[0:1, :] = flux[0:1, :] + mixed(7)
-            flux[1:2, :] = flux[1:2, :] + mixed(ROWS + 7)
+            flux[0:1, :] = flux[0:1, :] + thick[k] * (0.2 * into_x[0] - 0.8 * into_x[1])
+            flux[1:2, :] = flux[1:2, :] + thick[k] * (0.2 * out_x[0] - 0.8 * out_x[1])
         tracers_out(k).start()
         return 0
 
@@ -312,7 +315,6 @@
             here = load_wet(8 * r)
             ext[0, 8 * r + 4 : 8 * r + 12, :] = total[rows, :] * here
             ext[1, 8 * r + 4 : 8 * r + 12, :] = coefficient(depth_ref[rows, :], here)
-        most = jnp.max(tops[...], axis=0)
         tile = sublanes((8, LANE))
         for j in range(8):
             send_ref[j, 0:EXT, :] = ext[0, 16 * j : 16 * j + EXT, :]
@@ -323,7 +325,7 @@
             if j == 7:
                 edge = jnp.where((tile >= 4) & (tile <= 6), pltpu.roll(row_hi[EDGE:MESSAGE, :LANE], 4, 0), 0.0)
             send_ref[j, 2 * EXT : 2 * EXT + 8, :LANE] = edge
-            send_ref[j, 2 * EXT : 2 * EXT + 8, LANE:] = most
+            send_ref[j, 2 * EXT : 2 * EXT + 8, LANE:] = jnp.zeros((8, LANE), jnp.float32)
     for k in range(LEVELS):
         tracers_out(k).wait()
 
@@ -345,21 +347,19 @@
         block,
         block,
         narrow,
-        narrow,
-        pltpu.VMEM((2, ROWS + 8, COLS), jnp.float32),
+        pltpu.VMEM((3, LEVELS, ROWS, LANE), jnp.float32),
         pltpu.SemaphoreType.DMA((3, LEVELS)),
         pltpu.SemaphoreType.DMA((8,)),
     ]
     aliases = {}
     if first == 0:
-        thickness, depth, tops = extra
-        ins = [HBM] + ins + [HBM, ANY]
-        operands = [thickness] + operands + [depth, tops]
+        thickness, depth = extra
+        ins = [HBM] + ins + [HBM]
+        operands = [thickness] + operands + [depth]
         out_specs.append(VMEM)
         out_shape.append(f32(8, 2 * EXT + 8, COLS))
         scratch += [
             block,
-            pltpu.VMEM((16, 8, LANE), jnp.float32),
             block,
             pltpu.VMEM((8, COLS), jnp.float32),
             pltpu.VMEM((2, ROWS + 8, COLS), jnp.float32),
@@ -380,6 +380,29 @@
         cost_estimate=pl.CostEstimate(flops=24_000_000, bytes_accessed=9_400_000, transcendentals=0),
         name="advect_forcing" if first == 0 else "advect_rest",
     )(*operands)
+
+
+def insert_kernel(_, tops, out_hbm, most, sem):
+    top = jnp.max(tops[...], axis=0)
+    for j in range(8):
+        most[j] = top
+    copy = pltpu.make_async_copy(most, out_hbm.at[:, 2 * EXT :, LANE:], sem.at[0])
+    copy.start()
+    copy.wait()
+
+
+def insert(parcels, tops):
+    return pl.pallas_call(
+        insert_kernel,
+        in_specs=[HBM, VMEM],
+        out_specs=HBM,
+        out_shape=f32(8, 2 * EXT + 8, COLS),
+        scratch_shapes=[pltpu.VMEM((8, 8, LANE), jnp.float32), pltpu.SemaphoreType.DMA((1,))],
+        input_output_aliases={0: 0},
+        compiler_params=pltpu.CompilerParams(vmem_limit_bytes=58 * 2**20),
+        cost_estimate=pl.CostEstimate(flops=1000, bytes_accessed=100_000, transcendentals=0),
+        name="insert_maximum",
+    )(parcels, tops)
 
 
 NEAR = ((1, 0, 0.5), (-1, 0, 0.5), (0, 1, 0.5), (0, -1, 0.5), (1, 1, 0.125), (1, -1, 0.125), (-1, 1, 0.125), (-1, -1, 0.125))
@@ -473,8 +496,8 @@
     row_even, row_odd, col_even, col_odd, top = pack(thickness, tracers, velocity, ocean, depth)
     halos = (exchange(row_even, "bx", 0), exchange(row_odd, "bx", 1), exchange(col_even, "by", 0), exchange(col_odd, "by", 1))
     tops = lax.all_to_all(top, "bx", split_axis=0, concat_axis=0, tiled=True)
-    part, parcels = advect(0, tracers, velocity, ocean, *halos, (thickness, depth, tops))
-    got = lax.all_to_all(parcels, "by", split_axis=0, concat_axis=0, tiled=True)
+    part, parcels = advect(0, tracers, velocity, ocean, *halos, (thickness, depth))
+    got = lax.all_to_all(insert(parcels, tops), "by", split_axis=0, concat_axis=0, tiled=True)
     new_tracers = advect(2, tracers, velocity, ocean, *halos, part)[0]
     return new_tracers, solve(got)
 

time: 65 us -> 50.6 us (0.78)
  blocking collectives: 15.3 us -> 0 us
  Pallas kernels: 34.4 us -> 25.7 us
  starting transfers between devices: 13.1 us -> 21 us
  waiting for transfers between devices: 0.01 us -> 0.93 us
    all_to_all x1 -> x0, blocking collectives: 15.3 us -> none  [shards(): tops = lax.all_to_all(top, 'bx', split_axis=0, concat_axis=0, tiled=True)]
    pallas_call x2, Pallas kernels: 26.7 us -> 16.6 us  [advect(): pl.pallas_call(functools.partial(advect_kernel, first), in_specs=ins, out...]
    all_to_all x1 -> x2, starting transfers between devices: 5.72 us -> 13.7 us  [the longest x1 8.68 us: shards(): tops = lax.all_to_all(top, 'bx', split_axis=0, concat_axis=0, tiled=True)]
    pallas_call x0 -> x1, Pallas kernels: none -> 1.47 us  [insert(): pl.pallas_call(insert_kernel, in_specs=[HBM, VMEM], out_specs=HBM, out_sh...]
    all_to_all x1 -> x2, waiting for transfers between devices: 0.01 us -> 0.92 us  [the longest x1 0.92 us: shards(): lax.all_to_all(insert(parcels, tops), 'by', split_axis=0, concat_axis=0,...]
    unnamed x8 -> x10, local copies, waits for them, and re-layouts: 1.25 us -> 1.86 us
  transfers between devices with their start and end apart: 5 -> 6, of which waited for: 0 -> 1; matrix products, arithmetic and copies ran while one was open for 0% -> 0% of each run, Pallas kernels for 20% -> 33%
where the time goes in v4:
time: 50.6 us; the launch traced here: 50.2 us
  Pallas kernels  25.7 us (51%)
  starting transfers between devices  21 us (42%)
  local copies, waits for them, and re-layouts  1.86 us (4%)
  waiting for transfers between devices  0.93 us (2%)
  between operations  0.76 us (2%)
    pallas_call x2, Pallas kernels, advect(): pl.pallas_call(functools.partial(advect_kernel, first), in_specs=ins, out...  16.6 us
    all_to_all x1, starting transfers between devices, shards(): tops = lax.all_to_all(top, 'bx', split_axis=0, concat_axis=0, tiled=True)  8.68 us
    ppermute x4, starting transfers between devices, exchange(): return lax.ppermute(x, axis, pairs)  7.34 us
    pallas_call x1, Pallas kernels, pack(): pl.pallas_call(pack_kernel, in_specs=[HBM] * 5, out_specs=[VMEM] * 5, out...  5.03 us
    all_to_all x1, starting transfers between devices, shards(): lax.all_to_all(insert(parcels, tops), 'by', split_axis=0, concat_axis=0,...  4.98 us
    pallas_call x1, Pallas kernels, solve(): pl.pallas_call(solve_kernel, in_specs=[ANY], out_specs=VMEM, out_shape=f3...  2.62 us
    unnamed x10, local copies, waits for them, and re-layouts  1.86 us
    pallas_call x1, Pallas kernels, insert(): pl.pallas_call(insert_kernel, in_specs=[HBM, VMEM], out_specs=HBM, out_sh...  1.47 us
  transfers between devices with their start and end apart: 6, of which 1 were waited for; matrix products, arithmetic and copies ran while one was open for 0% of the time, Pallas kernels for 33%

profile of v4, /device:TPU:1, one launch (start us, length us, event | category | flops | bytes accessed | tf_op | source)
XLA Modules:
  0.0 50.2 jit_solution(6719754557387285063)
XLA Ops:
  0.6 5.0 %pack_edges.1 = (f32[80,256]{1,0:T(8,128)}, f32[80,256]{1,0:T(8,128)}, f32[128,128]{1,0:T(8,128)}, f32[128,128]{1,0:T(8,128)}, f32[16,8,128]{2,1,0:T(8,128)}) custom-call(f32[12]{0:T(128)} %refs_0_.2, f32[4,12,128,256]{3,2,1,0:T(8,128)} %refs_0_.3, f32[2,12,128,256]{3,2,1,0:T(8,128)} %refs_1_.3, s32[128,256]{1,0:T(8,128)} %refs_2_.3, f32[128,256]{1,0:T(8,128)} %refs_8_.1), custom_call_target="tpu_custom_call" | custom-call | flops 4000000 | bytes 7400000 | tf_op jit(solution)/shard_map/pack_edges/pallas_call | solution.py:166
  5.7 2.2 %collective-permute-start = (f32[80,256]{1,0:T(8,128)}, f32[80,256]{1,0:T(8,128)S(1)}, u32[]{:S(2)}, u32[]{:S(2)}) collective-permute-start(f32[80,256]{1,0:T(8,128)} %get-tuple-element.9), channel_id=1, source_target_pairs={{0,8},{8,0},{16,24},{24,16},{32,40},{40,32},{48,56},{56,48},{64,72... | collective-permute-start | bytes 245768 | tf_op jit(solution)/shard_map/ppermute | solution.py:492
  7.9 0.7 %collective-permute-start.1 = (f32[80,256]{1,0:T(8,128)}, f32[80,256]{1,0:T(8,128)S(1)}, u32[]{:S(2)}, u32[]{:S(2)}) collective-permute-start(f32[80,256]{1,0:T(8,128)} %get-tuple-element.10), channel_id=1, source_target_pairs={{8,16},{16,8},{24,32},{32,24},{40,48},{48,40},{56,64},{64,56},{72,... | collective-permute-start | bytes 245768 | tf_op jit(solution)/shard_map/ppermute | solution.py:492
  8.5 1.0 %collective-permute-start.2 = (f32[128,128]{1,0:T(8,128)}, f32[128,128]{1,0:T(8,128)S(1)}, u32[]{:S(2)}, u32[]{:S(2)}) collective-permute-start(f32[128,128]{1,0:T(8,128)} %get-tuple-element.11), channel_id=1, source_target_pairs={{0,1},{1,0},{2,3},{3,2},{4,5},{5,4},{6,7},{7,6},{8,9},{9,8},{10,11... | collective-permute-start | bytes 196616 | tf_op jit(solution)/shard_map/ppermute | solution.py:492
  9.6 3.4 %collective-permute-start.3 = (f32[128,128]{1,0:T(8,128)}, f32[128,128]{1,0:T(8,128)S(1)}, u32[]{:S(2)}, u32[]{:S(2)}) collective-permute-start(f32[128,128]{1,0:T(8,128)} %get-tuple-element.12), channel_id=1, source_target_pairs={{1,2},{2,1},{3,4},{4,3},{5,6},{6,5},{9,10},{10,9},{11,12},{12,11},... | collective-permute-start | bytes 196616 | tf_op jit(solution)/shard_map/ppermute | solution.py:492
  13.0 8.7 %all-to-all-start = ((f32[16,8,128]{2,1,0:T(8,128)}), f32[16,8,128]{2,1,0:T(8,128)S(1)}, u32[]{:S(2)}, u32[]{:S(2)}) async-start(f32[16,8,128]{2,1,0:T(8,128)} %get-tuple-element.15), calls=%async_computation | async-start | bytes 131072 | tf_op jit(solution)/shard_map/all_to_all | solution.py:498
  21.7 0.0 collective-permute-done.2.refs_6_.refs_5_
  21.7 0.0 copy-start.2
  21.7 0.0 collective-permute-done.3.refs_7_.refs_6_
  21.7 0.0 copy-start.3
  21.8 0.0 collective-permute-done.refs_4_.refs_3_
  21.8 0.0 copy-start
  21.8 0.0 collective-permute-done.1.refs_5_.refs_4_
  21.8 0.6 %copy-done.2 = f32[128,128]{1,0:T(8,128)} copy-done((f32[128,128]{1,0:T(8,128)}, f32[128,128]{1,0:T(8,128)S(1)}, u32[]{:S(2)}) %copy-start.2) | copy-done | bytes 65560
  22.3 0.0 copy-done.3
  22.4 0.0 copy-done
  22.4 0.0 copy-start.1
  22.4 0.6 %copy-done.1 = f32[80,256]{1,0:T(8,128)} copy-done((f32[80,256]{1,0:T(8,128)}, f32[80,256]{1,0:T(8,128)S(1)}, u32[]{:S(2)}) %copy-start.1) | copy-done | bytes 81944
  23.0 8.7 %advect_forcing.1 = (f32[4,12,128,256]{3,2,1,0:T(8,128)}, f32[8,56,256]{2,1,0:T(8,128)}) custom-call(f32[12]{0:T(128)} %refs_0_.2, f32[4,12,128,256]{3,2,1,0:T(8,128)} %refs_0_.3, f32[2,12,128,256]{3,2,1,0:T(8,128)} %refs_1_.3, s32[128,256]{1,0:T(8,128)} %refs_2_.3, f32[80,256]{1,0:T(8,128)} %copy-done, f32[80,256]{1,0:T(8,128)} %copy-done.1, ...), custom_call_target="tpu_custom_call" | custom-call | flops 24000000 | bytes 9400000 | tf_op jit(solution)/shard_map/advect_forcing/pallas_call | solution.py:372
  31.7 0.0 all-to-all-done.tops
  31.7 0.0 copy-start.4
  31.8 0.6 %copy-done.4 = f32[16,8,128]{2,1,0:T(8,128)} copy-done((f32[16,8,128]{2,1,0:T(8,128)}, f32[16,8,128]{2,1,0:T(8,128)S(1)}, u32[]{:S(2)}) %copy-start.4) | copy-done | bytes 65560
  32.4 1.5 %insert_maximum.1 = f32[8,56,256]{2,1,0:T(8,128)} custom-call(f32[8,56,256]{2,1,0:T(8,128)} %get-tuple-element.14._, f32[16,8,128]{2,1,0:T(8,128)} %copy-done.4), custom_call_target="tpu_custom_call", output_to_operand_aliasing={{}: (0, {})} | custom-call | flops 1000 | bytes 100000 | tf_op jit(solution)/shard_map/insert_maximum/pallas_call | solution.py:395
  33.8 5.0 %all-to-all-start.1 = ((f32[8,56,256]{2,1,0:T(8,128)}), f32[8,56,256]{2,1,0:T(8,128)S(1)}, u32[]{:S(2)}, u32[]{:S(2)}) async-start(f32[8,56,256]{2,1,0:T(8,128)} %insert_maximum.1), calls=%async_computation.1 | async-start | bytes 917504 | tf_op jit(solution)/shard_map/all_to_all | solution.py:500
  38.8 7.9 %advect_rest.1 = f32[4,12,128,256]{3,2,1,0:T(8,128)} custom-call(f32[4,12,128,256]{3,2,1,0:T(8,128)} %refs_0_.3, f32[2,12,128,256]{3,2,1,0:T(8,128)} %refs_1_.3, s32[128,256]{1,0:T(8,128)} %refs_2_.3, f32[80,256]{1,0:T(8,128)} %copy-done, f32[80,256]{1,0:T(8,128)} %copy-done.1, f32[128,128]{1,0:T(8,128)} %copy-done.2, ...), custom_call_target="tpu_custom_call", output_to_operand_aliasing={{}: (7, {})} | custom-call | flops 24000000 | bytes 9400000 | tf_op jit(solution)/shard_map/advect_rest/pallas_call | solution.py:372
  46.7 0.9 %all-to-all-done.1.got = f32[8,56,256]{2,1,0:T(8,128)S(1)} async-done(((f32[8,56,256]{2,1,0:T(8,128)}), f32[8,56,256]{2,1,0:T(8,128)S(1)}, u32[]{:S(2)}, u32[]{:S(2)}) %all-to-all-start.1) | async-done | bytes 458784 | tf_op jit(solution)/shard_map/all_to_all | solution.py:500
  47.6 2.6 %chebyshev.1 = f32[16,2048]{1,0:T(8,128)} custom-call(f32[8,56,256]{2,1,0:T(8,128)S(1)} %all-to-all-done.1.got), custom_call_target="tpu_custom_call" | custom-call | flops 6000000 | bytes 600000 | tf_op jit(solution)/shard_map/chebyshev/pallas_call | solution.py:469
Async XLA Ops:
  5.7 16.1 %collective-permute-start = (f32[80,256]{1,0:T(8,128)}, f32[80,256]{1,0:T(8,128)S(1)}, u32[]{:S(2)}, u32[]{:S(2)}) collective-permute-start(f32[80,256]{1,0:T(8,128)} %get-tuple-element.9), channel_id=1, source_target_pairs={{0,8},{8,0},{16,24},{24,16},{32,40},{40,32},{48,56},{56,48},{64,72... | collective-permute-start | bytes 245768 | tf_op jit(solution)/shard_map/ppermute | solution.py:492
  7.9 13.9 %collective-permute-start.1 = (f32[80,256]{1,0:T(8,128)}, f32[80,256]{1,0:T(8,128)S(1)}, u32[]{:S(2)}, u32[]{:S(2)}) collective-permute-start(f32[80,256]{1,0:T(8,128)} %get-tuple-element.10), channel_id=1, source_target_pairs={{8,16},{16,8},{24,32},{32,24},{40,48},{48,40},{56,64},{64,56},{72,... | collective-permute-start | bytes 245768 | tf_op jit(solution)/shard_map/ppermute | solution.py:492
  8.5 13.2 %collective-permute-start.2 = (f32[128,128]{1,0:T(8,128)}, f32[128,128]{1,0:T(8,128)S(1)}, u32[]{:S(2)}, u32[]{:S(2)}) collective-permute-start(f32[128,128]{1,0:T(8,128)} %get-tuple-element.11), channel_id=1, source_target_pairs={{0,1},{1,0},{2,3},{3,2},{4,5},{5,4},{6,7},{7,6},{8,9},{9,8},{10,11... | collective-permute-start | bytes 196616 | tf_op jit(solution)/shard_map/ppermute | solution.py:492
  9.6 12.2 %collective-permute-start.3 = (f32[128,128]{1,0:T(8,128)}, f32[128,128]{1,0:T(8,128)S(1)}, u32[]{:S(2)}, u32[]{:S(2)}) collective-permute-start(f32[128,128]{1,0:T(8,128)} %get-tuple-element.12), channel_id=1, source_target_pairs={{1,2},{2,1},{3,4},{4,3},{5,6},{6,5},{9,10},{10,9},{11,12},{12,11},... | collective-permute-start | bytes 196616 | tf_op jit(solution)/shard_map/ppermute | solution.py:492
  13.0 18.7 %all-to-all-start = ((f32[16,8,128]{2,1,0:T(8,128)}), f32[16,8,128]{2,1,0:T(8,128)S(1)}, u32[]{:S(2)}, u32[]{:S(2)}) async-start(f32[16,8,128]{2,1,0:T(8,128)} %get-tuple-element.15), calls=%async_computation | async-start | bytes 131072 | tf_op jit(solution)/shard_map/all_to_all | solution.py:498
  21.7 0.6 %copy-start.2 = (f32[128,128]{1,0:T(8,128)}, f32[128,128]{1,0:T(8,128)S(1)}, u32[]{:S(2)}) copy-start(f32[128,128]{1,0:T(8,128)S(1)} %collective-permute-done.2.refs_6_.refs_5_) | copy-start | bytes 196612
  21.7 0.6 %copy-start.3 = (f32[128,128]{1,0:T(8,128)}, f32[128,128]{1,0:T(8,128)S(1)}, u32[]{:S(2)}) copy-start(f32[128,128]{1,0:T(8,128)S(1)} %collective-permute-done.3.refs_7_.refs_6_) | copy-start | bytes 196612
  21.8 0.6 %copy-start = (f32[80,256]{1,0:T(8,128)}, f32[80,256]{1,0:T(8,128)S(1)}, u32[]{:S(2)}) copy-start(f32[80,256]{1,0:T(8,128)S(1)} %collective-permute-done.refs_4_.refs_3_) | copy-start | bytes 245764
  22.4 0.6 %copy-start.1 = (f32[80,256]{1,0:T(8,128)}, f32[80,256]{1,0:T(8,128)S(1)}, u32[]{:S(2)}) copy-start(f32[80,256]{1,0:T(8,128)S(1)} %collective-permute-done.1.refs_5_.refs_4_) | copy-start | bytes 245764
  31.7 0.6 %copy-start.4 = (f32[16,8,128]{2,1,0:T(8,128)}, f32[16,8,128]{2,1,0:T(8,128)S(1)}, u32[]{:S(2)}) copy-start(f32[16,8,128]{2,1,0:T(8,128)S(1)} %all-to-all-done.tops) | copy-start | bytes 196612
  33.8 13.8 %all-to-all-start.1 = ((f32[8,56,256]{2,1,0:T(8,128)}), f32[8,56,256]{2,1,0:T(8,128)S(1)}, u32[]{:S(2)}, u32[]{:S(2)}) async-start(f32[8,56,256]{2,1,0:T(8,128)} %insert_maximum.1), calls=%async_computation.1 | async-start | bytes 917504 | tf_op jit(solution)/shard_map/all_to_all | solution.py:500

commit v5 on v4

--- a/solution.py
+++ b/solution.py
@@ -17,6 +17,7 @@
 WIDE = 8 * COLS
 EXT = 24
 CHUNK = 32
+TALL = 16
 
 SPEED, WET, PART, COEF, EDGE, MESSAGE = 48, 60, 64, 68, 72, 80
 ANY = pl.BlockSpec(memory_space=pl.ANY)
@@ -189,21 +190,21 @@
 
 
 def ahead_y(x, edge):
-    last = lanes((8, LANE)) == LANE - 1
+    last = lanes((x.shape[0], LANE)) == LANE - 1
     a, b = pltpu.roll(x[:, :LANE], LANE - 1, 1), pltpu.roll(x[:, LANE:], LANE - 1, 1)
     return jnp.concatenate([jnp.where(last, b, a), jnp.where(last, edge, b)], 1)
 
 
 def behind_y(x, edge):
-    first = lanes((8, LANE)) == 0
+    first = lanes((x.shape[0], LANE)) == 0
     a, b = pltpu.roll(x[:, :LANE], 1, 1), pltpu.roll(x[:, LANE:], 1, 1)
     return jnp.concatenate([jnp.where(first, edge, a), jnp.where(first, a, b)], 1)
 
 
-def above(load, edge, r):
-    if r < TILES - 1:
-        return load(8 * r + 1)
-    return jnp.where(sublanes((8, COLS)) == 7, edge, pltpu.roll(load(8 * r), 7, 0))
+def above(load, edge, r, tall=8):
+    if (r + 1) * tall < ROWS:
+        return load(tall * r + 1)
+    return jnp.where(sublanes((tall, COLS)) == tall - 1, edge, pltpu.roll(load(tall * r), tall - 1, 0))
 
 
 def upwind(speed, here, ahead):
@@ -272,23 +273,23 @@
         u_before = row_lo[pl.ds(SPEED + k, 1), :] * w_before
         into_x = [upwind(u_before, row_lo[pl.ds((first + t) * LEVELS + k, 1), :], t_ref[t, k, 0:1, :]) for t in range(2)]
         carry, out_x = list(into_x), [None, None]
-        for r in range(TILES):
-            rows = pl.ds(8 * r, 8)
+        for r in range(ROWS // TALL):
+            rows = pl.ds(TALL * r, TALL)
             u = v_ref[0, k, rows, :] * w_x[rows, :]
             v = v_ref[1, k, rows, :] * w_y[rows, :]
             v_before = edges[2, k, rows, :] * before_y[rows, :]
             new = []
             for t in range(2):
-                load = lambda at: t_ref[t, k, at : at + 8, :]
+                load = lambda at: t_ref[t, k, at : at + TALL, :]
                 slot = (first + t) * LEVELS + k
-                c = load(8 * r)
+                c = load(TALL * r)
                 c_edge = edges[t, k, rows, :]
-                here_x = upwind(u, c, above(load, row_hi[pl.ds(slot, 1), :], r))
+                here_x = upwind(u, c, above(load, row_hi[pl.ds(slot, 1), :], r, TALL))
                 turned = pltpu.roll(here_x, 1, 0)
-                past_x = jnp.where(sublanes((8, COLS)) == 0, carry[t], turned)
-                carry[t] = turned
-                if r == TILES - 1:
-                    out_x[t] = here_x[7:8, :]
+                past_x = jnp.where(sublanes((TALL, COLS)) == 0, carry[t], turned)
+                carry[t] = turned[0:1, :]
+                if r == ROWS // TALL - 1:
+                    out_x[t] = here_x[TALL - 1 :, :]
                 here_y = upwind(v, c, ahead_y(c, c_edge))
                 past_y = behind_y(here_y, upwind(v_before, c_edge, c[:, :LANE]))
                 value = (c - (here_x - past_x)) - (here_y - past_y)
@@ -376,7 +377,7 @@
         out_shape=out_shape,
         scratch_shapes=scratch,
         input_output_aliases=aliases,
-        compiler_params=pltpu.CompilerParams(vmem_limit_bytes=58 * 2**20),
+        compiler_params=pltpu.CompilerParams(vmem_limit_bytes=48 * 2**20),
         cost_estimate=pl.CostEstimate(flops=24_000_000, bytes_accessed=9_400_000, transcendentals=0),
         name="advect_forcing" if first == 0 else "advect_rest",
     )(*operands)
@@ -399,7 +400,7 @@
         out_shape=f32(8, 2 * EXT + 8, COLS),
         scratch_shapes=[pltpu.VMEM((8, 8, LANE), jnp.float32), pltpu.SemaphoreType.DMA((1,))],
         input_output_aliases={0: 0},
-        compiler_params=pltpu.CompilerParams(vmem_limit_bytes=58 * 2**20),
+        compiler_params=pltpu.CompilerParams(vmem_limit_bytes=48 * 2**20),
         cost_estimate=pl.CostEstimate(flops=1000, bytes_accessed=100_000, transcendentals=0),
         name="insert_maximum",
     )(parcels, tops)

time: 50.6 us -> 50.1 us (level)
  Pallas kernels: 25.7 us -> 22.1 us
  waiting for transfers between devices: 0.93 us -> 2.5 us
  local copies, waits for them, and re-layouts: 1.86 us -> 3.21 us
    pallas_call x2, Pallas kernels: 16.6 us -> 12.8 us  [advect(): pl.pallas_call(functools.partial(advect_kernel, first), in_specs=ins, out...]
    all_to_all x1, waiting for transfers between devices: 0.92 us -> 2.49 us  [shards(): lax.all_to_all(insert(parcels, tops), 'by', split_axis=0, concat_axis=0,...]
    unnamed x10 -> x14, local copies, waits for them, and re-layouts: 1.86 us -> 3.21 us
    pallas_call x1, Pallas kernels: 2.62 us -> 3.31 us  [solve(): pl.pallas_call(solve_kernel, in_specs=[ANY], out_specs=VMEM, out_shape=f3...]
    pallas_call x1, Pallas kernels: 1.47 us -> 0.86 us  [insert(): pl.pallas_call(insert_kernel, in_specs=[HBM, VMEM], out_specs=HBM, out_sh...]
    ppermute x4, starting transfers between devices: 7.34 us -> 7.86 us  [exchange(): return lax.ppermute(x, axis, pairs)]
  transfers between devices with their start and end apart: 6 -> 6, of which waited for: 1 -> 1; matrix products, arithmetic and copies ran while one was open for 0% -> 0% of each run, Pallas kernels for 33% -> 26%
where the time goes in v5:
time: 50.1 us; the launch traced here: 49.7 us
  Pallas kernels  22.1 us (44%)
  starting transfers between devices  21.1 us (42%)
  local copies, waits for them, and re-layouts  3.21 us (6%)
  waiting for transfers between devices  2.5 us (5%)
  between operations  0.79 us (2%)
    pallas_call x2, Pallas kernels, advect(): pl.pallas_call(functools.partial(advect_kernel, first), in_specs=ins, out...  12.8 us
    all_to_all x1, starting transfers between devices, shards(): tops = lax.all_to_all(top, 'bx', split_axis=0, concat_axis=0, tiled=True)  8.22 us
    ppermute x4, starting transfers between devices, exchange(): return lax.ppermute(x, axis, pairs)  7.86 us
    pallas_call x1, Pallas kernels, pack(): pl.pallas_call(pack_kernel, in_specs=[HBM] * 5, out_specs=[VMEM] * 5, out...  5.16 us
    all_to_all x1, starting transfers between devices, shards(): lax.all_to_all(insert(parcels, tops), 'by', split_axis=0, concat_axis=0,...  4.97 us
    pallas_call x1, Pallas kernels, solve(): pl.pallas_call(solve_kernel, in_specs=[ANY], out_specs=VMEM, out_shape=f3...  3.31 us
    unnamed x14, local copies, waits for them, and re-layouts  3.21 us
    all_to_all x1, waiting for transfers between devices, shards(): lax.all_to_all(insert(parcels, tops), 'by', split_axis=0, concat_axis=0,...  2.49 us
  transfers between devices with their start and end apart: 6, of which 1 were waited for; matrix products, arithmetic and copies ran while one was open for 0% of the time, Pallas kernels for 26%

profile of v5, /device:TPU:1, one launch (start us, length us, event | category | flops | bytes accessed | tf_op | source)
XLA Modules:
  0.0 49.7 jit_solution(7869451476126330921)
XLA Ops:
  0.6 0.0 copy-start.4
  0.6 0.0 copy-start
  0.7 0.0 copy-start.5
  0.7 5.2 %pack_edges.1 = (f32[80,256]{1,0:T(8,128)}, f32[80,256]{1,0:T(8,128)}, f32[128,128]{1,0:T(8,128)}, f32[128,128]{1,0:T(8,128)}, f32[16,8,128]{2,1,0:T(8,128)}) custom-call(f32[12]{0:T(128)} %refs_0_.2, f32[4,12,128,256]{3,2,1,0:T(8,128)} %refs_0_.3, f32[2,12,128,256]{3,2,1,0:T(8,128)} %refs_1_.3, s32[128,256]{1,0:T(8,128)} %refs_2_.3, f32[128,256]{1,0:T(8,128)} %refs_8_.1), custom_call_target="tpu_custom_call" | custom-call | flops 4000000 | bytes 7400000 | tf_op jit(solution)/shard_map/pack_edges/pallas_call | solution.py:167
  5.8 2.2 %collective-permute-start = (f32[80,256]{1,0:T(8,128)}, f32[80,256]{1,0:T(8,128)S(1)}, u32[]{:S(2)}, u32[]{:S(2)}) collective-permute-start(f32[80,256]{1,0:T(8,128)} %get-tuple-element.9), channel_id=1, source_target_pairs={{0,8},{8,0},{16,24},{24,16},{32,40},{40,32},{48,56},{56,48},{64,72... | collective-permute-start | bytes 245768 | tf_op jit(solution)/shard_map/ppermute | solution.py:493
  8.0 1.3 %collective-permute-start.1 = (f32[80,256]{1,0:T(8,128)}, f32[80,256]{1,0:T(8,128)}, u32[]{:S(2)}, u32[]{:S(2)}) collective-permute-start(f32[80,256]{1,0:T(8,128)} %get-tuple-element.10), channel_id=1, source_target_pairs={{8,16},{16,8},{24,32},{32,24},{40,48},{48,40},{56,64},{64,56},{72,... | collective-permute-start | bytes 245768 | tf_op jit(solution)/shard_map/ppermute | solution.py:493
  9.3 1.0 %collective-permute-start.2 = (f32[128,128]{1,0:T(8,128)}, f32[128,128]{1,0:T(8,128)S(1)}, u32[]{:S(2)}, u32[]{:S(2)}) collective-permute-start(f32[128,128]{1,0:T(8,128)} %get-tuple-element.11), channel_id=1, source_target_pairs={{0,1},{1,0},{2,3},{3,2},{4,5},{5,4},{6,7},{7,6},{8,9},{9,8},{10,11... | collective-permute-start | bytes 196616 | tf_op jit(solution)/shard_map/ppermute | solution.py:493
  10.3 3.4 %collective-permute-start.3 = (f32[128,128]{1,0:T(8,128)}, f32[128,128]{1,0:T(8,128)}, u32[]{:S(2)}, u32[]{:S(2)}) collective-permute-start(f32[128,128]{1,0:T(8,128)} %get-tuple-element.12), channel_id=1, source_target_pairs={{1,2},{2,1},{3,4},{4,3},{5,6},{6,5},{9,10},{10,9},{11,12},{12,11},... | collective-permute-start | bytes 196616 | tf_op jit(solution)/shard_map/ppermute | solution.py:493
  13.7 8.2 %all-to-all-start = ((f32[16,8,128]{2,1,0:T(8,128)}), f32[16,8,128]{2,1,0:T(8,128)}, u32[]{:S(2)}, u32[]{:S(2)}) async-start(f32[16,8,128]{2,1,0:T(8,128)} %get-tuple-element.15), calls=%async_computation | async-start | bytes 131072 | tf_op jit(solution)/shard_map/all_to_all | solution.py:499
  21.9 0.0 collective-permute-done.2.refs_6_.refs_5_
  21.9 0.0 collective-permute-done.3.refs_7_.refs_6_
  22.0 0.0 collective-permute-done.refs_4_.refs_3_
  22.0 0.0 collective-permute-done.1.refs_5_.refs_4_
  22.0 0.0 copy-done.4
  22.0 0.0 copy-done
  22.0 0.0 copy-done.5
  22.0 0.0 copy-start.6
  22.0 0.6 %copy-done.6 = f32[12]{0:T(128)S(1)} copy-done((f32[12]{0:T(128)S(1)}, f32[12]{0:T(128)}, u32[]{:S(2)}) %copy-start.6) | copy-done | bytes 72
  22.7 6.4 %advect_forcing.1 = (f32[4,12,128,256]{3,2,1,0:T(8,128)}, f32[8,56,256]{2,1,0:T(8,128)S(1)}) custom-call(f32[12]{0:T(128)S(1)} %copy-done.6, f32[4,12,128,256]{3,2,1,0:T(8,128)} %refs_0_.3, f32[2,12,128,256]{3,2,1,0:T(8,128)S(1)} %copy-done, s32[128,256]{1,0:T(8,128)S(1)} %copy-done.4, f32[80,256]{1,0:T(8,128)S(1)} %collective-permute-done.refs_4_.refs_3_, ...), custom_call_target="tpu_custom_call" | custom-call | flops 24000000 | bytes 9400000 | tf_op jit(solution)/shard_map/advect_forcing/pallas_call | solution.py:373
  29.0 0.0 copy-start.1
  29.1 0.8 %copy-done.1 = f32[8,56,256]{2,1,0:T(8,128)} copy-done((f32[8,56,256]{2,1,0:T(8,128)}, f32[8,56,256]{2,1,0:T(8,128)S(1)}, u32[]{:S(2)}) %copy-start.1) | copy-done | bytes 458776
  29.8 0.0 all-to-all-done.tops
  29.8 0.0 copy-start.2
  29.8 1.0 %copy-done.2 = f32[8,56,256]{2,1,0:T(8,128)S(1)} copy-done((f32[8,56,256]{2,1,0:T(8,128)S(1)}, f32[8,56,256]{2,1,0:T(8,128)}, u32[]{:S(2)}) %copy-start.2) | copy-done | bytes 458776
  30.8 0.9 %insert_maximum.1 = f32[8,56,256]{2,1,0:T(8,128)S(1)} custom-call(f32[8,56,256]{2,1,0:T(8,128)S(1)} %copy-done.2, f32[16,8,128]{2,1,0:T(8,128)} %all-to-all-done.tops), custom_call_target="tpu_custom_call", output_to_operand_aliasing={{}: (0, {})} | custom-call | flops 1000 | bytes 100000 | tf_op jit(solution)/shard_map/insert_maximum/pallas_call | solution.py:396
  31.7 0.0 copy-start.3
  31.7 0.8 %copy-done.3 = f32[8,56,256]{2,1,0:T(8,128)} copy-done((f32[8,56,256]{2,1,0:T(8,128)}, f32[8,56,256]{2,1,0:T(8,128)S(1)}, u32[]{:S(2)}) %copy-start.3) | copy-done | bytes 458776
  32.5 5.0 %all-to-all-start.1 = ((f32[8,56,256]{2,1,0:T(8,128)}), f32[8,56,256]{2,1,0:T(8,128)}, u32[]{:S(2)}, u32[]{:S(2)}) async-start(f32[8,56,256]{2,1,0:T(8,128)} %copy-done.3), calls=%async_computation.1 | async-start | bytes 917504 | tf_op jit(solution)/shard_map/all_to_all | solution.py:501
  37.5 6.4 %advect_rest.1 = f32[4,12,128,256]{3,2,1,0:T(8,128)} custom-call(f32[4,12,128,256]{3,2,1,0:T(8,128)} %refs_0_.3, f32[2,12,128,256]{3,2,1,0:T(8,128)S(1)} %copy-done, s32[128,256]{1,0:T(8,128)S(1)} %copy-done.4, f32[80,256]{1,0:T(8,128)S(1)} %collective-permute-done.refs_4_.refs_3_, ...), custom_call_target="tpu_custom_call", output_to_operand_aliasing={{}: (7, {})} | custom-call | flops 24000000 | bytes 9400000 | tf_op jit(solution)/shard_map/advect_rest/pallas_call | solution.py:373
  43.9 2.5 %all-to-all-done.1.got = f32[8,56,256]{2,1,0:T(8,128)} async-done(((f32[8,56,256]{2,1,0:T(8,128)}), f32[8,56,256]{2,1,0:T(8,128)}, u32[]{:S(2)}, u32[]{:S(2)}) %all-to-all-start.1) | async-done | bytes 458784 | tf_op jit(solution)/shard_map/all_to_all | solution.py:501
  46.3 3.3 %chebyshev.1 = f32[16,2048]{1,0:T(8,128)} custom-call(f32[8,56,256]{2,1,0:T(8,128)} %all-to-all-done.1.got), custom_call_target="tpu_custom_call" | custom-call | flops 6000000 | bytes 600000 | tf_op jit(solution)/shard_map/chebyshev/pallas_call | solution.py:470
Async XLA Ops:
  0.6 21.3 %copy-start.4 = (s32[128,256]{1,0:T(8,128)S(1)}, s32[128,256]{1,0:T(8,128)}, u32[]{:S(2)}) copy-start(s32[128,256]{1,0:T(8,128)} %refs_2_.3) | copy-start | bytes 393220
  0.6 21.3 %copy-start = (f32[2,12,128,256]{3,2,1,0:T(8,128)S(1)}, f32[2,12,128,256]{3,2,1,0:T(8,128)}, u32[]{:S(2)}) copy-start(f32[2,12,128,256]{3,2,1,0:T(8,128)} %refs_1_.3) | copy-start | bytes 9437188
  0.7 21.3 %copy-start.5 = (f32[128,256]{1,0:T(8,128)S(1)}, f32[128,256]{1,0:T(8,128)}, u32[]{:S(2)}) copy-start(f32[128,256]{1,0:T(8,128)} %refs_8_.1) | copy-start | bytes 393220
  5.8 16.1 %collective-permute-start = (f32[80,256]{1,0:T(8,128)}, f32[80,256]{1,0:T(8,128)S(1)}, u32[]{:S(2)}, u32[]{:S(2)}) collective-permute-start(f32[80,256]{1,0:T(8,128)} %get-tuple-element.9), channel_id=1, source_target_pairs={{0,8},{8,0},{16,24},{24,16},{32,40},{40,32},{48,56},{56,48},{64,72... | collective-permute-start | bytes 245768 | tf_op jit(solution)/shard_map/ppermute | solution.py:493
  8.0 13.9 %collective-permute-start.1 = (f32[80,256]{1,0:T(8,128)}, f32[80,256]{1,0:T(8,128)}, u32[]{:S(2)}, u32[]{:S(2)}) collective-permute-start(f32[80,256]{1,0:T(8,128)} %get-tuple-element.10), channel_id=1, source_target_pairs={{8,16},{16,8},{24,32},{32,24},{40,48},{48,40},{56,64},{64,56},{72,... | collective-permute-start | bytes 245768 | tf_op jit(solution)/shard_map/ppermute | solution.py:493
  9.3 12.6 %collective-permute-start.2 = (f32[128,128]{1,0:T(8,128)}, f32[128,128]{1,0:T(8,128)S(1)}, u32[]{:S(2)}, u32[]{:S(2)}) collective-permute-start(f32[128,128]{1,0:T(8,128)} %get-tuple-element.11), channel_id=1, source_target_pairs={{0,1},{1,0},{2,3},{3,2},{4,5},{5,4},{6,7},{7,6},{8,9},{9,8},{10,11... | collective-permute-start | bytes 196616 | tf_op jit(solution)/shard_map/ppermute | solution.py:493
  10.3 11.7 %collective-permute-start.3 = (f32[128,128]{1,0:T(8,128)}, f32[128,128]{1,0:T(8,128)}, u32[]{:S(2)}, u32[]{:S(2)}) collective-permute-start(f32[128,128]{1,0:T(8,128)} %get-tuple-element.12), channel_id=1, source_target_pairs={{1,2},{2,1},{3,4},{4,3},{5,6},{6,5},{9,10},{10,9},{11,12},{12,11},... | collective-permute-start | bytes 196616 | tf_op jit(solution)/shard_map/ppermute | solution.py:493
  13.7 16.1 %all-to-all-start = ((f32[16,8,128]{2,1,0:T(8,128)}), f32[16,8,128]{2,1,0:T(8,128)}, u32[]{:S(2)}, u32[]{:S(2)}) async-start(f32[16,8,128]{2,1,0:T(8,128)} %get-tuple-element.15), calls=%async_computation | async-start | bytes 131072 | tf_op jit(solution)/shard_map/all_to_all | solution.py:499
  22.0 0.7 %copy-start.6 = (f32[12]{0:T(128)S(1)}, f32[12]{0:T(128)}, u32[]{:S(2)}) copy-start(f32[12]{0:T(128)} %refs_0_.2) | copy-start | bytes 148
  29.0 0.8 %copy-start.1 = (f32[8,56,256]{2,1,0:T(8,128)}, f32[8,56,256]{2,1,0:T(8,128)S(1)}, u32[]{:S(2)}) copy-start(f32[8,56,256]{2,1,0:T(8,128)S(1)} %get-tuple-element.14._) | copy-start | bytes 1376260
  29.8 1.0 %copy-start.2 = (f32[8,56,256]{2,1,0:T(8,128)S(1)}, f32[8,56,256]{2,1,0:T(8,128)}, u32[]{:S(2)}) copy-start(f32[8,56,256]{2,1,0:T(8,128)} %copy-done.1) | copy-start | bytes 1376260
  31.7 0.8 %copy-start.3 = (f32[8,56,256]{2,1,0:T(8,128)}, f32[8,56,256]{2,1,0:T(8,128)S(1)}, u32[]{:S(2)}) copy-start(f32[8,56,256]{2,1,0:T(8,128)S(1)} %insert_maximum.1) | copy-start | bytes 1376260
  32.5 13.9 %all-to-all-start.1 = ((f32[8,56,256]{2,1,0:T(8,128)}), f32[8,56,256]{2,1,0:T(8,128)}, u32[]{:S(2)}, u32[]{:S(2)}) async-start(f32[8,56,256]{2,1,0:T(8,128)} %copy-done.3), calls=%async_computation.1 | async-start | bytes 917504 | tf_op jit(solution)/shard_map/all_to_all | solution.py:501

commit v6 on v5

v6 whole, which is shorter than its diff:
```python
import functools

import jax
import jax.numpy as jnp
from jax import lax
from jax.experimental import pallas as pl
from jax.experimental.pallas import tpu as pltpu
from jax.sharding import PartitionSpec as P

ITERS = 3
TRACERS = 4
LEVELS = 12
ROWS = 128
COLS = 256
TILES = ROWS // 8
LANE = 128
WIDE = 8 * COLS
EXT = 24
CHUNK = 32
TALL = 16

SPEED, WET, PART, COEF, EDGE, MIXED, MESSAGE = 48, 60, 64, 68, 72, 80, 96
MOST = 100
ANY = pl.BlockSpec(memory_space=pl.ANY)
HBM = pl.BlockSpec(memory_space=pltpu.HBM)
VMEM = pl.BlockSpec(memory_space=pltpu.VMEM)


def f32(*shape):
    return jax.ShapeDtypeStruct(shape, jnp.float32)


def lanes(shape):
    return lax.broadcasted_iota(jnp.int32, shape, len(shape) - 1)


def sublanes(shape):
    return lax.broadcasted_iota(jnp.int32, shape, len(shape) - 2)


def coefficient(depth, wet):
    return depth * (0.1 + 0.9 * wet)


def positive(x):
    return jnp.maximum(x, 0.0)


def negative(x):
    return jnp.minimum(x, 0.0)


def upwind(speed, here, ahead):
    return speed * jnp.where(speed > 0.0, here, ahead)


def edge_terms(hi, lo, wet, thick_lanes):
    lane = lanes(hi.shape)
    used = (lane % 2 == 0) & (lane < 2 * LEVELS)
    last = jnp.broadcast_to(wet[:, COLS - 1 :], hi.shape)
    first = jnp.broadcast_to(wet[:, 0:1], hi.shape)
    speed = jnp.where(used, pltpu.roll(hi, LANE - 2 * SPEED, 1), 0.0)
    q_last = thick_lanes * (0.2 * hi - 0.8 * pltpu.roll(hi, LANE - 2 * LEVELS, 1))
    share = jnp.sum(jnp.where(speed > 0.0, speed * q_last, 0.0), axis=1, keepdims=True)
    terms = jnp.where(lane == 2 * LEVELS, share, jnp.minimum(speed, 0.0)) * last
    turned = pltpu.roll(lo, 65, 1)
    q_first = pltpu.roll(thick_lanes, 64, 1) * (0.2 * turned - 0.8 * pltpu.roll(turned, LANE - 2 * LEVELS, 1))
    used = (lane % 2 == 0) & (lane >= 64) & (lane < 64 + 2 * LEVELS)
    return terms + jnp.where(used, q_first, jnp.where(lane == 64 + 2 * LEVELS, 1.0, 0.0)) * first


def pack_kernel(thick_hbm, t_hbm, v_hbm, ocean_hbm, depth_hbm, row_even, row_odd, col_even, col_odd, top, part, terms,
                t_ref, v_ref, ocean_ref, depth_ref, thick, row_both, col_both, total, flux_x, flux_y, sems):
    odd_x, odd_y = lax.axis_index("bx") % 2, lax.axis_index("by") % 2
    row_hi, row_lo = row_both.at[0], row_both.at[1]
    col_hi, col_lo = col_both.at[0], col_both.at[1]
    chunks = ROWS // CHUNK

    def chunk_copies(c):
        rows = pl.ds(pl.multiple_of(c * CHUNK, CHUNK), CHUNK)
        return (
            pltpu.make_async_copy(t_hbm.at[:, :, rows, :], t_ref.at[:, :, rows, :], sems.at[0, c]),
            pltpu.make_async_copy(v_hbm.at[:, :, rows, :], v_ref.at[:, :, rows, :], sems.at[1, c]),
        )

    small = [
        pltpu.make_async_copy(ocean_hbm, ocean_ref, sems.at[2, 0]),
        pltpu.make_async_copy(depth_hbm, depth_ref, sems.at[2, 1]),
        pltpu.make_async_copy(thick_hbm, thick, sems.at[2, 2]),
    ]
    for copy in small:
        copy.start()
    for c in range(chunks):
        for copy in chunk_copies(c):
            copy.start()
    for copy in small:
        copy.wait()
    wet = ocean_ref[...].astype(jnp.float32)
    coef = coefficient(depth_ref[...], wet)
    most = jnp.max(jnp.max(coef, axis=0, keepdims=True), axis=1, keepdims=True)
    top[...] = jnp.broadcast_to(most[None], top.shape)
    thick_lanes = jnp.zeros((1, LANE), jnp.float32)
    for k in range(LEVELS):
        thick_lanes = jnp.where(lanes((1, LANE)) == 2 * k, thick[k], thick_lanes)

    def gather(c, _):
        for copy in chunk_copies(c):
            copy.wait()
        lane = lanes((CHUNK, LANE))
        rows = pl.ds(pl.multiple_of(c * CHUNK, CHUNK), CHUNK)
        before = pl.ds(jnp.maximum(c * CHUNK - 1, 0), 1)
        start = pl.ds(pl.multiple_of(c * CHUNK, CHUNK), 1)
        ocean = ocean_ref[rows, :].astype(jnp.float32)
        hi = jnp.where(lane == 2 * WET, pltpu.roll(ocean[:, LANE:], (2 * WET + 1) % LANE, 1), 0.0)
        lo = jnp.where(lane == 2 * WET - 1, pltpu.roll(ocean[:, :LANE], 2 * WET - 1, 1), 0.0)
        for k in range(LEVELS):
            for t in range(TRACERS):
                s = t * LEVELS + k
                hi = jnp.where(lane == 2 * s, pltpu.roll(t_ref[t, k, rows, LANE:], 2 * s + 1, 1), hi)
                place = (2 * s - 1) % LANE
                lo = jnp.where(lane == place, pltpu.roll(t_ref[t, k, rows, :LANE], place, 1), lo)
            s = SPEED + k
            hi = jnp.where(lane == 2 * s, pltpu.roll(v_ref[1, k, rows, LANE:], 2 * s + 1, 1), hi)
        col_hi[rows, :] = hi
        col_lo[rows, :] = lo
        terms[rows, :] = edge_terms(hi, lo, ocean, thick_lanes)
        whole = jnp.zeros((CHUNK, COLS), jnp.float32)
        out_x = jnp.zeros((CHUNK, COLS), jnp.float32)
        out_y = jnp.zeros((CHUNK, COLS), jnp.float32)
        between = jnp.zeros((1, COLS), jnp.float32)
        for k in range(LEVELS):
            warm, salt = 0.2 * thick[k], 0.8 * thick[k]
            q = warm * t_ref[0, k, rows, :] - salt * t_ref[1, k, rows, :]
            whole = whole + q
            out_x = out_x + upwind(v_ref[0, k, rows, :], q, pltpu.roll(q, CHUNK - 1, 0))
            out_y = out_y + upwind(v_ref[1, k, rows, :], q, pltpu.roll(q, COLS - 1, 1))
            mixed = lambda at: warm * t_ref[0, k, at, :] - salt * t_ref[1, k, at, :]
            between = between + upwind(v_ref[0, k, before, :], mixed(before), mixed(start))
        total[rows, :] = whole
        flux_y[rows, :] = out_y
        flux_x[before, :] = between
        flux_x[rows, :] = out_x
        return 0

    lax.fori_loop(0, chunks, gather, 0)
    load_wet = lambda at: ocean_ref[at : at + 8, :].astype(jnp.float32)
    row, col = sublanes((8, COLS)), lanes((8, COLS))
    turned = jnp.zeros((8, COLS), jnp.float32)
    for r in range(TILES):
        rows = pl.ds(8 * r, 8)
        here = load_wet(8 * r)
        out_x = flux_x[rows, :] * here
        if r < TILES - 1:
            out_x = out_x * load_wet(8 * r + 1)
        else:
            out_x = jnp.where(row == 7, 0.0, out_x * pltpu.roll(here, 7, 0))
        out_y = jnp.where(col == COLS - 1, 0.0, flux_y[rows, :] * (here * pltpu.roll(here, COLS - 1, 1)))
        past = turned
        turned = pltpu.roll(out_x, 1, 0)
        past_x = jnp.where(row == 0, past, turned)
        part[rows, :] = here * (total[rows, :] - (out_x - past_x) - (out_y - pltpu.roll(out_y, 1, 1)))
    for t in range(TRACERS):
        for k in range(LEVELS):
            s = t * LEVELS + k
            row_hi[s : s + 1, :] = t_ref[t, k, ROWS - 1 : ROWS, :]
            row_lo[s : s + 1, :] = t_ref[t, k, 0:1, :]
    row_lo[SPEED:WET, :] = jnp.zeros((WET - SPEED, COLS), jnp.float32)
    for k in range(LEVELS):
        row_hi[SPEED + k : SPEED + k + 1, :] = v_ref[0, k, ROWS - 1 : ROWS, :]
        for message, at in ((row_hi, ROWS - 1), (row_lo, 0)):
            line = slice(at, at + 1)
            message[MIXED + k : MIXED + k + 1, :] = (0.2 * thick[k]) * t_ref[0, k, line, :] - (0.8 * thick[k]) * t_ref[1, k, line, :]
    for message, rows, edge in ((row_hi, slice(ROWS - 4, ROWS), ROWS - 1), (row_lo, slice(0, 4), 0)):
        tile = slice(rows.start // 8 * 8, rows.start // 8 * 8 + 8)
        here = load_wet(tile.start)
        keep = slice(rows.start - tile.start, rows.stop - tile.start)
        message[WET:PART, :] = jnp.broadcast_to(here[edge - tile.start : edge - tile.start + 1, :], (PART - WET, COLS))
        message[PART:COEF, :] = part[tile, :][keep, :]
        message[COEF:EDGE, :] = coefficient(depth_ref[tile, :], here)[keep, :]
        message[EDGE:MIXED, :LANE] = terms[tile, :]
        message[EDGE:MIXED, LANE:] = jnp.zeros((8, LANE), jnp.float32)
        message[MIXED + LEVELS :, :] = jnp.zeros((MESSAGE - MIXED - LEVELS, COLS), jnp.float32)
    row_even[...] = row_both[odd_x]
    row_odd[...] = row_both[1 - odd_x]
    col_even[...] = col_both[odd_y]
    col_odd[...] = col_both[1 - odd_y]


def pack(thickness, tracers, velocity, ocean, depth):
    block = pltpu.VMEM((ROWS, COLS), jnp.float32)
    return pl.pallas_call(
        pack_kernel,
        in_specs=[HBM] * 5,
        out_specs=[VMEM] * 7,
        out_shape=[f32(MESSAGE, COLS)] * 2 + [f32(ROWS, LANE)] * 2 + [f32(16, 8, LANE), f32(ROWS, COLS), f32(ROWS, LANE)],
        scratch_shapes=[
            pltpu.VMEM((TRACERS, LEVELS, ROWS, COLS), jnp.float32),
            pltpu.VMEM((2, LEVELS, ROWS, COLS), jnp.float32),
            pltpu.VMEM((ROWS, COLS), jnp.int32),
            block,
            pltpu.SMEM((LEVELS,), jnp.float32),
            pltpu.VMEM((2, MESSAGE, COLS), jnp.float32),
            pltpu.VMEM((2, ROWS, LANE), jnp.float32),
            block,
            block,
            block,
            pltpu.SemaphoreType.DMA((3, 4)),
        ],
        compiler_params=pltpu.CompilerParams(vmem_limit_bytes=60 * 2**20),
        cost_estimate=pl.CostEstimate(flops=20_000_000, bytes_accessed=9_400_000, transcendentals=0),
        name="pack_edges",
    )(thickness, tracers, velocity, ocean, depth)


def parcel_kernel(even_hbm, odd_hbm, own_even_hbm, own_odd_hbm, part_hbm, terms_hbm, ocean_hbm, depth_hbm, tops_hbm, send_ref,
                  rows_in, rows_out, part, terms, ocean_ref, depth_ref, tops, ext, ext_terms, sems):
    odd_x = lax.axis_index("bx") % 2
    copies = [
        (even_hbm, rows_in.at[1 - odd_x]),
        (odd_hbm, rows_in.at[odd_x]),
        (own_even_hbm, rows_out.at[1 - odd_x]),
        (own_odd_hbm, rows_out.at[odd_x]),
        (part_hbm, part),
        (terms_hbm, terms),
        (ocean_hbm, ocean_ref),
        (depth_hbm, depth_ref),
        (tops_hbm, tops),
    ]
    copies = [pltpu.make_async_copy(a, b, sems.at[i]) for i, (a, b) in enumerate(copies)]
    for copy in copies:
        copy.start()
    for copy in copies:
        copy.wait()
    before, after, first, last = rows_in.at[0], rows_in.at[1], rows_out.at[0], rows_out.at[1]
    speed, mixed, wet = slice(SPEED, WET), slice(MIXED, MIXED + LEVELS), slice(WET, WET + 1)
    flux_lo = jnp.sum(upwind(before[speed, :], before[mixed, :], first[mixed, :]), axis=0, keepdims=True)
    flux_hi = jnp.sum(upwind(last[speed, :], last[mixed, :], after[mixed, :]), axis=0, keepdims=True)
    flux_lo = flux_lo * (before[wet, :] * first[wet, :])
    flux_hi = flux_hi * (last[wet, :] * after[wet, :])
    row = sublanes((4, COLS))
    ext[0, 0:4, :] = before[PART:COEF, :] - jnp.where(row == 3, flux_lo, 0.0)
    ext[0, ROWS + 4 :, :] = after[PART:COEF, :] + jnp.where(row == 0, flux_hi, 0.0)
    ext[1, 0:4, :] = before[COEF:EDGE, :]
    ext[1, ROWS + 4 :, :] = after[COEF:EDGE, :]
    ext_terms[0:4, :] = before[EDGE + 4 : MIXED, :LANE]
    ext_terms[ROWS + 4 :, :] = after[EDGE : EDGE + 4, :LANE]
    row = sublanes((8, COLS))
    for r in range(TILES):
        rows = slice(8 * r, 8 * r + 8)
        value = part[rows, :]
        if r == 0:
            value = value + jnp.where(row == 0, flux_lo, 0.0)
        if r == TILES - 1:
            value = value - jnp.where(row == 7, flux_hi, 0.0)
        ext[0, 8 * r + 4 : 8 * r + 12, :] = value
        ext[1, 8 * r + 4 : 8 * r + 12, :] = coefficient(depth_ref[rows, :], ocean_ref[rows, :].astype(jnp.float32))
        ext_terms[8 * r + 4 : 8 * r + 12, :] = terms[rows, :]
    most = jnp.max(tops[...], axis=0)[0:1, :]
    for j in range(8):
        at = 16 * j
        send_ref[j, 0:22, :] = ext[0, at + 1 : at + 23, :]
        send_ref[j, 22:44, :] = ext[1, at + 1 : at + 23, :]
        for half in range(2):
            value = ext_terms[at + 12 * half : at + 12 * half + 12, :]
            send_ref[j, 44:56, half * LANE : (half + 1) * LANE] = jnp.where(lanes((12, LANE)) == MOST, most, value)


def parcel(even, odd, own_even, own_odd, part, terms, ocean, depth, tops):
    block = pltpu.VMEM((ROWS, COLS), jnp.float32)
    return pl.pallas_call(
        parcel_kernel,
        in_specs=[ANY] * 9,
        out_specs=VMEM,
        out_shape=f32(8, 56, COLS),
        scratch_shapes=[
            pltpu.VMEM((2, MESSAGE, COLS), jnp.float32),
            pltpu.VMEM((2, MESSAGE, COLS), jnp.float32),
            block,
            pltpu.VMEM((ROWS, LANE), jnp.float32),
            pltpu.VMEM((ROWS, COLS), jnp.int32),
            block,
            pltpu.VMEM((16, 8, LANE), jnp.float32),
            pltpu.VMEM((2, ROWS + 8, COLS), jnp.float32),
            pltpu.VMEM((ROWS + 8, LANE), jnp.float32),
            pltpu.SemaphoreType.DMA((9,)),
        ],
        compiler_params=pltpu.CompilerParams(vmem_limit_bytes=53 * 2**20),
        cost_estimate=pl.CostEstimate(flops=1_000_000, bytes_accessed=1_500_000, transcendentals=0),
        name="parcels",
    )(even, odd, own_even, own_odd, part, terms, ocean, depth, tops)


def ahead_y(x, edge):
    last = lanes((x.shape[0], LANE)) == LANE - 1
    a, b = pltpu.roll(x[:, :LANE], LANE - 1, 1), pltpu.roll(x[:, LANE:], LANE - 1, 1)
    return jnp.concatenate([jnp.where(last, b, a), jnp.where(last, edge, b)], 1)


def behind_y(x, edge):
    first = lanes((x.shape[0], LANE)) == 0
    a, b = pltpu.roll(x[:, :LANE], 1, 1), pltpu.roll(x[:, LANE:], 1, 1)
    return jnp.concatenate([jnp.where(first, edge, a), jnp.where(first, a, b)], 1)


def above(load, edge, r, tall=8):
    if (r + 1) * tall < ROWS:
        return load(tall * r + 1)
    return jnp.where(sublanes((tall, COLS)) == tall - 1, edge, pltpu.roll(load(tall * r), tall - 1, 0))


def advect_kernel(t_hbm, v_hbm, ocean_hbm, row_even, row_odd, col_even, col_odd, out_hbm,
                  t_ref, v_ref, out_ref, ocean_ref, rows_in, cols_in, w_x, w_y, before_y, edges, sems, small_sems):
    odd_x, odd_y = lax.axis_index("bx") % 2, lax.axis_index("by") % 2
    row_lo, row_hi = rows_in.at[0], rows_in.at[1]
    small = [
        (ocean_hbm, ocean_ref),
        (row_even, rows_in.at[1 - odd_x]),
        (row_odd, rows_in.at[odd_x]),
        (col_even, cols_in.at[1 - odd_y]),
        (col_odd, cols_in.at[odd_y]),
    ]
    small = [pltpu.make_async_copy(a, b, small_sems.at[i]) for i, (a, b) in enumerate(small)]

    def tracers_in(k):
        return pltpu.make_async_copy(t_hbm.at[:, k], t_ref.at[:, k], sems.at[0, k])

    def velocity_in(k):
        return pltpu.make_async_copy(v_hbm.at[:, k], v_ref.at[:, k], sems.at[1, k])

    def tracers_out(k):
        return pltpu.make_async_copy(out_ref.at[:, k], out_hbm.at[:, k], sems.at[2, k])

    for copy in small:
        copy.start()
    for k in range(LEVELS):
        tracers_in(k).start()
        velocity_in(k).start()
    for copy in small:
        copy.wait()
    even = lanes((8, LANE)) % 2 == 0
    load_wet = lambda at: ocean_ref[at : at + 8, :].astype(jnp.float32)
    for r in range(TILES):
        rows = pl.ds(8 * r, 8)
        edge = jnp.where(even, cols_in[0, rows, :], cols_in[1, rows, :])
        for k in range(LEVELS):
            for i in range(TRACERS + 1):
                edges[i, k, rows, :] = pltpu.roll(edge, (LANE - 2 * (i * LEVELS + k)) % LANE, 1)
        here = load_wet(8 * r)
        wet_edge = pltpu.roll(edge, LANE - 2 * WET, 1)
        w_x[rows, :] = here * above(load_wet, row_hi[WET : WET + 1, :], r)
        w_y[rows, :] = here * ahead_y(here, wet_edge)
        before_y[rows, :] = here[:, :LANE] * wet_edge
    w_before = load_wet(0)[0:1, :] * row_lo[WET : WET + 1, :]

    def level(k, _):
        tracers_in(k).wait()
        velocity_in(k).wait()
        u_before = row_lo[pl.ds(SPEED + k, 1), :] * w_before
        carry = [upwind(u_before, row_lo[pl.ds(t * LEVELS + k, 1), :], t_ref[t, k, 0:1, :]) for t in range(TRACERS)]
        for r in range(ROWS // TALL):
            rows = pl.ds(TALL * r, TALL)
            u = v_ref[0, k, rows, :] * w_x[rows, :]
            v = v_ref[1, k, rows, :] * w_y[rows, :]
            v_before = edges[TRACERS, k, rows, :] * before_y[rows, :]
            for t in range(TRACERS):
                load = lambda at: t_ref[t, k, at : at + TALL, :]
                c = load(TALL * r)
                c_edge = edges[t, k, rows, :]
                here_x = upwind(u, c, above(load, row_hi[pl.ds(t * LEVELS + k, 1), :], r, TALL))
                turned = pltpu.roll(here_x, 1, 0)
                past_x = jnp.where(sublanes((TALL, COLS)) == 0, carry[t], turned)
                carry[t] = turned[0:1, :]
                here_y = upwind(v, c, ahead_y(c, c_edge))
                past_y = behind_y(here_y, upwind(v_before, c_edge, c[:, :LANE]))
                out_ref[t, k, rows, :] = (c - (here_x - past_x)) - (here_y - past_y)
        tracers_out(k).start()
        return 0

    lax.fori_loop(0, LEVELS, level, 0)
    for k in range(LEVELS):
        tracers_out(k).wait()


def advect(tracers, velocity, ocean, row_even, row_odd, col_even, col_odd):
    block = pltpu.VMEM((ROWS, COLS), jnp.float32)
    return pl.pallas_call(
        advect_kernel,
        in_specs=[HBM] * 3 + [ANY] * 4,
        out_specs=HBM,
        out_shape=f32(TRACERS, LEVELS, ROWS, COLS),
        scratch_shapes=[
            pltpu.VMEM((TRACERS, LEVELS, ROWS, COLS), jnp.float32),
            pltpu.VMEM((2, LEVELS, ROWS, COLS), jnp.float32),
            pltpu.VMEM((TRACERS, LEVELS, ROWS, COLS), jnp.float32),
            pltpu.VMEM((ROWS, COLS), jnp.int32),
            pltpu.VMEM((2, MESSAGE, COLS), jnp.float32),
            pltpu.VMEM((2, ROWS, LANE), jnp.float32),
            block,
            block,
            pltpu.VMEM((ROWS, LANE), jnp.float32),
            pltpu.VMEM((TRACERS + 1, LEVELS, ROWS, LANE), jnp.float32),
            pltpu.SemaphoreType.DMA((3, LEVELS)),
            pltpu.SemaphoreType.DMA((5,)),
        ],
        compiler_params=pltpu.CompilerParams(vmem_limit_bytes=52 * 2**20),
        cost_estimate=pl.CostEstimate(flops=40_000_000, bytes_accessed=15_800_000, transcendentals=0),
        name="advect",
    )(tracers, velocity, ocean, row_even, row_odd, col_even, col_odd)


NEAR = ((1, 0, 0.5), (-1, 0, 0.5), (0, 1, 0.5), (0, -1, 0.5), (1, 1, 0.125), (1, -1, 0.125), (-1, 1, 0.125), (-1, -1, 0.125))


def moved(x, rows, cols):
    if cols:
        lane = lanes(x.shape)
        x = pltpu.roll(x, (-cols) % x.shape[1], 1)
        x = jnp.where(lane == (x.shape[1] - 1 if cols > 0 else 0), 0.0, x)
    if rows:
        x = pltpu.roll(x, (-rows) % x.shape[0], 0)
    return x


def solve_kernel(got_ref, out_ref, h_ref, f_ref, weight):
    for j in range(8):
        cols = pl.ds(j * COLS, COLS)
        f_ref[1:23, cols] = got_ref[j, 0:22, :]
        h_ref[1:23, cols] = got_ref[j, 22:44, :]
    for ref in (f_ref, h_ref):
        for row in (0, EXT - 1):
            ref[row : row + 1, :] = jnp.zeros((1, WIDE), jnp.float32)
    lane = lanes((12, LANE))
    for j in range(7):
        for half in range(2):
            rows, part = slice(12 * half, 12 * half + 12), slice(LANE * half, LANE * half + LANE)
            pairs = got_ref[j, 44:56, part] * pltpu.roll(got_ref[j + 1, 44:56, part], 64, 1)
            flux = jnp.sum(jnp.where(lane < 32, pairs, 0.0), axis=1, keepdims=True)
            last = pl.ds((j + 1) * COLS - LANE, LANE)
            after = pl.ds((j + 1) * COLS, LANE)
            f_ref[rows, last] = f_ref[rows, last] - jnp.where(lane == LANE - 1, flux, 0.0)
            f_ref[rows, after] = f_ref[rows, after] + jnp.where(lane == 0, flux, 0.0)
    most = got_ref[0, 44:45, MOST : MOST + 1]
    for j in range(1, 8):
        most = jnp.maximum(most, got_ref[j, 44:45, MOST : MOST + 1])
    lam_max = 0.5 + 10.0 * most
    theta = (lam_max + 0.5) / 2.0
    delta = (lam_max - 0.5) / 2.0
    sigma = theta / delta
    rho = 1.0 / sigma
    h = h_ref[...]
    sides = {c: moved(h, 0, c) for c in (-1, 0, 1)}
    for n, (a, b, w) in enumerate(NEAR):
        weight[n] = w * (h + moved(sides[b], a, 0))
    inside = h > 0.0
    resid = f_ref[...]
    direction = resid / theta
    answer = jnp.zeros_like(resid)
    for _ in range(ITERS):
        sides = {c: moved(direction, 0, c) for c in (-1, 0, 1)}
        applied = 0.5 * direction
        for n, (a, b, w) in enumerate(NEAR):
            applied = applied + weight[n] * (direction - moved(sides[b], a, 0))
        resid = jnp.where(inside, resid - applied, 0.0)
        answer = answer + direction
        rho_next = 1.0 / (2.0 * sigma - rho)
        direction = rho_next * rho * direction + (2.0 * rho_next / delta) * resid
        rho = rho_next
    out_ref[...] = (answer + direction)[4:20, :]


def solve(got):
    return pl.pallas_call(
        solve_kernel,
        in_specs=[VMEM],
        out_specs=VMEM,
        out_shape=f32(16, WIDE),
        scratch_shapes=[
            pltpu.VMEM((EXT, WIDE), jnp.float32),
            pltpu.VMEM((EXT, WIDE), jnp.float32),
            pltpu.VMEM((8, EXT, WIDE), jnp.float32),
        ],
        compiler_params=pltpu.CompilerParams(vmem_limit_bytes=12 * 2**20),
        cost_estimate=pl.CostEstimate(flops=6_000_000, bytes_accessed=600_000, transcendentals=0),
        name="chebyshev",
    )(got)


def exchange(x, axis, odd):
    count = lax.axis_size(axis)
    pairs = []
    for i in range(odd, count - 1, 2):
        pairs += [(i, i + 1), (i + 1, i)]
    return lax.ppermute(x, axis, pairs)


def shards(tracers, velocity, ocean, thickness, depth):
    row_even, row_odd, col_even, col_odd, top, part, terms = pack(thickness, tracers, velocity, ocean, depth)
    from_even, from_odd = exchange(row_even, "bx", 0), exchange(row_odd, "bx", 1)
    tops = lax.all_to_all(top, "bx", split_axis=0, concat_axis=0, tiled=True)
    halos = (from_even, from_odd, exchange(col_even, "by", 0), exchange(col_odd, "by", 1))
    parcels = parcel(from_even, from_odd, row_even, row_odd, part, terms, ocean, depth, tops)
    got = lax.all_to_all(parcels, "by", split_axis=0, concat_axis=0, tiled=True)
    return advect(tracers, velocity, ocean, *halos), solve(got)


def solution(mesh):
    return jax.shard_map(
        shards,
        mesh=mesh,
        in_specs=(
            P(None, None, "bx", "by"),
            P(None, None, "bx", "by"),
            P("bx", "by"),
            P(),
            P("bx", "by"),
        ),
        out_specs=(P(None, None, "bx", "by"), P(("bx", "by"), None)),
        check_vma=False,
    )
```

time: 50.1 us -> 69.4 us (1.39)
  blocking collectives: 0 us -> 14.9 us
  Pallas kernels: 22.1 us -> 30.8 us
  starting transfers between devices: 21.1 us -> 14.5 us
  waiting for transfers between devices: 2.5 us -> 4.47 us
    all_to_all x0 -> x1, blocking collectives: none -> 14.9 us  [shards(): tops = lax.all_to_all(top, 'bx', split_axis=0, concat_axis=0, tiled=True)]
    pallas_call x5 -> x4, Pallas kernels: 22.1 us -> 30.8 us  [the longest x1 19.2 us: advect(): pl.pallas_call(advect_kernel, in_specs=[HBM] * 3 + [ANY] * 4, out_specs=H...]
    all_to_all x2 -> x1, starting transfers between devices: 13.2 us -> 7.99 us  [shards(): got = lax.all_to_all(parcels, 'by', split_axis=0, concat_axis=0, tiled=True)]
    ppermute x4, waiting for transfers between devices: 0.01 us -> 4.47 us  [exchange(): return lax.ppermute(x, axis, pairs)]
    all_to_all x2 -> x1, waiting for transfers between devices: 2.49 us -> 0.01 us  [shards(): got = lax.all_to_all(parcels, 'by', split_axis=0, concat_axis=0, tiled=True)]
    ppermute x4, starting transfers between devices: 7.86 us -> 6.54 us  [exchange(): return lax.ppermute(x, axis, pairs)]
    unnamed x14 -> x12, local copies, waits for them, and re-layouts: 3.21 us -> 3.53 us
  transfers between devices with their start and end apart: 6 -> 5, of which waited for: 1 -> 1; matrix products, arithmetic and copies ran while one was open for 0% -> 0% of each run, Pallas kernels for 26% -> 28%
where the time goes in v6:
time: 69.4 us; the launch traced here: 69 us
  Pallas kernels  30.8 us (44%)
  blocking collectives  14.9 us (21%)
  starting transfers between devices  14.5 us (21%)
  waiting for transfers between devices  4.47 us (6%)
  local copies, waits for them, and re-layouts  3.53 us (5%)
  between operations  0.73 us (1%)
    pallas_call x1, Pallas kernels, advect(): pl.pallas_call(advect_kernel, in_specs=[HBM] * 3 + [ANY] * 4, out_specs=H...  19.2 us
    all_to_all x1, blocking collectives, shards(): tops = lax.all_to_all(top, 'bx', split_axis=0, concat_axis=0, tiled=True)  14.9 us
    all_to_all x1, starting transfers between devices, shards(): got = lax.all_to_all(parcels, 'by', split_axis=0, concat_axis=0, tiled=True)  7.99 us
    ppermute x4, starting transfers between devices, exchange(): return lax.ppermute(x, axis, pairs)  6.54 us
    pallas_call x1, Pallas kernels, pack(): pl.pallas_call(pack_kernel, in_specs=[HBM] * 5, out_specs=[VMEM] * 7, out...  6.49 us
    ppermute x4, waiting for transfers between devices, exchange(): return lax.ppermute(x, axis, pairs)  4.47 us
    unnamed x12, local copies, waits for them, and re-layouts  3.53 us
    pallas_call x1, Pallas kernels, solve(): pl.pallas_call(solve_kernel, in_specs=[VMEM], out_specs=VMEM, out_shape=f...  3 us
  transfers between devices with their start and end apart: 5, of which 1 were waited for; matrix products, arithmetic and copies ran while one was open for 0% of the time, Pallas kernels for 28%

profile of v6, /device:TPU:1, one launch (start us, length us, event | category | flops | bytes accessed | tf_op | source)
XLA Modules:
  0.0 69.0 jit_solution(849066944711570468)
XLA Ops:
  0.6 0.0 copy-start
  0.6 0.0 copy-start.1
  0.7 6.5 %pack_edges.1 = (f32[96,256]{1,0:T(8,128)}, f32[96,256]{1,0:T(8,128)}, f32[128,128]{1,0:T(8,128)}, f32[128,128]{1,0:T(8,128)}, f32[16,8,128]{2,1,0:T(8,128)}, /*index=5*/f32[128,256]{1,0:T(8,128)}, f32[128,128]{1,0:T(8,128)}) custom-call(f32[12]{0:T(128)} %thick_hbm.1, f32[4,12,128,256]{3,2,1,0:T(8,128)} %t_hbm.3, f32[2,12,128,256]{3,2,1,0:T(8,128)} %v_hbm.3, ...), custom_call_target="tpu_custom_call" | custom-call | flops 20000000 | bytes 9400000 | tf_op jit(solution)/shard_map/pack_edges/pallas_call | solution.py:191
  7.1 2.2 %collective-permute-start = (f32[96,256]{1,0:T(8,128)}, f32[96,256]{1,0:T(8,128)S(1)}, u32[]{:S(2)}, u32[]{:S(2)}) collective-permute-start(f32[96,256]{1,0:T(8,128)} %get-tuple-element.9.own_even_hbm), channel_id=1, source_target_pairs={{0,8},{8,0},{16,24},{24,16},{32,40},{40,32},{48,56},{56,48},{64,72... | collective-permute-start | bytes 294920 | tf_op jit(solution)/shard_map/ppermute | solution.py:493
  9.4 0.7 collective-permute-start.1
  10.0 14.9 %all_to_all.10.tops_hbm = f32[16,8,128]{2,1,0:T(8,128)S(1)} all-to-all(f32[16,8,128]{2,1,0:T(8,128)} %get-tuple-element.15), channel_id=1, replica_groups=mesh['bx'=16,'by'=8] {'bx'}, dimensions={0} | all-to-all | bytes 131072 | tf_op jit(solution)/shard_map/all_to_all | solution.py:499
  24.9 0.0 collective-permute-done.row_even.even_hbm
  24.9 0.0 collective-permute-done.1.row_odd.odd_hbm
  24.9 0.0 copy-done
  24.9 0.0 copy-done.1
  25.0 0.0 copy-start.2
  25.0 0.9 %copy-done.2 = f32[128,256]{1,0:T(8,128)S(1)} copy-done((f32[128,256]{1,0:T(8,128)S(1)}, f32[128,256]{1,0:T(8,128)}, u32[]{:S(2)}) %copy-start.2) | copy-done | bytes 131096
  25.9 0.0 copy-start.3
  25.9 0.9 %copy-done.3 = f32[96,256]{1,0:T(8,128)S(1)} copy-done((f32[96,256]{1,0:T(8,128)S(1)}, f32[96,256]{1,0:T(8,128)}, u32[]{:S(2)}) %copy-start.3) | copy-done | bytes 98328
  26.8 0.0 copy-start.4
  26.8 0.9 %copy-done.4 = f32[96,256]{1,0:T(8,128)S(1)} copy-done((f32[96,256]{1,0:T(8,128)S(1)}, f32[96,256]{1,0:T(8,128)}, u32[]{:S(2)}) %copy-start.4) | copy-done | bytes 98328
  27.6 0.0 copy-start.5
  27.7 0.8 %copy-done.5 = f32[128,128]{1,0:T(8,128)S(1)} copy-done((f32[128,128]{1,0:T(8,128)S(1)}, f32[128,128]{1,0:T(8,128)}, u32[]{:S(2)}) %copy-start.5) | copy-done | bytes 65560
  28.5 2.1 %parcels.1 = f32[8,56,256]{2,1,0:T(8,128)} custom-call(f32[96,256]{1,0:T(8,128)S(1)} %collective-permute-done.row_even.even_hbm, f32[96,256]{1,0:T(8,128)S(1)} %collective-permute-done.1.row_odd.odd_hbm, f32[96,256]{1,0:T(8,128)S(1)} %copy-done.3, f32[96,256]{1,0:T(8,128)S(1)} %copy-done.4, f32[128,256]{1,0:T(8,128)S(1)} %copy-done.2, ...), custom_call_target="tpu_custom_call" | custom-call | flops 1000000 | bytes 1500000 | tf_op jit(solution)/shard_map/parcels/pallas_call | solution.py:270
  30.6 8.0 %all-to-all-start.1 = ((f32[8,56,256]{2,1,0:T(8,128)}), f32[8,56,256]{2,1,0:T(8,128)S(1)}, u32[]{:S(2)}, u32[]{:S(2)}) async-start(f32[8,56,256]{2,1,0:T(8,128)} %parcels.1), calls=%async_computation.1 | async-start | bytes 917504 | tf_op jit(solution)/shard_map/all_to_all | solution.py:502
  38.6 0.0 collective-permute-start.2
  38.6 3.7 %collective-permute-start.3 = (f32[128,128]{1,0:T(8,128)}, f32[128,128]{1,0:T(8,128)S(1)}, u32[]{:S(2)}, u32[]{:S(2)}) collective-permute-start(f32[128,128]{1,0:T(8,128)} %get-tuple-element.12), channel_id=1, source_target_pairs={{1,2},{2,1},{3,4},{4,3},{5,6},{6,5},{9,10},{10,9},{11,12},{12,11},... | collective-permute-start | bytes 196616 | tf_op jit(solution)/shard_map/ppermute | solution.py:493
  42.3 0.0 collective-permute-done.2.col_even
  42.3 4.5 %collective-permute-done.3.col_odd = f32[128,128]{1,0:T(8,128)S(1)} collective-permute-done((f32[128,128]{1,0:T(8,128)}, f32[128,128]{1,0:T(8,128)S(1)}, u32[]{:S(2)}, u32[]{:S(2)}) %collective-permute-start.3) | collective-permute-done | bytes 65568 | tf_op jit(solution)/shard_map/ppermute | solution.py:493
  46.8 19.2 %advect.1 = f32[4,12,128,256]{3,2,1,0:T(8,128)} custom-call(f32[4,12,128,256]{3,2,1,0:T(8,128)} %t_hbm.3, f32[2,12,128,256]{3,2,1,0:T(8,128)} %v_hbm.3, s32[128,256]{1,0:T(8,128)S(1)} %copy-done, f32[96,256]{1,0:T(8,128)S(1)} %collective-permute-done.row_even.even_hbm, f32[96,256]{1,0:T(8,128)S(1)} %collective-permute-done.1.row_odd.odd_hbm, ...), custom_call_target="tpu_custom_call" | custom-call | flops 40000000 | bytes 15800000 | tf_op jit(solution)/shard_map/advect/pallas_call | solution.py:386
  66.0 0.0 all-to-all-done.1.got_ref
  66.0 3.0 %chebyshev.1 = f32[16,2048]{1,0:T(8,128)} custom-call(f32[8,56,256]{2,1,0:T(8,128)S(1)} %all-to-all-done.1.got_ref), custom_call_target="tpu_custom_call" | custom-call | flops 6000000 | bytes 600000 | tf_op jit(solution)/shard_map/chebyshev/pallas_call | solution.py:472
Async XLA Ops:
  0.6 24.3 %copy-start = (s32[128,256]{1,0:T(8,128)S(1)}, s32[128,256]{1,0:T(8,128)}, u32[]{:S(2)}) copy-start(s32[128,256]{1,0:T(8,128)} %ocean_hbm.5) | copy-start | bytes 393220
  0.6 24.3 %copy-start.1 = (f32[128,256]{1,0:T(8,128)S(1)}, f32[128,256]{1,0:T(8,128)}, u32[]{:S(2)}) copy-start(f32[128,256]{1,0:T(8,128)} %depth_hbm.3) | copy-start | bytes 393220
  7.1 17.8 %collective-permute-start = (f32[96,256]{1,0:T(8,128)}, f32[96,256]{1,0:T(8,128)S(1)}, u32[]{:S(2)}, u32[]{:S(2)}) collective-permute-start(f32[96,256]{1,0:T(8,128)} %get-tuple-element.9.own_even_hbm), channel_id=1, source_target_pairs={{0,8},{8,0},{16,24},{24,16},{32,40},{40,32},{48,56},{56,48},{64,72... | collective-permute-start | bytes 294920 | tf_op jit(solution)/shard_map/ppermute | solution.py:493
  9.4 15.6 %collective-permute-start.1 = (f32[96,256]{1,0:T(8,128)}, f32[96,256]{1,0:T(8,128)S(1)}, u32[]{:S(2)}, u32[]{:S(2)}) collective-permute-start(f32[96,256]{1,0:T(8,128)} %get-tuple-element.10.own_odd_hbm), channel_id=1, source_target_pairs={{8,16},{16,8},{24,32},{32,24},{40,48},{48,40},{56,64},{64,56},{72,... | collective-permute-start | bytes 294920 | tf_op jit(solution)/shard_map/ppermute | solution.py:493
  25.0 0.9 %copy-start.2 = (f32[128,256]{1,0:T(8,128)S(1)}, f32[128,256]{1,0:T(8,128)}, u32[]{:S(2)}) copy-start(f32[128,256]{1,0:T(8,128)} %get-tuple-element.13.part_hbm) | copy-start | bytes 393220
  25.9 0.9 %copy-start.3 = (f32[96,256]{1,0:T(8,128)S(1)}, f32[96,256]{1,0:T(8,128)}, u32[]{:S(2)}) copy-start(f32[96,256]{1,0:T(8,128)} %get-tuple-element.9.own_even_hbm) | copy-start | bytes 294916
  26.8 0.9 %copy-start.4 = (f32[96,256]{1,0:T(8,128)S(1)}, f32[96,256]{1,0:T(8,128)}, u32[]{:S(2)}) copy-start(f32[96,256]{1,0:T(8,128)} %get-tuple-element.10.own_odd_hbm) | copy-start | bytes 294916
  27.6 0.8 %copy-start.5 = (f32[128,128]{1,0:T(8,128)S(1)}, f32[128,128]{1,0:T(8,128)}, u32[]{:S(2)}) copy-start(f32[128,128]{1,0:T(8,128)} %get-tuple-element.14.terms_hbm) | copy-start | bytes 196612
  30.6 35.4 %all-to-all-start.1 = ((f32[8,56,256]{2,1,0:T(8,128)}), f32[8,56,256]{2,1,0:T(8,128)S(1)}, u32[]{:S(2)}, u32[]{:S(2)}) async-start(f32[8,56,256]{2,1,0:T(8,128)} %parcels.1), calls=%async_computation.1 | async-start | bytes 917504 | tf_op jit(solution)/shard_map/all_to_all | solution.py:502
  38.6 3.7 %collective-permute-start.2 = (f32[128,128]{1,0:T(8,128)}, f32[128,128]{1,0:T(8,128)S(1)}, u32[]{:S(2)}, u32[]{:S(2)}) collective-permute-start(f32[128,128]{1,0:T(8,128)} %get-tuple-element.11), channel_id=1, source_target_pairs={{0,1},{1,0},{2,3},{3,2},{4,5},{5,4},{6,7},{7,6},{8,9},{9,8},{10,11... | collective-permute-start | bytes 196616 | tf_op jit(solution)/shard_map/ppermute | solution.py:493
  38.6 8.2 %collective-permute-start.3 = (f32[128,128]{1,0:T(8,128)}, f32[128,128]{1,0:T(8,128)S(1)}, u32[]{:S(2)}, u32[]{:S(2)}) collective-permute-start(f32[128,128]{1,0:T(8,128)} %get-tuple-element.12), channel_id=1, source_target_pairs={{1,2},{2,1},{3,4},{4,3},{5,6},{6,5},{9,10},{10,9},{11,12},{12,11},... | collective-permute-start | bytes 196616 | tf_op jit(solution)/shard_map/ppermute | solution.py:493

commit v7 on v6

--- a/solution.py
+++ b/solution.py
@@ -212,7 +212,7 @@
     )(thickness, tracers, velocity, ocean, depth)
 
 
-def parcel_kernel(even_hbm, odd_hbm, own_even_hbm, own_odd_hbm, part_hbm, terms_hbm, ocean_hbm, depth_hbm, tops_hbm, send_ref,
+def parcel_kernel(even_hbm, odd_hbm, own_even_hbm, own_odd_hbm, part_hbm, terms_hbm, ocean_hbm, depth_hbm, tops_hbm, _, __, send_ref,
                   rows_in, rows_out, part, terms, ocean_ref, depth_ref, tops, ext, ext_terms, sems):
     odd_x = lax.axis_index("bx") % 2
     copies = [
@@ -265,11 +265,11 @@
             send_ref[j, 44:56, half * LANE : (half + 1) * LANE] = jnp.where(lanes((12, LANE)) == MOST, most, value)
 
 
-def parcel(even, odd, own_even, own_odd, part, terms, ocean, depth, tops):
+def parcel(even, odd, own_even, own_odd, part, terms, ocean, depth, tops, col_even, col_odd):
     block = pltpu.VMEM((ROWS, COLS), jnp.float32)
     return pl.pallas_call(
         parcel_kernel,
-        in_specs=[ANY] * 9,
+        in_specs=[ANY] * 11,
         out_specs=VMEM,
         out_shape=f32(8, 56, COLS),
         scratch_shapes=[
@@ -284,10 +284,10 @@
             pltpu.VMEM((ROWS + 8, LANE), jnp.float32),
             pltpu.SemaphoreType.DMA((9,)),
         ],
-        compiler_params=pltpu.CompilerParams(vmem_limit_bytes=53 * 2**20),
+        compiler_params=pltpu.CompilerParams(vmem_limit_bytes=60 * 2**20),
         cost_estimate=pl.CostEstimate(flops=1_000_000, bytes_accessed=1_500_000, transcendentals=0),
         name="parcels",
-    )(even, odd, own_even, own_odd, part, terms, ocean, depth, tops)
+    )(even, odd, own_even, own_odd, part, terms, ocean, depth, tops, col_even, col_odd)
 
 
 def ahead_y(x, edge):
@@ -322,13 +322,13 @@
     small = [pltpu.make_async_copy(a, b, small_sems.at[i]) for i, (a, b) in enumerate(small)]
 
     def tracers_in(k):
-        return pltpu.make_async_copy(t_hbm.at[:, k], t_ref.at[:, k], sems.at[0, k])
+        return pltpu.make_async_copy(t_hbm.at[:, k], t_ref.at[k], sems.at[0, k])
 
     def velocity_in(k):
-        return pltpu.make_async_copy(v_hbm.at[:, k], v_ref.at[:, k], sems.at[1, k])
+        return pltpu.make_async_copy(v_hbm.at[:, k], v_ref.at[k], sems.at[1, k])
 
     def tracers_out(k):
-        return pltpu.make_async_copy(out_ref.at[:, k], out_hbm.at[:, k], sems.at[2, k])
+        return pltpu.make_async_copy(out_ref.at[k], out_hbm.at[:, k], sems.at[2, k])
 
     for copy in small:
         copy.start()
@@ -344,7 +344,7 @@
         edge = jnp.where(even, cols_in[0, rows, :], cols_in[1, rows, :])
         for k in range(LEVELS):
             for i in range(TRACERS + 1):
-                edges[i, k, rows, :] = pltpu.roll(edge, (LANE - 2 * (i * LEVELS + k)) % LANE, 1)
+                edges[k, i, rows, :] = pltpu.roll(edge, (LANE - 2 * (i * LEVELS + k)) % LANE, 1)
         here = load_wet(8 * r)
         wet_edge = pltpu.roll(edge, LANE - 2 * WET, 1)
         w_x[rows, :] = here * above(load_wet, row_hi[WET : WET + 1, :], r)
@@ -356,23 +356,29 @@
         tracers_in(k).wait()
         velocity_in(k).wait()
         u_before = row_lo[pl.ds(SPEED + k, 1), :] * w_before
-        carry = [upwind(u_before, row_lo[pl.ds(t * LEVELS + k, 1), :], t_ref[t, k, 0:1, :]) for t in range(TRACERS)]
-        for r in range(ROWS // TALL):
-            rows = pl.ds(TALL * r, TALL)
-            u = v_ref[0, k, rows, :] * w_x[rows, :]
-            v = v_ref[1, k, rows, :] * w_y[rows, :]
-            v_before = edges[TRACERS, k, rows, :] * before_y[rows, :]
-            for t in range(TRACERS):
-                load = lambda at: t_ref[t, k, at : at + TALL, :]
-                c = load(TALL * r)
-                c_edge = edges[t, k, rows, :]
-                here_x = upwind(u, c, above(load, row_hi[pl.ds(t * LEVELS + k, 1), :], r, TALL))
-                turned = pltpu.roll(here_x, 1, 0)
-                past_x = jnp.where(sublanes((TALL, COLS)) == 0, carry[t], turned)
-                carry[t] = turned[0:1, :]
-                here_y = upwind(v, c, ahead_y(c, c_edge))
-                past_y = behind_y(here_y, upwind(v_before, c_edge, c[:, :LANE]))
-                out_ref[t, k, rows, :] = (c - (here_x - past_x)) - (here_y - past_y)
+
+        def pair(p, _):
+            tracers = [2 * p, 2 * p + 1]
+            carry = [upwind(u_before, row_lo[pl.ds(t * LEVELS + k, 1), :], t_ref[k, t, 0:1, :]) for t in tracers]
+            for r in range(ROWS // TALL):
+                rows = pl.ds(TALL * r, TALL)
+                u = v_ref[k, 0, rows, :] * w_x[rows, :]
+                v = v_ref[k, 1, rows, :] * w_y[rows, :]
+                v_before = edges[k, TRACERS, rows, :] * before_y[rows, :]
+                for i, t in enumerate(tracers):
+                    load = lambda at: t_ref[k, t, at : at + TALL, :]
+                    c = load(TALL * r)
+                    c_edge = edges[k, t, rows, :]
+                    here_x = upwind(u, c, above(load, row_hi[pl.ds(t * LEVELS + k, 1), :], r, TALL))
+                    turned = pltpu.roll(here_x, 1, 0)
+                    past_x = jnp.where(sublanes((TALL, COLS)) == 0, carry[i], turned)
+                    carry[i] = turned[0:1, :]
+                    here_y = upwind(v, c, ahead_y(c, c_edge))
+                    past_y = behind_y(here_y, upwind(v_before, c_edge, c[:, :LANE]))
+                    out_ref[k, t, rows, :] = (c - (here_x - past_x)) - (here_y - past_y)
+            return 0
+
+        lax.fori_loop(0, 2, pair, 0)
         tracers_out(k).start()
         return 0
 
@@ -389,20 +395,20 @@
         out_specs=HBM,
         out_shape=f32(TRACERS, LEVELS, ROWS, COLS),
         scratch_shapes=[
-            pltpu.VMEM((TRACERS, LEVELS, ROWS, COLS), jnp.float32),
-            pltpu.VMEM((2, LEVELS, ROWS, COLS), jnp.float32),
-            pltpu.VMEM((TRACERS, LEVELS, ROWS, COLS), jnp.float32),
+            pltpu.VMEM((LEVELS, TRACERS, ROWS, COLS), jnp.float32),
+            pltpu.VMEM((LEVELS, 2, ROWS, COLS), jnp.float32),
+            pltpu.VMEM((LEVELS, TRACERS, ROWS, COLS), jnp.float32),
             pltpu.VMEM((ROWS, COLS), jnp.int32),
             pltpu.VMEM((2, MESSAGE, COLS), jnp.float32),
             pltpu.VMEM((2, ROWS, LANE), jnp.float32),
             block,
             block,
             pltpu.VMEM((ROWS, LANE), jnp.float32),
-            pltpu.VMEM((TRACERS + 1, LEVELS, ROWS, LANE), jnp.float32),
+            pltpu.VMEM((LEVELS, TRACERS + 1, ROWS, LANE), jnp.float32),
             pltpu.SemaphoreType.DMA((3, LEVELS)),
             pltpu.SemaphoreType.DMA((5,)),
         ],
-        compiler_params=pltpu.CompilerParams(vmem_limit_bytes=52 * 2**20),
+        compiler_params=pltpu.CompilerParams(vmem_limit_bytes=60 * 2**20),
         cost_estimate=pl.CostEstimate(flops=40_000_000, bytes_accessed=15_800_000, transcendentals=0),
         name="advect",
     )(tracers, velocity, ocean, row_even, row_odd, col_even, col_odd)
@@ -479,7 +485,7 @@
             pltpu.VMEM((EXT, WIDE), jnp.float32),
             pltpu.VMEM((8, EXT, WIDE), jnp.float32),
         ],
-        compiler_params=pltpu.CompilerParams(vmem_limit_bytes=12 * 2**20),
+        compiler_params=pltpu.CompilerParams(vmem_limit_bytes=60 * 2**20),
         cost_estimate=pl.CostEstimate(flops=6_000_000, bytes_accessed=600_000, transcendentals=0),
         name="chebyshev",
     )(got)
@@ -498,7 +504,7 @@
     from_even, from_odd = exchange(row_even, "bx", 0), exchange(row_odd, "bx", 1)
     tops = lax.all_to_all(top, "bx", split_axis=0, concat_axis=0, tiled=True)
     halos = (from_even, from_odd, exchange(col_even, "by", 0), exchange(col_odd, "by", 1))
-    parcels = parcel(from_even, from_odd, row_even, row_odd, part, terms, ocean, depth, tops)
+    parcels = parcel(from_even, from_odd, row_even, row_odd, part, terms, ocean, depth, tops, *halos[2:])
     got = lax.all_to_all(parcels, "by", split_axis=0, concat_axis=0, tiled=True)
     return advect(tracers, velocity, ocean, *halos), solve(got)
 

time: 69.4 us -> 56.2 us (0.81)
  Pallas kernels: 30.8 us -> 25.3 us
  waiting for transfers between devices: 4.47 us -> 0.01 us
  local copies, waits for them, and re-layouts: 3.53 us -> 1.43 us
  starting transfers between devices: 14.5 us -> 13.1 us
    pallas_call x1, Pallas kernels: 19.2 us -> 12.6 us  [advect(): pl.pallas_call(advect_kernel, in_specs=[HBM] * 3 + [ANY] * 4, out_specs=H...]
    ppermute x4, waiting for transfers between devices: 4.47 us -> 0.01 us  [exchange(): return lax.ppermute(x, axis, pairs)]
    all_to_all x1, starting transfers between devices: 7.99 us -> 5.72 us  [shards(): got = lax.all_to_all(parcels, 'by', split_axis=0, concat_axis=0, tiled=True)]
    unnamed x12 -> x10, local copies, waits for them, and re-layouts: 3.53 us -> 1.43 us
    pallas_call x1, Pallas kernels: 3 us -> 4.02 us  [solve(): pl.pallas_call(solve_kernel, in_specs=[VMEM], out_specs=VMEM, out_shape=f...]
    ppermute x4, starting transfers between devices: 6.54 us -> 7.34 us  [exchange(): return lax.ppermute(x, axis, pairs)]
  transfers between devices with their start and end apart: 5 -> 5, of which waited for: 1 -> 0; matrix products, arithmetic and copies ran while one was open for 0% -> 0% of each run, Pallas kernels for 28% -> 23%
where the time goes in v7:
time: 56.2 us; the launch traced here: 55.8 us
  Pallas kernels  25.3 us (45%)
  blocking collectives  15.3 us (27%)
  starting transfers between devices  13.1 us (23%)
  local copies, waits for them, and re-layouts  1.43 us (3%)
  between operations  0.73 us (1%)
    all_to_all x1, blocking collectives, shards(): tops = lax.all_to_all(top, 'bx', split_axis=0, concat_axis=0, tiled=True)  15.3 us
    pallas_call x1, Pallas kernels, advect(): pl.pallas_call(advect_kernel, in_specs=[HBM] * 3 + [ANY] * 4, out_specs=H...  12.6 us
    ppermute x4, starting transfers between devices, exchange(): return lax.ppermute(x, axis, pairs)  7.34 us
    pallas_call x1, Pallas kernels, pack(): pl.pallas_call(pack_kernel, in_specs=[HBM] * 5, out_specs=[VMEM] * 7, out...  6.47 us
    all_to_all x1, starting transfers between devices, shards(): got = lax.all_to_all(parcels, 'by', split_axis=0, concat_axis=0, tiled=True)  5.72 us
    pallas_call x1, Pallas kernels, solve(): pl.pallas_call(solve_kernel, in_specs=[VMEM], out_specs=VMEM, out_shape=f...  4.02 us
    pallas_call x1, Pallas kernels, parcel(): pl.pallas_call(parcel_kernel, in_specs=[ANY] * 11, out_specs=VMEM, out_sh...  2.17 us
    unnamed x10, local copies, waits for them, and re-layouts  1.43 us
  transfers between devices with their start and end apart: 5, of which 0 were waited for; matrix products, arithmetic and copies ran while one was open for 0% of the time, Pallas kernels for 23%

profile of v7, /device:TPU:1, one launch (start us, length us, event | category | flops | bytes accessed | tf_op | source)
XLA Modules:
  0.0 55.8 jit_solution(9893649726812073440)
XLA Ops:
  0.6 6.5 %pack_edges.1 = (f32[96,256]{1,0:T(8,128)}, f32[96,256]{1,0:T(8,128)}, f32[128,128]{1,0:T(8,128)}, f32[128,128]{1,0:T(8,128)}, f32[16,8,128]{2,1,0:T(8,128)}, /*index=5*/f32[128,256]{1,0:T(8,128)}, f32[128,128]{1,0:T(8,128)}) custom-call(f32[12]{0:T(128)} %thick_hbm.1, f32[4,12,128,256]{3,2,1,0:T(8,128)} %t_hbm.3, f32[2,12,128,256]{3,2,1,0:T(8,128)} %v_hbm.3, ...), custom_call_target="tpu_custom_call" | custom-call | flops 20000000 | bytes 9400000 | tf_op jit(solution)/shard_map/pack_edges/pallas_call | solution.py:191
  7.1 2.2 %collective-permute-start = (f32[96,256]{1,0:T(8,128)}, f32[96,256]{1,0:T(8,128)S(1)}, u32[]{:S(2)}, u32[]{:S(2)}) collective-permute-start(f32[96,256]{1,0:T(8,128)} %get-tuple-element.9.own_even_hbm), channel_id=1, source_target_pairs={{0,8},{8,0},{16,24},{24,16},{32,40},{40,32},{48,56},{56,48},{64,72... | collective-permute-start | bytes 294920 | tf_op jit(solution)/shard_map/ppermute | solution.py:499
  9.3 0.7 %collective-permute-start.1 = (f32[96,256]{1,0:T(8,128)}, f32[96,256]{1,0:T(8,128)S(1)}, u32[]{:S(2)}, u32[]{:S(2)}) collective-permute-start(f32[96,256]{1,0:T(8,128)} %get-tuple-element.10.own_odd_hbm), channel_id=1, source_target_pairs={{8,16},{16,8},{24,32},{32,24},{40,48},{48,40},{56,64},{64,56},{72,... | collective-permute-start | bytes 294920 | tf_op jit(solution)/shard_map/ppermute | solution.py:499
  10.0 1.0 %collective-permute-start.2 = (f32[128,128]{1,0:T(8,128)}, f32[128,128]{1,0:T(8,128)S(1)}, u32[]{:S(2)}, u32[]{:S(2)}) collective-permute-start(f32[128,128]{1,0:T(8,128)} %get-tuple-element.11), channel_id=1, source_target_pairs={{0,1},{1,0},{2,3},{3,2},{4,5},{5,4},{6,7},{7,6},{8,9},{9,8},{10,11... | collective-permute-start | bytes 196616 | tf_op jit(solution)/shard_map/ppermute | solution.py:499
  11.0 3.4 %collective-permute-start.3 = (f32[128,128]{1,0:T(8,128)}, f32[128,128]{1,0:T(8,128)S(1)}, u32[]{:S(2)}, u32[]{:S(2)}) collective-permute-start(f32[128,128]{1,0:T(8,128)} %get-tuple-element.12), channel_id=1, source_target_pairs={{1,2},{2,1},{3,4},{4,3},{5,6},{6,5},{9,10},{10,9},{11,12},{12,11},... | collective-permute-start | bytes 196616 | tf_op jit(solution)/shard_map/ppermute | solution.py:499
  14.5 15.3 %all_to_all.10.tops_hbm = f32[16,8,128]{2,1,0:T(8,128)} all-to-all(f32[16,8,128]{2,1,0:T(8,128)} %get-tuple-element.15), channel_id=1, replica_groups=mesh['bx'=16,'by'=8] {'bx'}, dimensions={0} | all-to-all | bytes 131072 | tf_op jit(solution)/shard_map/all_to_all | solution.py:505
  29.8 0.0 collective-permute-done.2.col_even._
  29.8 0.0 copy-start.3
  29.8 0.0 collective-permute-done.3.col_odd.__
  29.8 0.0 copy-start.4
  29.8 0.0 collective-permute-done.row_even.even_hbm
  29.8 0.0 copy-start.1
  29.8 0.0 collective-permute-done.1.row_odd.odd_hbm
  29.8 0.0 copy-start.2
  29.8 0.6 %copy-done.3 = f32[128,128]{1,0:T(8,128)} copy-done((f32[128,128]{1,0:T(8,128)}, f32[128,128]{1,0:T(8,128)S(1)}, u32[]{:S(2)}) %copy-start.3) | copy-done | bytes 65560
  30.4 0.0 copy-done.4
  30.4 0.0 copy-done.1
  30.5 0.0 copy-done.2
  30.5 2.2 %parcels.1 = f32[8,56,256]{2,1,0:T(8,128)} custom-call(f32[96,256]{1,0:T(8,128)} %copy-done.1, f32[96,256]{1,0:T(8,128)} %copy-done.2, f32[96,256]{1,0:T(8,128)} %get-tuple-element.9.own_even_hbm, f32[96,256]{1,0:T(8,128)} %get-tuple-element.10.own_odd_hbm, f32[128,256]{1,0:T(8,128)} %get-tuple-element.13.part_hbm, f32[128,128]{1,0:T(8,128)} %get-tuple-element.14.terms_hbm, ...), custom_call_target="tpu_custom_call" | custom-call | flops 1000000 | bytes 1500000 | tf_op jit(solution)/shard_map/parcels/pallas_call | solution.py:270
  32.7 5.7 %all-to-all-start.1 = ((f32[8,56,256]{2,1,0:T(8,128)}), f32[8,56,256]{2,1,0:T(8,128)S(1)}, u32[]{:S(2)}, u32[]{:S(2)}) async-start(f32[8,56,256]{2,1,0:T(8,128)} %parcels.1), calls=%async_computation.1 | async-start | bytes 917504 | tf_op jit(solution)/shard_map/all_to_all | solution.py:508
  38.4 12.6 %advect.1 = f32[4,12,128,256]{3,2,1,0:T(8,128)} custom-call(f32[4,12,128,256]{3,2,1,0:T(8,128)} %t_hbm.3, f32[2,12,128,256]{3,2,1,0:T(8,128)} %v_hbm.3, s32[128,256]{1,0:T(8,128)} %ocean_hbm.5, f32[96,256]{1,0:T(8,128)} %copy-done.1, f32[96,256]{1,0:T(8,128)} %copy-done.2, f32[128,128]{1,0:T(8,128)} %copy-done.3, f32[128,128]{1,0:T(8,128)} %copy-done.4), custom_call_target="tpu_custom_call" | custom-call | flops 40000000 | bytes 15800000 | tf_op jit(solution)/shard_map/advect/pallas_call | solution.py:392
  51.0 0.0 all-to-all-done.1.got_ref
  51.0 0.0 copy-start
  51.1 0.8 %copy-done = f32[8,56,256]{2,1,0:T(8,128)} copy-done((f32[8,56,256]{2,1,0:T(8,128)}, f32[8,56,256]{2,1,0:T(8,128)S(1)}, u32[]{:S(2)}) %copy-start) | copy-done | bytes 458776
  51.8 4.0 %chebyshev.1 = f32[16,2048]{1,0:T(8,128)} custom-call(f32[8,56,256]{2,1,0:T(8,128)} %copy-done), custom_call_target="tpu_custom_call" | custom-call | flops 6000000 | bytes 600000 | tf_op jit(solution)/shard_map/chebyshev/pallas_call | solution.py:478
Async XLA Ops:
  7.1 22.7 %collective-permute-start = (f32[96,256]{1,0:T(8,128)}, f32[96,256]{1,0:T(8,128)S(1)}, u32[]{:S(2)}, u32[]{:S(2)}) collective-permute-start(f32[96,256]{1,0:T(8,128)} %get-tuple-element.9.own_even_hbm), channel_id=1, source_target_pairs={{0,8},{8,0},{16,24},{24,16},{32,40},{40,32},{48,56},{56,48},{64,72... | collective-permute-start | bytes 294920 | tf_op jit(solution)/shard_map/ppermute | solution.py:499
  9.3 20.5 %collective-permute-start.1 = (f32[96,256]{1,0:T(8,128)}, f32[96,256]{1,0:T(8,128)S(1)}, u32[]{:S(2)}, u32[]{:S(2)}) collective-permute-start(f32[96,256]{1,0:T(8,128)} %get-tuple-element.10.own_odd_hbm), channel_id=1, source_target_pairs={{8,16},{16,8},{24,32},{32,24},{40,48},{48,40},{56,64},{64,56},{72,... | collective-permute-start | bytes 294920 | tf_op jit(solution)/shard_map/ppermute | solution.py:499
  10.0 19.8 %collective-permute-start.2 = (f32[128,128]{1,0:T(8,128)}, f32[128,128]{1,0:T(8,128)S(1)}, u32[]{:S(2)}, u32[]{:S(2)}) collective-permute-start(f32[128,128]{1,0:T(8,128)} %get-tuple-element.11), channel_id=1, source_target_pairs={{0,1},{1,0},{2,3},{3,2},{4,5},{5,4},{6,7},{7,6},{8,9},{9,8},{10,11... | collective-permute-start | bytes 196616 | tf_op jit(solution)/shard_map/ppermute | solution.py:499
  11.0 18.8 %collective-permute-start.3 = (f32[128,128]{1,0:T(8,128)}, f32[128,128]{1,0:T(8,128)S(1)}, u32[]{:S(2)}, u32[]{:S(2)}) collective-permute-start(f32[128,128]{1,0:T(8,128)} %get-tuple-element.12), channel_id=1, source_target_pairs={{1,2},{2,1},{3,4},{4,3},{5,6},{6,5},{9,10},{10,9},{11,12},{12,11},... | collective-permute-start | bytes 196616 | tf_op jit(solution)/shard_map/ppermute | solution.py:499
  29.8 0.6 %copy-start.3 = (f32[128,128]{1,0:T(8,128)}, f32[128,128]{1,0:T(8,128)S(1)}, u32[]{:S(2)}) copy-start(f32[128,128]{1,0:T(8,128)S(1)} %collective-permute-done.2.col_even._) | copy-start | bytes 196612
  29.8 0.6 %copy-start.4 = (f32[128,128]{1,0:T(8,128)}, f32[128,128]{1,0:T(8,128)S(1)}, u32[]{:S(2)}) copy-start(f32[128,128]{1,0:T(8,128)S(1)} %collective-permute-done.3.col_odd.__) | copy-start | bytes 196612
  29.8 0.7 %copy-start.1 = (f32[96,256]{1,0:T(8,128)}, f32[96,256]{1,0:T(8,128)S(1)}, u32[]{:S(2)}) copy-start(f32[96,256]{1,0:T(8,128)S(1)} %collective-permute-done.row_even.even_hbm) | copy-start | bytes 294916
  29.8 0.7 %copy-start.2 = (f32[96,256]{1,0:T(8,128)}, f32[96,256]{1,0:T(8,128)S(1)}, u32[]{:S(2)}) copy-start(f32[96,256]{1,0:T(8,128)S(1)} %collective-permute-done.1.row_odd.odd_hbm) | copy-start | bytes 294916
  32.7 18.4 %all-to-all-start.1 = ((f32[8,56,256]{2,1,0:T(8,128)}), f32[8,56,256]{2,1,0:T(8,128)S(1)}, u32[]{:S(2)}, u32[]{:S(2)}) async-start(f32[8,56,256]{2,1,0:T(8,128)} %parcels.1), calls=%async_computation.1 | async-start | bytes 917504 | tf_op jit(solution)/shard_map/all_to_all | solution.py:508
  51.0 0.8 %copy-start = (f32[8,56,256]{2,1,0:T(8,128)}, f32[8,56,256]{2,1,0:T(8,128)S(1)}, u32[]{:S(2)}) copy-start(f32[8,56,256]{2,1,0:T(8,128)S(1)} %all-to-all-done.1.got_ref) | copy-start | bytes 1376260

commit v8 on v5

--- a/solution.py
+++ b/solution.py
@@ -18,8 +18,9 @@
 EXT = 24
 CHUNK = 32
 TALL = 16
-
-SPEED, WET, PART, COEF, EDGE, MESSAGE = 48, 60, 64, 68, 72, 80
+LIMA, LIMB = 48, 48
+
+SPEED, WET, THICK, PART, COEF, EDGE, MESSAGE = 48, 60, 61, 64, 68, 72, 80
 ANY = pl.BlockSpec(memory_space=pl.ANY)
 HBM = pl.BlockSpec(memory_space=pltpu.HBM)
 VMEM = pl.BlockSpec(memory_space=pltpu.VMEM)
@@ -114,6 +115,9 @@
     coef = coefficient(depth_ref[...], wet)
     most = jnp.max(jnp.max(coef, axis=0, keepdims=True), axis=1, keepdims=True)
     top[...] = jnp.broadcast_to(most[None], top.shape)
+    thick_lanes = jnp.zeros((1, COLS), jnp.float32)
+    for k in range(LEVELS):
+        thick_lanes = jnp.where(lanes((1, COLS)) == k, thick[k], thick_lanes)
 
     def gather(c, _):
         chunk_copy(c).wait()
@@ -151,7 +155,8 @@
         q = [0.2 * t_ref[0, k, rows, :] - 0.8 * t_ref[1, k, rows, :] for k in range(LEVELS)]
         speed_x = [u[k] for k in range(LEVELS)]
         speed_y = [v[k] for k in range(LEVELS)]
-        message[WET:PART, :] = jnp.broadcast_to(here[7:8, :] if keep else here[0:1, :], (PART - WET, COLS))
+        message[WET:THICK, :] = here[7:8, :] if keep else here[0:1, :]
+        message[THICK:PART, :] = jnp.broadcast_to(thick_lanes, (PART - THICK, COLS))
         message[PART:COEF, :] = edge_forcing(q, speed_x, speed_y, here, thick)[keep : keep + 4, :]
         message[COEF:EDGE, :] = coefficient(depth_ref[rows, :], here)[keep : keep + 4, :]
         message[EDGE:MESSAGE, :LANE] = edge_terms(q, speed_y, here, thick)
@@ -213,7 +218,7 @@
 
 def advect_kernel(first, *refs):
     if first == 0:
-        (thick_hbm, t_hbm, v_hbm, ocean_hbm, row_even, row_odd, col_even, col_odd, depth_hbm, out_hbm, send_ref,
+        (t_hbm, v_hbm, ocean_hbm, row_even, row_odd, col_even, col_odd, depth_hbm, out_hbm, send_ref,
          t_ref, v_ref, out_ref, ocean_ref, rows_in, cols_in, w_x, w_y, before_y, edges, sems, small_sems,
          depth_ref, total, flux, ext, thick) = refs
     else:
@@ -229,17 +234,17 @@
         (col_odd, cols_in.at[odd_y]),
     ]
     if first == 0:
-        small += [(depth_hbm, depth_ref), (thick_hbm, thick)]
+        small += [(depth_hbm, depth_ref)]
     small = [pltpu.make_async_copy(a, b, small_sems.at[i]) for i, (a, b) in enumerate(small)]
 
     def tracers_in(k):
-        return pltpu.make_async_copy(t_hbm.at[first : first + 2, k], t_ref.at[:, k], sems.at[0, k])
+        return pltpu.make_async_copy(t_hbm.at[first : first + 2, k], t_ref.at[k], sems.at[0, k])
 
     def velocity_in(k):
-        return pltpu.make_async_copy(v_hbm.at[:, k], v_ref.at[:, k], sems.at[1, k])
+        return pltpu.make_async_copy(v_hbm.at[:, k], v_ref.at[k], sems.at[1, k])
 
     def tracers_out(k):
-        return pltpu.make_async_copy(out_ref.at[:, k], out_hbm.at[first : first + 2, k], sems.at[2, k])
+        return pltpu.make_async_copy(out_ref.at[k], out_hbm.at[first : first + 2, k], sems.at[2, k])
 
     for copy in small:
         copy.start()
@@ -255,7 +260,7 @@
         edge = jnp.where(even, cols_in[0, rows, :], cols_in[1, rows, :])
         for k in range(LEVELS):
             for i, slot in enumerate((first * LEVELS + k, (first + 1) * LEVELS + k, SPEED + k)):
-                edges[i, k, rows, :] = pltpu.roll(edge, (LANE - 2 * slot) % LANE, 1)
+                edges[k, i, rows, :] = pltpu.roll(edge, (LANE - 2 * slot) % LANE, 1)
         here = load_wet(8 * r)
         wet_edge = pltpu.roll(edge, LANE - 2 * WET, 1)
         w_x[rows, :] = here * above(load_wet, row_hi[WET : WET + 1, :], r)
@@ -266,24 +271,29 @@
     w_before = load_wet(0)[0:1, :] * row_lo[WET : WET + 1, :]
     if first == 0:
         flux[...] = jnp.zeros((8, COLS), jnp.float32)
+        line = rows_in[1 - odd_x, THICK : THICK + 1, :]
+        for k in range(LEVELS):
+            thick[k : k + 1, :] = jnp.broadcast_to(line[:, k : k + 1], (1, COLS))
 
     def level(k, _):
         tracers_in(k).wait()
         velocity_in(k).wait()
         u_before = row_lo[pl.ds(SPEED + k, 1), :] * w_before
-        into_x = [upwind(u_before, row_lo[pl.ds((first + t) * LEVELS + k, 1), :], t_ref[t, k, 0:1, :]) for t in range(2)]
+        into_x = [upwind(u_before, row_lo[pl.ds((first + t) * LEVELS + k, 1), :], t_ref[k, t, 0:1, :]) for t in range(2)]
         carry, out_x = list(into_x), [None, None]
+        if first == 0:
+            depth = thick[pl.ds(k, 1), :]
         for r in range(ROWS // TALL):
             rows = pl.ds(TALL * r, TALL)
-            u = v_ref[0, k, rows, :] * w_x[rows, :]
-            v = v_ref[1, k, rows, :] * w_y[rows, :]
-            v_before = edges[2, k, rows, :] * before_y[rows, :]
+            u = v_ref[k, 0, rows, :] * w_x[rows, :]
+            v = v_ref[k, 1, rows, :] * w_y[rows, :]
+            v_before = edges[k, 2, rows, :] * before_y[rows, :]
             new = []
             for t in range(2):
-                load = lambda at: t_ref[t, k, at : at + TALL, :]
+                load = lambda at: t_ref[k, t, at : at + TALL, :]
                 slot = (first + t) * LEVELS + k
                 c = load(TALL * r)
-                c_edge = edges[t, k, rows, :]
+                c_edge = edges[k, t, rows, :]
                 here_x = upwind(u, c, above(load, row_hi[pl.ds(slot, 1), :], r, TALL))
                 turned = pltpu.roll(here_x, 1, 0)
                 past_x = jnp.where(sublanes((TALL, COLS)) == 0, carry[t], turned)
@@ -293,13 +303,13 @@
                 here_y = upwind(v, c, ahead_y(c, c_edge))
                 past_y = behind_y(here_y, upwind(v_before, c_edge, c[:, :LANE]))
                 value = (c - (here_x - past_x)) - (here_y - past_y)
-                out_ref[t, k, rows, :] = value
+                out_ref[k, t, rows, :] = value
                 new.append(value)
             if first == 0:
-                total[rows, :] = total[rows, :] + ((0.2 * thick[k]) * new[0] - (0.8 * thick[k]) * new[1])
+                total[rows, :] = total[rows, :] + depth * (0.2 * new[0] - 0.8 * new[1])
         if first == 0:
-            flux[0:1, :] = flux[0:1, :] + thick[k] * (0.2 * into_x[0] - 0.8 * into_x[1])
-            flux[1:2, :] = flux[1:2, :] + thick[k] * (0.2 * out_x[0] - 0.8 * out_x[1])
+            flux[0:1, :] = flux[0:1, :] + depth * (0.2 * into_x[0] - 0.8 * into_x[1])
+            flux[1:2, :] = flux[1:2, :] + depth * (0.2 * out_x[0] - 0.8 * out_x[1])
         tracers_out(k).start()
         return 0
 
@@ -339,24 +349,23 @@
     block = pltpu.VMEM((ROWS, COLS), jnp.float32)
     narrow = pltpu.VMEM((ROWS, LANE), jnp.float32)
     scratch = [
-        pltpu.VMEM((2, LEVELS, ROWS, COLS), jnp.float32),
-        pltpu.VMEM((2, LEVELS, ROWS, COLS), jnp.float32),
-        pltpu.VMEM((2, LEVELS, ROWS, COLS), jnp.float32),
+        pltpu.VMEM((LEVELS, 2, ROWS, COLS), jnp.float32),
+        pltpu.VMEM((LEVELS, 2, ROWS, COLS), jnp.float32),
+        pltpu.VMEM((LEVELS, 2, ROWS, COLS), jnp.float32),
         pltpu.VMEM((ROWS, COLS), jnp.int32),
         pltpu.VMEM((2, MESSAGE, COLS), jnp.float32),
         pltpu.VMEM((2, ROWS, LANE), jnp.float32),
         block,
         block,
         narrow,
-        pltpu.VMEM((3, LEVELS, ROWS, LANE), jnp.float32),
+        pltpu.VMEM((LEVELS, 3, ROWS, LANE), jnp.float32),
         pltpu.SemaphoreType.DMA((3, LEVELS)),
         pltpu.SemaphoreType.DMA((8,)),
     ]
     aliases = {}
     if first == 0:
-        thickness, depth = extra
-        ins = [HBM] + ins + [HBM]
-        operands = [thickness] + operands + [depth]
+        ins = ins + [HBM]
+        operands = operands + [extra]
         out_specs.append(VMEM)
         out_shape.append(f32(8, 2 * EXT + 8, COLS))
         scratch += [
@@ -364,7 +373,7 @@
             block,
             pltpu.VMEM((8, COLS), jnp.float32),
             pltpu.VMEM((2, ROWS + 8, COLS), jnp.float32),
-            pltpu.SMEM((LEVELS,), jnp.float32),
+            pltpu.VMEM((16, COLS), jnp.float32),
         ]
     else:
         aliases = {len(operands): 0}
@@ -377,7 +386,7 @@
         out_shape=out_shape,
         scratch_shapes=scratch,
         input_output_aliases=aliases,
-        compiler_params=pltpu.CompilerParams(vmem_limit_bytes=48 * 2**20),
+        compiler_params=pltpu.CompilerParams(vmem_limit_bytes=(LIMA if first == 0 else LIMB) * 2**20),
         cost_estimate=pl.CostEstimate(flops=24_000_000, bytes_accessed=9_400_000, transcendentals=0),
         name="advect_forcing" if first == 0 else "advect_rest",
     )(*operands)
@@ -400,7 +409,7 @@
         out_shape=f32(8, 2 * EXT + 8, COLS),
         scratch_shapes=[pltpu.VMEM((8, 8, LANE), jnp.float32), pltpu.SemaphoreType.DMA((1,))],
         input_output_aliases={0: 0},
-        compiler_params=pltpu.CompilerParams(vmem_limit_bytes=48 * 2**20),
+        compiler_params=pltpu.CompilerParams(vmem_limit_bytes=60 * 2**20),
         cost_estimate=pl.CostEstimate(flops=1000, bytes_accessed=100_000, transcendentals=0),
         name="insert_maximum",
     )(parcels, tops)
@@ -497,7 +506,7 @@
     row_even, row_odd, col_even, col_odd, top = pack(thickness, tracers, velocity, ocean, depth)
     halos = (exchange(row_even, "bx", 0), exchange(row_odd, "bx", 1), exchange(col_even, "by", 0), exchange(col_odd, "by", 1))
     tops = lax.all_to_all(top, "bx", split_axis=0, concat_axis=0, tiled=True)
-    part, parcels = advect(0, tracers, velocity, ocean, *halos, (thickness, depth))
+    part, parcels = advect(0, tracers, velocity, ocean, *halos, depth)
     got = lax.all_to_all(insert(parcels, tops), "by", split_axis=0, concat_axis=0, tiled=True)
     new_tracers = advect(2, tracers, velocity, ocean, *halos, part)[0]
     return new_tracers, solve(got)

time: 50.1 us -> 48.3 us (0.964)
  local copies, waits for them, and re-layouts: 3.21 us -> 0.77 us
  Pallas kernels: 22.1 us -> 22.8 us
    unnamed x14 -> x8, local copies, waits for them, and re-layouts: 3.21 us -> 0.77 us
    pallas_call x1, Pallas kernels: 0.86 us -> 1.46 us  [insert(): pl.pallas_call(insert_kernel, in_specs=[HBM, VMEM], out_specs=HBM, out_sh...]
  transfers between devices with their start and end apart: 6 -> 6, of which waited for: 1 -> 1; matrix products, arithmetic and copies ran while one was open for 0% -> 0% of each run, Pallas kernels for 26% -> 27%
where the time goes in v8:
time: 48.3 us; the launch traced here: 47.9 us
  Pallas kernels  22.8 us (47%)
  starting transfers between devices  21.1 us (44%)
  waiting for transfers between devices  2.5 us (5%)
  local copies, waits for them, and re-layouts  0.77 us (2%)
  between operations  0.77 us (2%)
    pallas_call x2, Pallas kernels, advect(): pl.pallas_call(functools.partial(advect_kernel, first), in_specs=ins, out...  12.9 us
    all_to_all x1, starting transfers between devices, shards(): tops = lax.all_to_all(top, 'bx', split_axis=0, concat_axis=0, tiled=True)  8.21 us
    ppermute x4, starting transfers between devices, exchange(): return lax.ppermute(x, axis, pairs)  7.87 us
    pallas_call x1, Pallas kernels, pack(): pl.pallas_call(pack_kernel, in_specs=[HBM] * 5, out_specs=[VMEM] * 5, out...  5.17 us
    all_to_all x1, starting transfers between devices, shards(): lax.all_to_all(insert(parcels, tops), 'by', split_axis=0, concat_axis=0,...  4.98 us
    pallas_call x1, Pallas kernels, solve(): pl.pallas_call(solve_kernel, in_specs=[ANY], out_specs=VMEM, out_shape=f3...  3.31 us
    all_to_all x1, waiting for transfers between devices, shards(): lax.all_to_all(insert(parcels, tops), 'by', split_axis=0, concat_axis=0,...  2.49 us
    pallas_call x1, Pallas kernels, insert(): pl.pallas_call(insert_kernel, in_specs=[HBM, VMEM], out_specs=HBM, out_sh...  1.46 us
  transfers between devices with their start and end apart: 6, of which 1 were waited for; matrix products, arithmetic and copies ran while one was open for 0% of the time, Pallas kernels for 27%

profile of v8, /device:TPU:1, one launch (start us, length us, event | category | flops | bytes accessed | tf_op | source)
XLA Modules:
  0.0 47.9 jit_solution(18433796721207026775)
XLA Ops:
  0.6 0.0 copy-start.2
  0.6 0.0 copy-start
  0.7 0.0 copy-start.3
  0.7 5.2 %pack_edges.1 = (f32[80,256]{1,0:T(8,128)}, f32[80,256]{1,0:T(8,128)}, f32[128,128]{1,0:T(8,128)}, f32[128,128]{1,0:T(8,128)}, f32[16,8,128]{2,1,0:T(8,128)}) custom-call(f32[12]{0:T(128)} %thick_hbm.1, f32[4,12,128,256]{3,2,1,0:T(8,128)} %refs_0_.3, f32[2,12,128,256]{3,2,1,0:T(8,128)} %refs_1_.3, s32[128,256]{1,0:T(8,128)} %refs_2_.3, f32[128,256]{1,0:T(8,128)} %refs_7_.1), custom_call_target="tpu_custom_call" | custom-call | flops 4000000 | bytes 7400000 | tf_op jit(solution)/shard_map/pack_edges/pallas_call | solution.py:172
  5.8 2.2 %collective-permute-start = (f32[80,256]{1,0:T(8,128)}, f32[80,256]{1,0:T(8,128)S(1)}, u32[]{:S(2)}, u32[]{:S(2)}) collective-permute-start(f32[80,256]{1,0:T(8,128)} %get-tuple-element.9), channel_id=1, source_target_pairs={{0,8},{8,0},{16,24},{24,16},{32,40},{40,32},{48,56},{56,48},{64,72... | collective-permute-start | bytes 245768 | tf_op jit(solution)/shard_map/ppermute | solution.py:502
  8.0 1.3 %collective-permute-start.1 = (f32[80,256]{1,0:T(8,128)}, f32[80,256]{1,0:T(8,128)}, u32[]{:S(2)}, u32[]{:S(2)}) collective-permute-start(f32[80,256]{1,0:T(8,128)} %get-tuple-element.10), channel_id=1, source_target_pairs={{8,16},{16,8},{24,32},{32,24},{40,48},{48,40},{56,64},{64,56},{72,... | collective-permute-start | bytes 245768 | tf_op jit(solution)/shard_map/ppermute | solution.py:502
  9.3 1.0 %collective-permute-start.2 = (f32[128,128]{1,0:T(8,128)}, f32[128,128]{1,0:T(8,128)S(1)}, u32[]{:S(2)}, u32[]{:S(2)}) collective-permute-start(f32[128,128]{1,0:T(8,128)} %get-tuple-element.11), channel_id=1, source_target_pairs={{0,1},{1,0},{2,3},{3,2},{4,5},{5,4},{6,7},{7,6},{8,9},{9,8},{10,11... | collective-permute-start | bytes 196616 | tf_op jit(solution)/shard_map/ppermute | solution.py:502
  10.3 3.4 %collective-permute-start.3 = (f32[128,128]{1,0:T(8,128)}, f32[128,128]{1,0:T(8,128)}, u32[]{:S(2)}, u32[]{:S(2)}) collective-permute-start(f32[128,128]{1,0:T(8,128)} %get-tuple-element.12), channel_id=1, source_target_pairs={{1,2},{2,1},{3,4},{4,3},{5,6},{6,5},{9,10},{10,9},{11,12},{12,11},... | collective-permute-start | bytes 196616 | tf_op jit(solution)/shard_map/ppermute | solution.py:502
  13.7 8.2 %all-to-all-start = ((f32[16,8,128]{2,1,0:T(8,128)}), f32[16,8,128]{2,1,0:T(8,128)}, u32[]{:S(2)}, u32[]{:S(2)}) async-start(f32[16,8,128]{2,1,0:T(8,128)} %get-tuple-element.15), calls=%async_computation | async-start | bytes 131072 | tf_op jit(solution)/shard_map/all_to_all | solution.py:508
  21.9 0.0 collective-permute-done.2.refs_5_
  21.9 0.0 collective-permute-done.3.refs_6_
  22.0 0.0 collective-permute-done.refs_3_
  22.0 0.0 collective-permute-done.1.refs_4_
  22.0 0.0 copy-done.2
  22.0 0.0 copy-done
  22.0 0.0 copy-done.3
  22.0 6.5 %advect_forcing.1 = (f32[4,12,128,256]{3,2,1,0:T(8,128)}, f32[8,56,256]{2,1,0:T(8,128)S(1)}) custom-call(f32[4,12,128,256]{3,2,1,0:T(8,128)} %refs_0_.3, f32[2,12,128,256]{3,2,1,0:T(8,128)S(1)} %copy-done, s32[128,256]{1,0:T(8,128)S(1)} %copy-done.2, f32[80,256]{1,0:T(8,128)S(1)} %collective-permute-done.refs_3_, f32[80,256]{1,0:T(8,128)} %collective-permute-done.1.refs_4_, ...), custom_call_target="tpu_custom_call" | custom-call | flops 24000000 | bytes 9400000 | tf_op jit(solution)/shard_map/advect_forcing/pallas_call | solution.py:382
  28.5 0.0 copy-start.1
  28.5 0.8 %copy-done.1 = f32[8,56,256]{2,1,0:T(8,128)} copy-done((f32[8,56,256]{2,1,0:T(8,128)}, f32[8,56,256]{2,1,0:T(8,128)S(1)}, u32[]{:S(2)}) %copy-start.1) | copy-done | bytes 458776
  29.2 0.0 all-to-all-done.tops
  29.3 1.5 %insert_maximum.1 = f32[8,56,256]{2,1,0:T(8,128)} custom-call(f32[8,56,256]{2,1,0:T(8,128)} %copy-done.1, f32[16,8,128]{2,1,0:T(8,128)} %all-to-all-done.tops), custom_call_target="tpu_custom_call", output_to_operand_aliasing={{}: (0, {})} | custom-call | flops 1000 | bytes 100000 | tf_op jit(solution)/shard_map/insert_maximum/pallas_call | solution.py:405
  30.7 5.0 %all-to-all-start.1 = ((f32[8,56,256]{2,1,0:T(8,128)}), f32[8,56,256]{2,1,0:T(8,128)}, u32[]{:S(2)}, u32[]{:S(2)}) async-start(f32[8,56,256]{2,1,0:T(8,128)} %insert_maximum.1), calls=%async_computation.1 | async-start | bytes 917504 | tf_op jit(solution)/shard_map/all_to_all | solution.py:510
  35.7 6.4 %advect_rest.1 = f32[4,12,128,256]{3,2,1,0:T(8,128)} custom-call(f32[4,12,128,256]{3,2,1,0:T(8,128)} %refs_0_.3, f32[2,12,128,256]{3,2,1,0:T(8,128)S(1)} %copy-done, s32[128,256]{1,0:T(8,128)S(1)} %copy-done.2, f32[80,256]{1,0:T(8,128)S(1)} %collective-permute-done.refs_3_, ...), custom_call_target="tpu_custom_call", output_to_operand_aliasing={{}: (7, {})} | custom-call | flops 24000000 | bytes 9400000 | tf_op jit(solution)/shard_map/advect_rest/pallas_call | solution.py:382
  42.1 2.5 %all-to-all-done.1.got = f32[8,56,256]{2,1,0:T(8,128)} async-done(((f32[8,56,256]{2,1,0:T(8,128)}), f32[8,56,256]{2,1,0:T(8,128)}, u32[]{:S(2)}, u32[]{:S(2)}) %all-to-all-start.1) | async-done | bytes 458784 | tf_op jit(solution)/shard_map/all_to_all | solution.py:510
  44.6 3.3 %chebyshev.1 = f32[16,2048]{1,0:T(8,128)} custom-call(f32[8,56,256]{2,1,0:T(8,128)} %all-to-all-done.1.got), custom_call_target="tpu_custom_call" | custom-call | flops 6000000 | bytes 600000 | tf_op jit(solution)/shard_map/chebyshev/pallas_call | solution.py:479
Async XLA Ops:
  0.6 21.4 %copy-start.2 = (s32[128,256]{1,0:T(8,128)S(1)}, s32[128,256]{1,0:T(8,128)}, u32[]{:S(2)}) copy-start(s32[128,256]{1,0:T(8,128)} %refs_2_.3) | copy-start | bytes 393220
  0.6 21.4 %copy-start = (f32[2,12,128,256]{3,2,1,0:T(8,128)S(1)}, f32[2,12,128,256]{3,2,1,0:T(8,128)}, u32[]{:S(2)}) copy-start(f32[2,12,128,256]{3,2,1,0:T(8,128)} %refs_1_.3) | copy-start | bytes 9437188
  0.7 21.4 %copy-start.3 = (f32[128,256]{1,0:T(8,128)S(1)}, f32[128,256]{1,0:T(8,128)}, u32[]{:S(2)}) copy-start(f32[128,256]{1,0:T(8,128)} %refs_7_.1) | copy-start | bytes 393220
  5.8 16.1 %collective-permute-start = (f32[80,256]{1,0:T(8,128)}, f32[80,256]{1,0:T(8,128)S(1)}, u32[]{:S(2)}, u32[]{:S(2)}) collective-permute-start(f32[80,256]{1,0:T(8,128)} %get-tuple-element.9), channel_id=1, source_target_pairs={{0,8},{8,0},{16,24},{24,16},{32,40},{40,32},{48,56},{56,48},{64,72... | collective-permute-start | bytes 245768 | tf_op jit(solution)/shard_map/ppermute | solution.py:502
  8.0 13.9 %collective-permute-start.1 = (f32[80,256]{1,0:T(8,128)}, f32[80,256]{1,0:T(8,128)}, u32[]{:S(2)}, u32[]{:S(2)}) collective-permute-start(f32[80,256]{1,0:T(8,128)} %get-tuple-element.10), channel_id=1, source_target_pairs={{8,16},{16,8},{24,32},{32,24},{40,48},{48,40},{56,64},{64,56},{72,... | collective-permute-start | bytes 245768 | tf_op jit(solution)/shard_map/ppermute | solution.py:502
  9.3 12.6 %collective-permute-start.2 = (f32[128,128]{1,0:T(8,128)}, f32[128,128]{1,0:T(8,128)S(1)}, u32[]{:S(2)}, u32[]{:S(2)}) collective-permute-start(f32[128,128]{1,0:T(8,128)} %get-tuple-element.11), channel_id=1, source_target_pairs={{0,1},{1,0},{2,3},{3,2},{4,5},{5,4},{6,7},{7,6},{8,9},{9,8},{10,11... | collective-permute-start | bytes 196616 | tf_op jit(solution)/shard_map/ppermute | solution.py:502
  10.3 11.7 %collective-permute-start.3 = (f32[128,128]{1,0:T(8,128)}, f32[128,128]{1,0:T(8,128)}, u32[]{:S(2)}, u32[]{:S(2)}) collective-permute-start(f32[128,128]{1,0:T(8,128)} %get-tuple-element.12), channel_id=1, source_target_pairs={{1,2},{2,1},{3,4},{4,3},{5,6},{6,5},{9,10},{10,9},{11,12},{12,11},... | collective-permute-start | bytes 196616 | tf_op jit(solution)/shard_map/ppermute | solution.py:502
  13.7 15.5 %all-to-all-start = ((f32[16,8,128]{2,1,0:T(8,128)}), f32[16,8,128]{2,1,0:T(8,128)}, u32[]{:S(2)}, u32[]{:S(2)}) async-start(f32[16,8,128]{2,1,0:T(8,128)} %get-tuple-element.15), calls=%async_computation | async-start | bytes 131072 | tf_op jit(solution)/shard_map/all_to_all | solution.py:508
  28.5 0.8 %copy-start.1 = (f32[8,56,256]{2,1,0:T(8,128)}, f32[8,56,256]{2,1,0:T(8,128)S(1)}, u32[]{:S(2)}) copy-start(f32[8,56,256]{2,1,0:T(8,128)S(1)} %get-tuple-element.14._) | copy-start | bytes 1376260
  30.7 13.9 %all-to-all-start.1 = ((f32[8,56,256]{2,1,0:T(8,128)}), f32[8,56,256]{2,1,0:T(8,128)}, u32[]{:S(2)}, u32[]{:S(2)}) async-start(f32[8,56,256]{2,1,0:T(8,128)} %insert_maximum.1), calls=%async_computation.1 | async-start | bytes 917504 | tf_op jit(solution)/shard_map/all_to_all | solution.py:510

commit v9 on v8

--- a/solution.py
+++ b/solution.py
@@ -18,7 +18,7 @@
 EXT = 24
 CHUNK = 32
 TALL = 16
-LIMA, LIMB = 48, 48
+LIMA, LIMB, LIMC = 48, 48, 53
 
 SPEED, WET, THICK, PART, COEF, EDGE, MESSAGE = 48, 60, 61, 64, 68, 72, 80
 ANY = pl.BlockSpec(memory_space=pl.ANY)
@@ -326,17 +326,19 @@
             here = load_wet(8 * r)
             ext[0, 8 * r + 4 : 8 * r + 12, :] = total[rows, :] * here
             ext[1, 8 * r + 4 : 8 * r + 12, :] = coefficient(depth_ref[rows, :], here)
-        tile = sublanes((8, LANE))
         for j in range(8):
-            send_ref[j, 0:EXT, :] = ext[0, 16 * j : 16 * j + EXT, :]
-            send_ref[j, EXT : 2 * EXT, :] = ext[1, 16 * j : 16 * j + EXT, :]
-            edge = jnp.zeros((8, LANE), jnp.float32)
-            if j == 0:
-                edge = jnp.where((tile >= 1) & (tile <= 3), pltpu.roll(row_lo[EDGE:MESSAGE, :LANE], 4, 0), 0.0)
-            if j == 7:
-                edge = jnp.where((tile >= 4) & (tile <= 6), pltpu.roll(row_hi[EDGE:MESSAGE, :LANE], 4, 0), 0.0)
-            send_ref[j, 2 * EXT : 2 * EXT + 8, :LANE] = edge
-            send_ref[j, 2 * EXT : 2 * EXT + 8, LANE:] = jnp.zeros((8, LANE), jnp.float32)
+            at = 16 * j
+            send_ref[j, 0:22, :] = ext[0, at + 1 : at + 23, :]
+            send_ref[j, 22:44, :] = ext[1, at + 1 : at + 23, :]
+            line = jnp.zeros((1, LANE), jnp.float32)
+            halves = [line, line]
+            if j in (0, 7):
+                for i in range(3):
+                    factors = row_lo[EDGE + 5 + i : EDGE + 6 + i, :LANE] if j == 0 else row_hi[EDGE + i : EDGE + 1 + i, :LANE]
+                    at = 32 * (i if j == 0 else 3 + i)
+                    halves[at // LANE] = halves[at // LANE] + (pltpu.roll(factors, at % LANE, 1) if at % LANE else factors)
+            send_ref[j, 44:45, :] = jnp.concatenate(halves, 1)
+            send_ref[j, 45:48, :] = jnp.zeros((3, COLS), jnp.float32)
     for k in range(LEVELS):
         tracers_out(k).wait()
 
@@ -367,7 +369,7 @@
         ins = ins + [HBM]
         operands = operands + [extra]
         out_specs.append(VMEM)
-        out_shape.append(f32(8, 2 * EXT + 8, COLS))
+        out_shape.append(f32(8, 48, COLS))
         scratch += [
             block,
             block,
@@ -392,103 +394,106 @@
     )(*operands)
 
 
-def insert_kernel(_, tops, out_hbm, most, sem):
-    top = jnp.max(tops[...], axis=0)
-    for j in range(8):
-        most[j] = top
-    copy = pltpu.make_async_copy(most, out_hbm.at[:, 2 * EXT :, LANE:], sem.at[0])
-    copy.start()
-    copy.wait()
-
-
-def insert(parcels, tops):
-    return pl.pallas_call(
-        insert_kernel,
-        in_specs=[HBM, VMEM],
-        out_specs=HBM,
-        out_shape=f32(8, 2 * EXT + 8, COLS),
-        scratch_shapes=[pltpu.VMEM((8, 8, LANE), jnp.float32), pltpu.SemaphoreType.DMA((1,))],
-        input_output_aliases={0: 0},
-        compiler_params=pltpu.CompilerParams(vmem_limit_bytes=60 * 2**20),
-        cost_estimate=pl.CostEstimate(flops=1000, bytes_accessed=100_000, transcendentals=0),
-        name="insert_maximum",
-    )(parcels, tops)
-
-
-NEAR = ((1, 0, 0.5), (-1, 0, 0.5), (0, 1, 0.5), (0, -1, 0.5), (1, 1, 0.125), (1, -1, 0.125), (-1, 1, 0.125), (-1, -1, 0.125))
-
-
-def moved(x, rows, cols):
-    if cols:
-        lane = lanes(x.shape)
-        x = pltpu.roll(x, (-cols) % x.shape[1], 1)
-        x = jnp.where(lane == (x.shape[1] - 1 if cols > 0 else 0), 0.0, x)
-    if rows:
-        x = pltpu.roll(x, (-rows) % x.shape[0], 0)
-    return x
-
-
-def solve_kernel(got, out_ref, h_ref, f_ref, misc, weight, sems):
-    copies = []
-    for j in range(8):
-        cols = pl.ds(j * COLS, COLS)
-        copies.append(pltpu.make_async_copy(got.at[j, 0:EXT, :], f_ref.at[:, cols], sems.at[0, j]))
-        copies.append(pltpu.make_async_copy(got.at[j, EXT : 2 * EXT, :], h_ref.at[:, cols], sems.at[1, j]))
-        copies.append(pltpu.make_async_copy(got.at[j, 2 * EXT :, :], misc.at[j], sems.at[2, j]))
+def insert_kernel(parcels_hbm, tops_hbm, out_ref, tops, sems):
+    copies = [pltpu.make_async_copy(tops_hbm, tops, sems.at[0]), pltpu.make_async_copy(parcels_hbm, out_ref, sems.at[1])]
     for copy in copies:
         copy.start()
     for copy in copies:
         copy.wait()
+    most = jnp.max(tops[...], axis=0)[0:1, :]
+    for j in range(8):
+        out_ref[j, 45:46, :LANE] = most
+
+
+def insert(parcels, tops):
+    return pl.pallas_call(
+        insert_kernel,
+        in_specs=[ANY] * 2,
+        out_specs=VMEM,
+        out_shape=f32(8, 48, COLS),
+        scratch_shapes=[pltpu.VMEM((16, 8, LANE), jnp.float32), pltpu.SemaphoreType.DMA((2,))],
+        compiler_params=pltpu.CompilerParams(vmem_limit_bytes=LIMC * 2**20),
+        cost_estimate=pl.CostEstimate(flops=1000, bytes_accessed=900_000, transcendentals=0),
+        name="insert_maximum",
+    )(parcels, tops)
+
+
+NEAR = ((0, 1, 0.5), (1, 0, 0.5), (1, 1, 0.125), (1, -1, 0.125))
+PADDED = WIDE + LANE
+
+
+def moved(x, rows, cols):
+    if cols:
+        x = pltpu.roll(x, (-cols) % x.shape[1], 1)
+    if rows:
+        x = pltpu.roll(x, (-rows) % x.shape[0], 0)
+    return x
+
+
+def solve_kernel(got_ref, out_ref, h_ref, resid_ref, direction_ref, answer_ref, weight):
+    for ref in (h_ref, resid_ref):
+        for row in (0, EXT - 1):
+            ref[row : row + 1, :] = jnp.zeros((1, PADDED), jnp.float32)
+        ref[:, WIDE:] = jnp.zeros((EXT, LANE), jnp.float32)
+    for j in range(8):
+        cols = pl.ds(j * COLS, COLS)
+        resid_ref[1:23, cols] = got_ref[j, 0:22, :]
+        h_ref[1:23, cols] = got_ref[j, 22:44, :]
     lane, tile = lanes((8, LANE)), sublanes((8, LANE))
+    group, row = lanes((8, COLS)), sublanes((8, COLS))
+    used = (row >= 1) & (row <= 6) & (group >= 32 * (row - 1)) & (group <= 32 * (row - 1) + LEVELS)
     for j in range(7):
-        pairs = misc[j, :, :LANE] * pltpu.roll(misc[j + 1, :, :LANE], LANE - 16, 1)
-        flux = jnp.sum(jnp.where(lane <= LEVELS, pairs, 0.0), axis=1, keepdims=True)
+        pairs = got_ref[j, 44:45, :] * pltpu.roll(got_ref[j + 1, 44:45, :], COLS - 16, 1)
+        flux = jnp.sum(jnp.where(used, pairs, 0.0), axis=1, keepdims=True)
         for rows, there in ((pl.ds(0, 8), tile < 4), (pl.ds(16, 8), tile >= 4)):
             last = pl.ds((j + 1) * COLS - LANE, LANE)
             after = pl.ds((j + 1) * COLS, LANE)
-            f_ref[rows, last] = f_ref[rows, last] - jnp.where(there & (lane == LANE - 1), flux, 0.0)
-            f_ref[rows, after] = f_ref[rows, after] + jnp.where(there & (lane == 0), flux, 0.0)
-    most = jnp.max(misc[:, :, LANE:], axis=0)[0:1, 0:1]
+            resid_ref[rows, last] = resid_ref[rows, last] - jnp.where(there & (lane == LANE - 1), flux, 0.0)
+            resid_ref[rows, after] = resid_ref[rows, after] + jnp.where(there & (lane == 0), flux, 0.0)
+    most = got_ref[0, 45:46, 0:1]
+    for j in range(1, 8):
+        most = jnp.maximum(most, got_ref[j, 45:46, 0:1])
     lam_max = 0.5 + 10.0 * most
     theta = (lam_max + 0.5) / 2.0
     delta = (lam_max - 0.5) / 2.0
     sigma = theta / delta
-    rho = 1.0 / sigma
     h = h_ref[...]
     sides = {c: moved(h, 0, c) for c in (-1, 0, 1)}
     for n, (a, b, w) in enumerate(NEAR):
         weight[n] = w * (h + moved(sides[b], a, 0))
-    inside = h > 0.0
-    resid = f_ref[...]
-    direction = resid / theta
-    answer = jnp.zeros_like(resid)
-    for _ in range(ITERS):
-        sides = {c: moved(direction, 0, c) for c in (-1, 0, 1)}
-        applied = 0.5 * direction
-        for n, (a, b, w) in enumerate(NEAR):
-            applied = applied + weight[n] * (direction - moved(sides[b], a, 0))
-        resid = jnp.where(inside, resid - applied, 0.0)
-        answer = answer + direction
+    direction_ref[...] = resid_ref[...] / theta
+    answer_ref[...] = direction_ref[...]
+
+    def step(_, rho):
+        direction = direction_ref[...]
+        east, west = moved(direction, 0, 1), moved(direction, 0, -1)
+        right = weight[0] * (direction - east)
+        down = weight[1] * (direction - moved(direction, 1, 0))
+        right_down = weight[2] * (direction - moved(east, 1, 0))
+        left_down = weight[3] * (direction - moved(west, 1, 0))
+        applied = (0.5 * direction + (right - moved(right, 0, -1))) + ((down + right_down) + left_down)
+        applied = applied - moved(down + (moved(right_down, 0, -1) + moved(left_down, 0, 1)), -1, 0)
+        resid = jnp.where(h_ref[...] > 0.0, resid_ref[...] - applied, 0.0)
+        resid_ref[...] = resid
         rho_next = 1.0 / (2.0 * sigma - rho)
         direction = rho_next * rho * direction + (2.0 * rho_next / delta) * resid
-        rho = rho_next
-    out_ref[...] = (answer + direction)[4:20, :]
+        direction_ref[...] = direction
+        answer_ref[...] = answer_ref[...] + direction
+        return rho_next
+
+    lax.fori_loop(0, ITERS, step, 1.0 / sigma)
+    out_ref[...] = answer_ref[4:20, :WIDE]
 
 
 def solve(got):
+    wide = pltpu.VMEM((EXT, PADDED), jnp.float32)
     return pl.pallas_call(
         solve_kernel,
-        in_specs=[ANY],
+        in_specs=[VMEM],
         out_specs=VMEM,
         out_shape=f32(16, WIDE),
-        scratch_shapes=[
-            pltpu.VMEM((EXT, WIDE), jnp.float32),
-            pltpu.VMEM((EXT, WIDE), jnp.float32),
-            pltpu.VMEM((8, 8, COLS), jnp.float32),
-            pltpu.VMEM((8, EXT, WIDE), jnp.float32),
-            pltpu.SemaphoreType.DMA((3, 8)),
-        ],
-        compiler_params=pltpu.CompilerParams(vmem_limit_bytes=12 * 2**20),
+        scratch_shapes=[wide, wide, wide, wide, pltpu.VMEM((4, EXT, PADDED), jnp.float32)],
+        compiler_params=pltpu.CompilerParams(vmem_limit_bytes=60 * 2**20),
         cost_estimate=pl.CostEstimate(flops=6_000_000, bytes_accessed=600_000, transcendentals=0),
         name="chebyshev",
     )(got)

time: 48.3 us -> 48.7 us (level)
  local copies, waits for them, and re-layouts: 0.77 us -> 1.74 us
  waiting for transfers between devices: 2.5 us -> 1.8 us
    unnamed x8 -> x10, local copies, waits for them, and re-layouts: 0.77 us -> 1.74 us
    all_to_all x1, waiting for transfers between devices: 2.49 us -> 1.79 us  [shards(): lax.all_to_all(insert(parcels, tops), 'by', split_axis=0, concat_axis=0,...]
where the time goes in v9:
time: 48.7 us; the launch traced here: 48.3 us
  Pallas kernels  22.9 us (47%)
  starting transfers between devices  21.1 us (43%)
  waiting for transfers between devices  1.8 us (4%)
  local copies, waits for them, and re-layouts  1.74 us (4%)
  between operations  0.77 us (2%)
    pallas_call x2, Pallas kernels, advect(): pl.pallas_call(functools.partial(advect_kernel, first), in_specs=ins, out...  12.9 us
    all_to_all x1, starting transfers between devices, shards(): tops = lax.all_to_all(top, 'bx', split_axis=0, concat_axis=0, tiled=True)  8.22 us
    ppermute x4, starting transfers between devices, exchange(): return lax.ppermute(x, axis, pairs)  7.86 us
    pallas_call x1, Pallas kernels, pack(): pl.pallas_call(pack_kernel, in_specs=[HBM] * 5, out_specs=[VMEM] * 5, out...  5.16 us
    all_to_all x1, starting transfers between devices, shards(): lax.all_to_all(insert(parcels, tops), 'by', split_axis=0, concat_axis=0,...  5 us
    pallas_call x1, Pallas kernels, solve(): pl.pallas_call(solve_kernel, in_specs=[VMEM], out_specs=VMEM, out_shape=f...  3.28 us
    all_to_all x1, waiting for transfers between devices, shards(): lax.all_to_all(insert(parcels, tops), 'by', split_axis=0, concat_axis=0,...  1.79 us
    unnamed x10, local copies, waits for them, and re-layouts  1.74 us
  transfers between devices with their start and end apart: 6, of which 1 were waited for; matrix products, arithmetic and copies ran while one was open for 0% of the time, Pallas kernels for 27%

profile of v9, /device:TPU:1, one launch (start us, length us, event | category | flops | bytes accessed | tf_op | source)
XLA Modules:
  0.0 48.3 jit_solution(14394797824717279116)
XLA Ops:
  0.6 0.0 copy-start.1
  0.6 0.0 copy-start
  0.7 0.0 copy-start.2
  0.7 5.2 %pack_edges.1 = (f32[80,256]{1,0:T(8,128)}, f32[80,256]{1,0:T(8,128)}, f32[128,128]{1,0:T(8,128)}, f32[128,128]{1,0:T(8,128)}, f32[16,8,128]{2,1,0:T(8,128)}) custom-call(f32[12]{0:T(128)} %thick_hbm.1, f32[4,12,128,256]{3,2,1,0:T(8,128)} %refs_0_.3, f32[2,12,128,256]{3,2,1,0:T(8,128)} %refs_1_.3, s32[128,256]{1,0:T(8,128)} %refs_2_.3, f32[128,256]{1,0:T(8,128)} %refs_7_.1), custom_call_target="tpu_custom_call" | custom-call | flops 4000000 | bytes 7400000 | tf_op jit(solution)/shard_map/pack_edges/pallas_call | solution.py:172
  5.8 2.2 %collective-permute-start = (f32[80,256]{1,0:T(8,128)}, f32[80,256]{1,0:T(8,128)S(1)}, u32[]{:S(2)}, u32[]{:S(2)}) collective-permute-start(f32[80,256]{1,0:T(8,128)} %get-tuple-element.9), channel_id=1, source_target_pairs={{0,8},{8,0},{16,24},{24,16},{32,40},{40,32},{48,56},{56,48},{64,72... | collective-permute-start | bytes 245768 | tf_op jit(solution)/shard_map/ppermute | solution.py:507
  8.0 1.3 %collective-permute-start.1 = (f32[80,256]{1,0:T(8,128)}, f32[80,256]{1,0:T(8,128)}, u32[]{:S(2)}, u32[]{:S(2)}) collective-permute-start(f32[80,256]{1,0:T(8,128)} %get-tuple-element.10), channel_id=1, source_target_pairs={{8,16},{16,8},{24,32},{32,24},{40,48},{48,40},{56,64},{64,56},{72,... | collective-permute-start | bytes 245768 | tf_op jit(solution)/shard_map/ppermute | solution.py:507
  9.3 1.0 %collective-permute-start.2 = (f32[128,128]{1,0:T(8,128)}, f32[128,128]{1,0:T(8,128)S(1)}, u32[]{:S(2)}, u32[]{:S(2)}) collective-permute-start(f32[128,128]{1,0:T(8,128)} %get-tuple-element.11), channel_id=1, source_target_pairs={{0,1},{1,0},{2,3},{3,2},{4,5},{5,4},{6,7},{7,6},{8,9},{9,8},{10,11... | collective-permute-start | bytes 196616 | tf_op jit(solution)/shard_map/ppermute | solution.py:507
  10.3 3.4 %collective-permute-start.3 = (f32[128,128]{1,0:T(8,128)}, f32[128,128]{1,0:T(8,128)}, u32[]{:S(2)}, u32[]{:S(2)}) collective-permute-start(f32[128,128]{1,0:T(8,128)} %get-tuple-element.12), channel_id=1, source_target_pairs={{1,2},{2,1},{3,4},{4,3},{5,6},{6,5},{9,10},{10,9},{11,12},{12,11},... | collective-permute-start | bytes 196616 | tf_op jit(solution)/shard_map/ppermute | solution.py:507
  13.7 8.2 %all-to-all-start = ((f32[16,8,128]{2,1,0:T(8,128)}), f32[16,8,128]{2,1,0:T(8,128)}, u32[]{:S(2)}, u32[]{:S(2)}) async-start(f32[16,8,128]{2,1,0:T(8,128)} %get-tuple-element.15), calls=%async_computation | async-start | bytes 131072 | tf_op jit(solution)/shard_map/all_to_all | solution.py:513
  21.9 0.0 collective-permute-done.2.refs_5_
  21.9 0.0 collective-permute-done.3.refs_6_
  22.0 0.0 collective-permute-done.refs_3_
  22.0 0.0 collective-permute-done.1.refs_4_
  22.0 0.0 copy-done.1
  22.0 0.0 copy-done
  22.0 0.0 copy-done.2
  22.0 6.5 %advect_forcing.1 = (f32[4,12,128,256]{3,2,1,0:T(8,128)}, f32[8,48,256]{2,1,0:T(8,128)S(1)}) custom-call(f32[4,12,128,256]{3,2,1,0:T(8,128)} %refs_0_.3, f32[2,12,128,256]{3,2,1,0:T(8,128)S(1)} %copy-done, s32[128,256]{1,0:T(8,128)S(1)} %copy-done.1, f32[80,256]{1,0:T(8,128)S(1)} %collective-permute-done.refs_3_, f32[80,256]{1,0:T(8,128)} %collective-permute-done.1.refs_4_, ...), custom_call_target="tpu_custom_call" | custom-call | flops 24000000 | bytes 9400000 | tf_op jit(solution)/shard_map/advect_forcing/pallas_call | solution.py:384
  28.5 0.0 copy-start.3
  28.5 0.7 %copy-done.3 = f32[8,48,256]{2,1,0:T(8,128)} copy-done((f32[8,48,256]{2,1,0:T(8,128)}, f32[8,48,256]{2,1,0:T(8,128)S(1)}, u32[]{:S(2)}) %copy-start.3) | copy-done | bytes 393240
  29.2 0.0 all-to-all-done.tops_hbm
  29.2 0.0 copy-start.4
  29.2 1.0 %copy-done.4 = f32[8,48,256]{2,1,0:T(8,128)S(1)} copy-done((f32[8,48,256]{2,1,0:T(8,128)S(1)}, f32[8,48,256]{2,1,0:T(8,128)}, u32[]{:S(2)}) %copy-start.4) | copy-done | bytes 393240
  30.2 1.6 %insert_maximum.1 = f32[8,48,256]{2,1,0:T(8,128)} custom-call(f32[8,48,256]{2,1,0:T(8,128)S(1)} %copy-done.4, f32[16,8,128]{2,1,0:T(8,128)} %all-to-all-done.tops_hbm), custom_call_target="tpu_custom_call" | custom-call | flops 1000 | bytes 900000 | tf_op jit(solution)/shard_map/insert_maximum/pallas_call | solution.py:409
  31.8 5.0 %all-to-all-start.1 = ((f32[8,48,256]{2,1,0:T(8,128)}), f32[8,48,256]{2,1,0:T(8,128)}, u32[]{:S(2)}, u32[]{:S(2)}) async-start(f32[8,48,256]{2,1,0:T(8,128)} %insert_maximum.1), calls=%async_computation.1 | async-start | bytes 786432 | tf_op jit(solution)/shard_map/all_to_all | solution.py:515
  36.8 6.4 %advect_rest.1 = f32[4,12,128,256]{3,2,1,0:T(8,128)} custom-call(f32[4,12,128,256]{3,2,1,0:T(8,128)} %refs_0_.3, f32[2,12,128,256]{3,2,1,0:T(8,128)S(1)} %copy-done, s32[128,256]{1,0:T(8,128)S(1)} %copy-done.1, f32[80,256]{1,0:T(8,128)S(1)} %collective-permute-done.refs_3_, ...), custom_call_target="tpu_custom_call", output_to_operand_aliasing={{}: (7, {})} | custom-call | flops 24000000 | bytes 9400000 | tf_op jit(solution)/shard_map/advect_rest/pallas_call | solution.py:384
  43.2 1.8 %all-to-all-done.1.got_ref = f32[8,48,256]{2,1,0:T(8,128)} async-done(((f32[8,48,256]{2,1,0:T(8,128)}), f32[8,48,256]{2,1,0:T(8,128)}, u32[]{:S(2)}, u32[]{:S(2)}) %all-to-all-start.1) | async-done | bytes 393248 | tf_op jit(solution)/shard_map/all_to_all | solution.py:515
  45.0 3.3 %chebyshev.1 = f32[16,2048]{1,0:T(8,128)} custom-call(f32[8,48,256]{2,1,0:T(8,128)} %all-to-all-done.1.got_ref), custom_call_target="tpu_custom_call" | custom-call | flops 6000000 | bytes 600000 | tf_op jit(solution)/shard_map/chebyshev/pallas_call | solution.py:490
Async XLA Ops:
  0.6 21.3 %copy-start.1 = (s32[128,256]{1,0:T(8,128)S(1)}, s32[128,256]{1,0:T(8,128)}, u32[]{:S(2)}) copy-start(s32[128,256]{1,0:T(8,128)} %refs_2_.3) | copy-start | bytes 393220
  0.6 21.3 %copy-start = (f32[2,12,128,256]{3,2,1,0:T(8,128)S(1)}, f32[2,12,128,256]{3,2,1,0:T(8,128)}, u32[]{:S(2)}) copy-start(f32[2,12,128,256]{3,2,1,0:T(8,128)} %refs_1_.3) | copy-start | bytes 9437188
  0.7 21.3 %copy-start.2 = (f32[128,256]{1,0:T(8,128)S(1)}, f32[128,256]{1,0:T(8,128)}, u32[]{:S(2)}) copy-start(f32[128,256]{1,0:T(8,128)} %refs_7_.1) | copy-start | bytes 393220
  5.8 16.1 %collective-permute-start = (f32[80,256]{1,0:T(8,128)}, f32[80,256]{1,0:T(8,128)S(1)}, u32[]{:S(2)}, u32[]{:S(2)}) collective-permute-start(f32[80,256]{1,0:T(8,128)} %get-tuple-element.9), channel_id=1, source_target_pairs={{0,8},{8,0},{16,24},{24,16},{32,40},{40,32},{48,56},{56,48},{64,72... | collective-permute-start | bytes 245768 | tf_op jit(solution)/shard_map/ppermute | solution.py:507
  8.0 13.9 %collective-permute-start.1 = (f32[80,256]{1,0:T(8,128)}, f32[80,256]{1,0:T(8,128)}, u32[]{:S(2)}, u32[]{:S(2)}) collective-permute-start(f32[80,256]{1,0:T(8,128)} %get-tuple-element.10), channel_id=1, source_target_pairs={{8,16},{16,8},{24,32},{32,24},{40,48},{48,40},{56,64},{64,56},{72,... | collective-permute-start | bytes 245768 | tf_op jit(solution)/shard_map/ppermute | solution.py:507
  9.3 12.6 %collective-permute-start.2 = (f32[128,128]{1,0:T(8,128)}, f32[128,128]{1,0:T(8,128)S(1)}, u32[]{:S(2)}, u32[]{:S(2)}) collective-permute-start(f32[128,128]{1,0:T(8,128)} %get-tuple-element.11), channel_id=1, source_target_pairs={{0,1},{1,0},{2,3},{3,2},{4,5},{5,4},{6,7},{7,6},{8,9},{9,8},{10,11... | collective-permute-start | bytes 196616 | tf_op jit(solution)/shard_map/ppermute | solution.py:507
  10.3 11.7 %collective-permute-start.3 = (f32[128,128]{1,0:T(8,128)}, f32[128,128]{1,0:T(8,128)}, u32[]{:S(2)}, u32[]{:S(2)}) collective-permute-start(f32[128,128]{1,0:T(8,128)} %get-tuple-element.12), channel_id=1, source_target_pairs={{1,2},{2,1},{3,4},{4,3},{5,6},{6,5},{9,10},{10,9},{11,12},{12,11},... | collective-permute-start | bytes 196616 | tf_op jit(solution)/shard_map/ppermute | solution.py:507
  13.7 15.5 %all-to-all-start = ((f32[16,8,128]{2,1,0:T(8,128)}), f32[16,8,128]{2,1,0:T(8,128)}, u32[]{:S(2)}, u32[]{:S(2)}) async-start(f32[16,8,128]{2,1,0:T(8,128)} %get-tuple-element.15), calls=%async_computation | async-start | bytes 131072 | tf_op jit(solution)/shard_map/all_to_all | solution.py:513
  28.5 0.7 %copy-start.3 = (f32[8,48,256]{2,1,0:T(8,128)}, f32[8,48,256]{2,1,0:T(8,128)S(1)}, u32[]{:S(2)}) copy-start(f32[8,48,256]{2,1,0:T(8,128)S(1)} %get-tuple-element.14.parcels_hbm) | copy-start | bytes 1179652
  29.2 1.0 %copy-start.4 = (f32[8,48,256]{2,1,0:T(8,128)S(1)}, f32[8,48,256]{2,1,0:T(8,128)}, u32[]{:S(2)}) copy-start(f32[8,48,256]{2,1,0:T(8,128)} %copy-done.3) | copy-start | bytes 1179652
  31.8 13.2 %all-to-all-start.1 = ((f32[8,48,256]{2,1,0:T(8,128)}), f32[8,48,256]{2,1,0:T(8,128)}, u32[]{:S(2)}, u32[]{:S(2)}) async-start(f32[8,48,256]{2,1,0:T(8,128)} %insert_maximum.1), calls=%async_computation.1 | async-start | bytes 786432 | tf_op jit(solution)/shard_map/all_to_all | solution.py:515

commit v10 on v9

--- a/solution.py
+++ b/solution.py
@@ -18,7 +18,7 @@
 EXT = 24
 CHUNK = 32
 TALL = 16
-LIMA, LIMB, LIMC = 48, 48, 53
+LIMA, LIMB = 48, 48
 
 SPEED, WET, THICK, PART, COEF, EDGE, MESSAGE = 48, 60, 61, 64, 68, 72, 80
 ANY = pl.BlockSpec(memory_space=pl.ANY)
@@ -394,26 +394,23 @@
     )(*operands)
 
 
-def insert_kernel(parcels_hbm, tops_hbm, out_ref, tops, sems):
-    copies = [pltpu.make_async_copy(tops_hbm, tops, sems.at[0]), pltpu.make_async_copy(parcels_hbm, out_ref, sems.at[1])]
-    for copy in copies:
-        copy.start()
-    for copy in copies:
-        copy.wait()
-    most = jnp.max(tops[...], axis=0)[0:1, :]
-    for j in range(8):
-        out_ref[j, 45:46, :LANE] = most
+def insert_kernel(_, tops, out_hbm, most, sem):
+    most[...] = jnp.broadcast_to(jnp.max(tops[...], axis=0)[0:1, :][None], most.shape)
+    copy = pltpu.make_async_copy(most, out_hbm.at[:, 45:46, :LANE], sem.at[0])
+    copy.start()
+    copy.wait()
 
 
 def insert(parcels, tops):
     return pl.pallas_call(
         insert_kernel,
-        in_specs=[ANY] * 2,
-        out_specs=VMEM,
+        in_specs=[HBM, VMEM],
+        out_specs=HBM,
         out_shape=f32(8, 48, COLS),
-        scratch_shapes=[pltpu.VMEM((16, 8, LANE), jnp.float32), pltpu.SemaphoreType.DMA((2,))],
-        compiler_params=pltpu.CompilerParams(vmem_limit_bytes=LIMC * 2**20),
-        cost_estimate=pl.CostEstimate(flops=1000, bytes_accessed=900_000, transcendentals=0),
+        scratch_shapes=[pltpu.VMEM((8, 1, LANE), jnp.float32), pltpu.SemaphoreType.DMA((1,))],
+        input_output_aliases={0: 0},
+        compiler_params=pltpu.CompilerParams(vmem_limit_bytes=60 * 2**20),
+        cost_estimate=pl.CostEstimate(flops=1000, bytes_accessed=100_000, transcendentals=0),
         name="insert_maximum",
     )(parcels, tops)
 

time: 48.7 us -> 47.5 us (0.975)
  local copies, waits for them, and re-layouts: 1.74 us -> 0.75 us
    unnamed x10 -> x8, local copies, waits for them, and re-layouts: 1.74 us -> 0.75 us
where the time goes in v10:
time: 47.5 us; the launch traced here: 47.1 us
  Pallas kernels  22.7 us (48%)
  starting transfers between devices  21.1 us (44%)
  waiting for transfers between devices  1.8 us (4%)
  between operations  0.77 us (2%)
  local copies, waits for them, and re-layouts  0.75 us (2%)
    pallas_call x2, Pallas kernels, advect(): pl.pallas_call(functools.partial(advect_kernel, first), in_specs=ins, out...  12.9 us
    all_to_all x1, starting transfers between devices, shards(): tops = lax.all_to_all(top, 'bx', split_axis=0, concat_axis=0, tiled=True)  8.22 us
    ppermute x4, starting transfers between devices, exchange(): return lax.ppermute(x, axis, pairs)  7.87 us
    pallas_call x1, Pallas kernels, pack(): pl.pallas_call(pack_kernel, in_specs=[HBM] * 5, out_specs=[VMEM] * 5, out...  5.17 us
    all_to_all x1, starting transfers between devices, shards(): lax.all_to_all(insert(parcels, tops), 'by', split_axis=0, concat_axis=0,...  5 us
    pallas_call x1, Pallas kernels, solve(): pl.pallas_call(solve_kernel, in_specs=[VMEM], out_specs=VMEM, out_shape=f...  3.28 us
    all_to_all x1, waiting for transfers between devices, shards(): lax.all_to_all(insert(parcels, tops), 'by', split_axis=0, concat_axis=0,...  1.79 us
    pallas_call x1, Pallas kernels, insert(): pl.pallas_call(insert_kernel, in_specs=[HBM, VMEM], out_specs=HBM, out_sh...  1.43 us
  transfers between devices with their start and end apart: 6, of which 1 were waited for; matrix products, arithmetic and copies ran while one was open for 0% of the time, Pallas kernels for 27%

profile of v10, /device:TPU:1, one launch (start us, length us, event | category | flops | bytes accessed | tf_op | source)
XLA Modules:
  0.0 47.1 jit_solution(8093742955498338677)
XLA Ops:
  0.6 0.0 copy-start.2
  0.6 0.0 copy-start
  0.7 0.0 copy-start.3
  0.7 5.2 %pack_edges.1 = (f32[80,256]{1,0:T(8,128)}, f32[80,256]{1,0:T(8,128)}, f32[128,128]{1,0:T(8,128)}, f32[128,128]{1,0:T(8,128)}, f32[16,8,128]{2,1,0:T(8,128)}) custom-call(f32[12]{0:T(128)} %thick_hbm.1, f32[4,12,128,256]{3,2,1,0:T(8,128)} %refs_0_.3, f32[2,12,128,256]{3,2,1,0:T(8,128)} %refs_1_.3, s32[128,256]{1,0:T(8,128)} %refs_2_.3, f32[128,256]{1,0:T(8,128)} %refs_7_.1), custom_call_target="tpu_custom_call" | custom-call | flops 4000000 | bytes 7400000 | tf_op jit(solution)/shard_map/pack_edges/pallas_call | solution.py:172
  5.8 2.2 %collective-permute-start = (f32[80,256]{1,0:T(8,128)}, f32[80,256]{1,0:T(8,128)S(1)}, u32[]{:S(2)}, u32[]{:S(2)}) collective-permute-start(f32[80,256]{1,0:T(8,128)} %get-tuple-element.9), channel_id=1, source_target_pairs={{0,8},{8,0},{16,24},{24,16},{32,40},{40,32},{48,56},{56,48},{64,72... | collective-permute-start | bytes 245768 | tf_op jit(solution)/shard_map/ppermute | solution.py:504
  8.0 1.3 %collective-permute-start.1 = (f32[80,256]{1,0:T(8,128)}, f32[80,256]{1,0:T(8,128)}, u32[]{:S(2)}, u32[]{:S(2)}) collective-permute-start(f32[80,256]{1,0:T(8,128)} %get-tuple-element.10), channel_id=1, source_target_pairs={{8,16},{16,8},{24,32},{32,24},{40,48},{48,40},{56,64},{64,56},{72,... | collective-permute-start | bytes 245768 | tf_op jit(solution)/shard_map/ppermute | solution.py:504
  9.3 1.0 %collective-permute-start.2 = (f32[128,128]{1,0:T(8,128)}, f32[128,128]{1,0:T(8,128)S(1)}, u32[]{:S(2)}, u32[]{:S(2)}) collective-permute-start(f32[128,128]{1,0:T(8,128)} %get-tuple-element.11), channel_id=1, source_target_pairs={{0,1},{1,0},{2,3},{3,2},{4,5},{5,4},{6,7},{7,6},{8,9},{9,8},{10,11... | collective-permute-start | bytes 196616 | tf_op jit(solution)/shard_map/ppermute | solution.py:504
  10.3 3.4 %collective-permute-start.3 = (f32[128,128]{1,0:T(8,128)}, f32[128,128]{1,0:T(8,128)}, u32[]{:S(2)}, u32[]{:S(2)}) collective-permute-start(f32[128,128]{1,0:T(8,128)} %get-tuple-element.12), channel_id=1, source_target_pairs={{1,2},{2,1},{3,4},{4,3},{5,6},{6,5},{9,10},{10,9},{11,12},{12,11},... | collective-permute-start | bytes 196616 | tf_op jit(solution)/shard_map/ppermute | solution.py:504
  13.7 8.2 %all-to-all-start = ((f32[16,8,128]{2,1,0:T(8,128)}), f32[16,8,128]{2,1,0:T(8,128)}, u32[]{:S(2)}, u32[]{:S(2)}) async-start(f32[16,8,128]{2,1,0:T(8,128)} %get-tuple-element.15), calls=%async_computation | async-start | bytes 131072 | tf_op jit(solution)/shard_map/all_to_all | solution.py:510
  21.9 0.0 collective-permute-done.2.refs_5_
  21.9 0.0 collective-permute-done.3.refs_6_
  22.0 0.0 collective-permute-done.refs_3_
  22.0 0.0 collective-permute-done.1.refs_4_
  22.0 0.0 copy-done.2
  22.0 0.0 copy-done
  22.0 0.0 copy-done.3
  22.0 6.5 %advect_forcing.1 = (f32[4,12,128,256]{3,2,1,0:T(8,128)}, f32[8,48,256]{2,1,0:T(8,128)S(1)}) custom-call(f32[4,12,128,256]{3,2,1,0:T(8,128)} %refs_0_.3, f32[2,12,128,256]{3,2,1,0:T(8,128)S(1)} %copy-done, s32[128,256]{1,0:T(8,128)S(1)} %copy-done.2, f32[80,256]{1,0:T(8,128)S(1)} %collective-permute-done.refs_3_, f32[80,256]{1,0:T(8,128)} %collective-permute-done.1.refs_4_, ...), custom_call_target="tpu_custom_call" | custom-call | flops 24000000 | bytes 9400000 | tf_op jit(solution)/shard_map/advect_forcing/pallas_call | solution.py:384
  28.5 0.0 copy-start.1
  28.5 0.7 %copy-done.1 = f32[8,48,256]{2,1,0:T(8,128)} copy-done((f32[8,48,256]{2,1,0:T(8,128)}, f32[8,48,256]{2,1,0:T(8,128)S(1)}, u32[]{:S(2)}) %copy-start.1) | copy-done | bytes 393240
  29.2 0.0 all-to-all-done.tops
  29.2 1.4 %insert_maximum.1 = f32[8,48,256]{2,1,0:T(8,128)} custom-call(f32[8,48,256]{2,1,0:T(8,128)} %copy-done.1, f32[16,8,128]{2,1,0:T(8,128)} %all-to-all-done.tops), custom_call_target="tpu_custom_call", output_to_operand_aliasing={{}: (0, {})} | custom-call | flops 1000 | bytes 100000 | tf_op jit(solution)/shard_map/insert_maximum/pallas_call | solution.py:405
  30.7 5.0 %all-to-all-start.1 = ((f32[8,48,256]{2,1,0:T(8,128)}), f32[8,48,256]{2,1,0:T(8,128)}, u32[]{:S(2)}, u32[]{:S(2)}) async-start(f32[8,48,256]{2,1,0:T(8,128)} %insert_maximum.1), calls=%async_computation.1 | async-start | bytes 786432 | tf_op jit(solution)/shard_map/all_to_all | solution.py:512
  35.7 6.4 %advect_rest.1 = f32[4,12,128,256]{3,2,1,0:T(8,128)} custom-call(f32[4,12,128,256]{3,2,1,0:T(8,128)} %refs_0_.3, f32[2,12,128,256]{3,2,1,0:T(8,128)S(1)} %copy-done, s32[128,256]{1,0:T(8,128)S(1)} %copy-done.2, f32[80,256]{1,0:T(8,128)S(1)} %collective-permute-done.refs_3_, ...), custom_call_target="tpu_custom_call", output_to_operand_aliasing={{}: (7, {})} | custom-call | flops 24000000 | bytes 9400000 | tf_op jit(solution)/shard_map/advect_rest/pallas_call | solution.py:384
  42.1 1.8 %all-to-all-done.1.got_ref = f32[8,48,256]{2,1,0:T(8,128)} async-done(((f32[8,48,256]{2,1,0:T(8,128)}), f32[8,48,256]{2,1,0:T(8,128)}, u32[]{:S(2)}, u32[]{:S(2)}) %all-to-all-start.1) | async-done | bytes 393248 | tf_op jit(solution)/shard_map/all_to_all | solution.py:512
  43.9 3.3 %chebyshev.1 = f32[16,2048]{1,0:T(8,128)} custom-call(f32[8,48,256]{2,1,0:T(8,128)} %all-to-all-done.1.got_ref), custom_call_target="tpu_custom_call" | custom-call | flops 6000000 | bytes 600000 | tf_op jit(solution)/shard_map/chebyshev/pallas_call | solution.py:487
Async XLA Ops:
  0.6 21.4 %copy-start.2 = (s32[128,256]{1,0:T(8,128)S(1)}, s32[128,256]{1,0:T(8,128)}, u32[]{:S(2)}) copy-start(s32[128,256]{1,0:T(8,128)} %refs_2_.3) | copy-start | bytes 393220
  0.6 21.4 %copy-start = (f32[2,12,128,256]{3,2,1,0:T(8,128)S(1)}, f32[2,12,128,256]{3,2,1,0:T(8,128)}, u32[]{:S(2)}) copy-start(f32[2,12,128,256]{3,2,1,0:T(8,128)} %refs_1_.3) | copy-start | bytes 9437188
  0.7 21.4 %copy-start.3 = (f32[128,256]{1,0:T(8,128)S(1)}, f32[128,256]{1,0:T(8,128)}, u32[]{:S(2)}) copy-start(f32[128,256]{1,0:T(8,128)} %refs_7_.1) | copy-start | bytes 393220
  5.8 16.1 %collective-permute-start = (f32[80,256]{1,0:T(8,128)}, f32[80,256]{1,0:T(8,128)S(1)}, u32[]{:S(2)}, u32[]{:S(2)}) collective-permute-start(f32[80,256]{1,0:T(8,128)} %get-tuple-element.9), channel_id=1, source_target_pairs={{0,8},{8,0},{16,24},{24,16},{32,40},{40,32},{48,56},{56,48},{64,72... | collective-permute-start | bytes 245768 | tf_op jit(solution)/shard_map/ppermute | solution.py:504
  8.0 13.9 %collective-permute-start.1 = (f32[80,256]{1,0:T(8,128)}, f32[80,256]{1,0:T(8,128)}, u32[]{:S(2)}, u32[]{:S(2)}) collective-permute-start(f32[80,256]{1,0:T(8,128)} %get-tuple-element.10), channel_id=1, source_target_pairs={{8,16},{16,8},{24,32},{32,24},{40,48},{48,40},{56,64},{64,56},{72,... | collective-permute-start | bytes 245768 | tf_op jit(solution)/shard_map/ppermute | solution.py:504
  9.3 12.6 %collective-permute-start.2 = (f32[128,128]{1,0:T(8,128)}, f32[128,128]{1,0:T(8,128)S(1)}, u32[]{:S(2)}, u32[]{:S(2)}) collective-permute-start(f32[128,128]{1,0:T(8,128)} %get-tuple-element.11), channel_id=1, source_target_pairs={{0,1},{1,0},{2,3},{3,2},{4,5},{5,4},{6,7},{7,6},{8,9},{9,8},{10,11... | collective-permute-start | bytes 196616 | tf_op jit(solution)/shard_map/ppermute | solution.py:504
  10.3 11.7 %collective-permute-start.3 = (f32[128,128]{1,0:T(8,128)}, f32[128,128]{1,0:T(8,128)}, u32[]{:S(2)}, u32[]{:S(2)}) collective-permute-start(f32[128,128]{1,0:T(8,128)} %get-tuple-element.12), channel_id=1, source_target_pairs={{1,2},{2,1},{3,4},{4,3},{5,6},{6,5},{9,10},{10,9},{11,12},{12,11},... | collective-permute-start | bytes 196616 | tf_op jit(solution)/shard_map/ppermute | solution.py:504
  13.7 15.5 %all-to-all-start = ((f32[16,8,128]{2,1,0:T(8,128)}), f32[16,8,128]{2,1,0:T(8,128)}, u32[]{:S(2)}, u32[]{:S(2)}) async-start(f32[16,8,128]{2,1,0:T(8,128)} %get-tuple-element.15), calls=%async_computation | async-start | bytes 131072 | tf_op jit(solution)/shard_map/all_to_all | solution.py:510
  28.5 0.7 %copy-start.1 = (f32[8,48,256]{2,1,0:T(8,128)}, f32[8,48,256]{2,1,0:T(8,128)S(1)}, u32[]{:S(2)}) copy-start(f32[8,48,256]{2,1,0:T(8,128)S(1)} %get-tuple-element.14._) | copy-start | bytes 1179652
  30.7 13.2 %all-to-all-start.1 = ((f32[8,48,256]{2,1,0:T(8,128)}), f32[8,48,256]{2,1,0:T(8,128)}, u32[]{:S(2)}, u32[]{:S(2)}) async-start(f32[8,48,256]{2,1,0:T(8,128)} %insert_maximum.1), calls=%async_computation.1 | async-start | bytes 786432 | tf_op jit(solution)/shard_map/all_to_all | solution.py:512

commit v11 on v10

--- a/solution.py
+++ b/solution.py
@@ -415,27 +415,34 @@
     )(parcels, tops)
 
 
-NEAR = ((0, 1, 0.5), (1, 0, 0.5), (1, 1, 0.125), (1, -1, 0.125))
+NEAR = ((1, 0, 0.5), (-1, 0, 0.5), (0, 1, 0.5), (0, -1, 0.5), (1, 1, 0.125), (1, -1, 0.125), (-1, 1, 0.125), (-1, -1, 0.125))
 PADDED = WIDE + LANE
 
 
-def moved(x, rows, cols):
-    if cols:
-        x = pltpu.roll(x, (-cols) % x.shape[1], 1)
-    if rows:
-        x = pltpu.roll(x, (-rows) % x.shape[0], 0)
-    return x
-
-
-def solve_kernel(got_ref, out_ref, h_ref, resid_ref, direction_ref, answer_ref, weight):
-    for ref in (h_ref, resid_ref):
-        for row in (0, EXT - 1):
-            ref[row : row + 1, :] = jnp.zeros((1, PADDED), jnp.float32)
-        ref[:, WIDE:] = jnp.zeros((EXT, LANE), jnp.float32)
+def solve_kernel(got_ref, out_ref, h_ref, resid_ref, answer_ref, weight, buffers):
+    here = slice(8, 8 + EXT)
+
+    def spread():
+        field = buffers[0, here, :]
+        buffers[1, here, :] = pltpu.roll(field, PADDED - 1, 1)
+        buffers[2, here, :] = pltpu.roll(field, 1, 1)
+
+    def near(rows, cols, block):
+        return buffers[{0: 0, 1: 1, -1: 2}[cols], 8 + rows : 8 + rows + EXT, block]
+
+    def block_at(c):
+        return pl.ds(c * COLS, COLS)
+
+    for n in range(3):
+        for rows in (slice(0, 16), slice(EXT, 16 + EXT)):
+            buffers[n, rows, :] = jnp.zeros((16, PADDED), jnp.float32)
+    buffers[0, 16:EXT, WIDE:] = jnp.zeros((EXT - 16, LANE), jnp.float32)
+    for row in (0, EXT - 1):
+        resid_ref[row : row + 1, :] = jnp.zeros((1, WIDE), jnp.float32)
     for j in range(8):
         cols = pl.ds(j * COLS, COLS)
         resid_ref[1:23, cols] = got_ref[j, 0:22, :]
-        h_ref[1:23, cols] = got_ref[j, 22:44, :]
+        buffers[0, 9:31, cols] = got_ref[j, 22:44, :]
     lane, tile = lanes((8, LANE)), sublanes((8, LANE))
     group, row = lanes((8, COLS)), sublanes((8, COLS))
     used = (row >= 1) & (row <= 6) & (group >= 32 * (row - 1)) & (group <= 32 * (row - 1) + LEVELS)
@@ -454,42 +461,62 @@
     theta = (lam_max + 0.5) / 2.0
     delta = (lam_max - 0.5) / 2.0
     sigma = theta / delta
-    h = h_ref[...]
-    sides = {c: moved(h, 0, c) for c in (-1, 0, 1)}
-    for n, (a, b, w) in enumerate(NEAR):
-        weight[n] = w * (h + moved(sides[b], a, 0))
-    direction_ref[...] = resid_ref[...] / theta
-    answer_ref[...] = direction_ref[...]
+    spread()
+
+    def weigh(c, _):
+        block = block_at(c)
+        h = near(0, 0, block)
+        h_ref[:, block] = h
+        for n, (a, b, w) in enumerate(NEAR):
+            weight[n, :, block] = w * (h + near(a, b, block))
+        return 0
+
+    for c in range(WIDE // COLS):
+        weigh(c, 0)
+    direction = resid_ref[...] / theta
+    buffers[0, here, :WIDE] = direction
+    answer_ref[...] = direction
 
     def step(_, rho):
-        direction = direction_ref[...]
-        east, west = moved(direction, 0, 1), moved(direction, 0, -1)
-        right = weight[0] * (direction - east)
-        down = weight[1] * (direction - moved(direction, 1, 0))
-        right_down = weight[2] * (direction - moved(east, 1, 0))
-        left_down = weight[3] * (direction - moved(west, 1, 0))
-        applied = (0.5 * direction + (right - moved(right, 0, -1))) + ((down + right_down) + left_down)
-        applied = applied - moved(down + (moved(right_down, 0, -1) + moved(left_down, 0, 1)), -1, 0)
-        resid = jnp.where(h_ref[...] > 0.0, resid_ref[...] - applied, 0.0)
-        resid_ref[...] = resid
+        spread()
         rho_next = 1.0 / (2.0 * sigma - rho)
-        direction = rho_next * rho * direction + (2.0 * rho_next / delta) * resid
-        direction_ref[...] = direction
-        answer_ref[...] = answer_ref[...] + direction
+        keep, add = rho_next * rho, 2.0 * rho_next / delta
+
+        def update(c, _):
+            block = block_at(c)
+            direction = near(0, 0, block)
+            applied = 0.5 * direction
+            for n, (a, b, _) in enumerate(NEAR):
+                applied = applied + weight[n, :, block] * (direction - near(a, b, block))
+            resid = jnp.where(h_ref[:, block] > 0.0, resid_ref[:, block] - applied, 0.0)
+            resid_ref[:, block] = resid
+            direction = keep * direction + add * resid
+            buffers[0, here, block] = direction
+            answer_ref[:, block] = answer_ref[:, block] + direction
+            return 0
+
+        for c in range(WIDE // COLS):
+            update(c, 0)
         return rho_next
 
     lax.fori_loop(0, ITERS, step, 1.0 / sigma)
-    out_ref[...] = answer_ref[4:20, :WIDE]
+    out_ref[...] = answer_ref[4:20, :]
 
 
 def solve(got):
-    wide = pltpu.VMEM((EXT, PADDED), jnp.float32)
+    wide = pltpu.VMEM((EXT, WIDE), jnp.float32)
     return pl.pallas_call(
         solve_kernel,
         in_specs=[VMEM],
         out_specs=VMEM,
         out_shape=f32(16, WIDE),
-        scratch_shapes=[wide, wide, wide, wide, pltpu.VMEM((4, EXT, PADDED), jnp.float32)],
+        scratch_shapes=[
+            wide,
+            wide,
+            wide,
+            pltpu.VMEM((8, EXT, WIDE), jnp.float32),
+            pltpu.VMEM((3, EXT + 16, PADDED), jnp.float32),
+        ],
         compiler_params=pltpu.CompilerParams(vmem_limit_bytes=60 * 2**20),
         cost_estimate=pl.CostEstimate(flops=6_000_000, bytes_accessed=600_000, transcendentals=0),
         name="chebyshev",
@@ -506,7 +533,8 @@
 
 def shards(tracers, velocity, ocean, thickness, depth):
     row_even, row_odd, col_even, col_odd, top = pack(thickness, tracers, velocity, ocean, depth)
-    halos = (exchange(row_even, "bx", 0), exchange(row_odd, "bx", 1), exchange(col_even, "by", 0), exchange(col_odd, "by", 1))
+    from_row_odd, from_col_odd = exchange(row_odd, "bx", 1), exchange(col_odd, "by", 1)
+    halos = (exchange(row_even, "bx", 0), from_row_odd, exchange(col_even, "by", 0), from_col_odd)
     tops = lax.all_to_all(top, "bx", split_axis=0, concat_axis=0, tiled=True)
     part, parcels = advect(0, tracers, velocity, ocean, *halos, depth)
     got = lax.all_to_all(insert(parcels, tops), "by", split_axis=0, concat_axis=0, tiled=True)

time: 47.5 us -> 47.4 us (level)
  no operation moved by 1% of the time
where the time goes in v11:
time: 47.4 us; the launch traced here: 47 us
  Pallas kernels  22.6 us (48%)
  starting transfers between devices  21.1 us (45%)
  waiting for transfers between devices  1.8 us (4%)
  between operations  0.77 us (2%)
  local copies, waits for them, and re-layouts  0.75 us (2%)
    pallas_call x2, Pallas kernels, advect(): pl.pallas_call(functools.partial(advect_kernel, first), in_specs=ins, out...  12.9 us
    all_to_all x1, starting transfers between devices, shards(): tops = lax.all_to_all(top, 'bx', split_axis=0, concat_axis=0, tiled=True)  8.22 us
    ppermute x4, starting transfers between devices, exchange(): return lax.ppermute(x, axis, pairs)  7.87 us
    pallas_call x1, Pallas kernels, pack(): pl.pallas_call(pack_kernel, in_specs=[HBM] * 5, out_specs=[VMEM] * 5, out...  5.17 us
    all_to_all x1, starting transfers between devices, shards(): lax.all_to_all(insert(parcels, tops), 'by', split_axis=0, concat_axis=0,...  5 us
    pallas_call x1, Pallas kernels, solve(): pl.pallas_call(solve_kernel, in_specs=[VMEM], out_specs=VMEM, out_shape=f...  3.18 us
    all_to_all x1, waiting for transfers between devices, shards(): lax.all_to_all(insert(parcels, tops), 'by', split_axis=0, concat_axis=0,...  1.79 us
    pallas_call x1, Pallas kernels, insert(): pl.pallas_call(insert_kernel, in_specs=[HBM, VMEM], out_specs=HBM, out_sh...  1.43 us
  transfers between devices with their start and end apart: 6, of which 1 were waited for; matrix products, arithmetic and copies ran while one was open for 0% of the time, Pallas kernels for 27%

profile of v11, /device:TPU:1, one launch (start us, length us, event | category | flops | bytes accessed | tf_op | source)
XLA Modules:
  0.0 47.0 jit_solution(14730669268644241410)
XLA Ops:
  0.6 0.0 copy-start.2
  0.6 0.0 copy-start
  0.7 0.0 copy-start.3
  0.7 5.2 %pack_edges.1 = (f32[80,256]{1,0:T(8,128)}, f32[80,256]{1,0:T(8,128)}, f32[128,128]{1,0:T(8,128)}, f32[128,128]{1,0:T(8,128)}, f32[16,8,128]{2,1,0:T(8,128)}) custom-call(f32[12]{0:T(128)} %thick_hbm.1, f32[4,12,128,256]{3,2,1,0:T(8,128)} %refs_0_.3, f32[2,12,128,256]{3,2,1,0:T(8,128)} %refs_1_.3, s32[128,256]{1,0:T(8,128)} %refs_2_.3, f32[128,256]{1,0:T(8,128)} %refs_7_.1), custom_call_target="tpu_custom_call" | custom-call | flops 4000000 | bytes 7400000 | tf_op jit(solution)/shard_map/pack_edges/pallas_call | solution.py:172
  5.8 2.2 %collective-permute-start = (f32[80,256]{1,0:T(8,128)}, f32[80,256]{1,0:T(8,128)S(1)}, u32[]{:S(2)}, u32[]{:S(2)}) collective-permute-start(f32[80,256]{1,0:T(8,128)} %get-tuple-element.9), channel_id=1, source_target_pairs={{0,8},{8,0},{16,24},{24,16},{32,40},{40,32},{48,56},{56,48},{64,72... | collective-permute-start | bytes 245768 | tf_op jit(solution)/shard_map/ppermute | solution.py:531
  8.0 1.3 %collective-permute-start.1 = (f32[80,256]{1,0:T(8,128)}, f32[80,256]{1,0:T(8,128)}, u32[]{:S(2)}, u32[]{:S(2)}) collective-permute-start(f32[80,256]{1,0:T(8,128)} %get-tuple-element.10), channel_id=1, source_target_pairs={{8,16},{16,8},{24,32},{32,24},{40,48},{48,40},{56,64},{64,56},{72,... | collective-permute-start | bytes 245768 | tf_op jit(solution)/shard_map/ppermute | solution.py:531
  9.3 1.0 %collective-permute-start.2 = (f32[128,128]{1,0:T(8,128)}, f32[128,128]{1,0:T(8,128)S(1)}, u32[]{:S(2)}, u32[]{:S(2)}) collective-permute-start(f32[128,128]{1,0:T(8,128)} %get-tuple-element.11), channel_id=1, source_target_pairs={{0,1},{1,0},{2,3},{3,2},{4,5},{5,4},{6,7},{7,6},{8,9},{9,8},{10,11... | collective-permute-start | bytes 196616 | tf_op jit(solution)/shard_map/ppermute | solution.py:531
  10.3 3.4 %collective-permute-start.3 = (f32[128,128]{1,0:T(8,128)}, f32[128,128]{1,0:T(8,128)}, u32[]{:S(2)}, u32[]{:S(2)}) collective-permute-start(f32[128,128]{1,0:T(8,128)} %get-tuple-element.12), channel_id=1, source_target_pairs={{1,2},{2,1},{3,4},{4,3},{5,6},{6,5},{9,10},{10,9},{11,12},{12,11},... | collective-permute-start | bytes 196616 | tf_op jit(solution)/shard_map/ppermute | solution.py:531
  13.7 8.2 %all-to-all-start = ((f32[16,8,128]{2,1,0:T(8,128)}), f32[16,8,128]{2,1,0:T(8,128)}, u32[]{:S(2)}, u32[]{:S(2)}) async-start(f32[16,8,128]{2,1,0:T(8,128)} %get-tuple-element.15), calls=%async_computation | async-start | bytes 131072 | tf_op jit(solution)/shard_map/all_to_all | solution.py:538
  21.9 0.0 collective-permute-done.2.refs_5_
  21.9 0.0 collective-permute-done.3.refs_6_
  22.0 0.0 collective-permute-done.refs_3_
  22.0 0.0 collective-permute-done.1.refs_4_
  22.0 0.0 copy-done.2
  22.0 0.0 copy-done
  22.0 0.0 copy-done.3
  22.0 6.5 %advect_forcing.1 = (f32[4,12,128,256]{3,2,1,0:T(8,128)}, f32[8,48,256]{2,1,0:T(8,128)S(1)}) custom-call(f32[4,12,128,256]{3,2,1,0:T(8,128)} %refs_0_.3, f32[2,12,128,256]{3,2,1,0:T(8,128)S(1)} %copy-done, s32[128,256]{1,0:T(8,128)S(1)} %copy-done.2, f32[80,256]{1,0:T(8,128)S(1)} %collective-permute-done.refs_3_, f32[80,256]{1,0:T(8,128)} %collective-permute-done.1.refs_4_, ...), custom_call_target="tpu_custom_call" | custom-call | flops 24000000 | bytes 9400000 | tf_op jit(solution)/shard_map/advect_forcing/pallas_call | solution.py:384
  28.5 0.0 copy-start.1
  28.5 0.7 %copy-done.1 = f32[8,48,256]{2,1,0:T(8,128)} copy-done((f32[8,48,256]{2,1,0:T(8,128)}, f32[8,48,256]{2,1,0:T(8,128)S(1)}, u32[]{:S(2)}) %copy-start.1) | copy-done | bytes 393240
  29.2 0.0 all-to-all-done.tops
  29.2 1.4 %insert_maximum.1 = f32[8,48,256]{2,1,0:T(8,128)} custom-call(f32[8,48,256]{2,1,0:T(8,128)} %copy-done.1, f32[16,8,128]{2,1,0:T(8,128)} %all-to-all-done.tops), custom_call_target="tpu_custom_call", output_to_operand_aliasing={{}: (0, {})} | custom-call | flops 1000 | bytes 100000 | tf_op jit(solution)/shard_map/insert_maximum/pallas_call | solution.py:405
  30.7 5.0 %all-to-all-start.1 = ((f32[8,48,256]{2,1,0:T(8,128)}), f32[8,48,256]{2,1,0:T(8,128)}, u32[]{:S(2)}, u32[]{:S(2)}) async-start(f32[8,48,256]{2,1,0:T(8,128)} %insert_maximum.1), calls=%async_computation.1 | async-start | bytes 786432 | tf_op jit(solution)/shard_map/all_to_all | solution.py:540
  35.7 6.4 %advect_rest.1 = f32[4,12,128,256]{3,2,1,0:T(8,128)} custom-call(f32[4,12,128,256]{3,2,1,0:T(8,128)} %refs_0_.3, f32[2,12,128,256]{3,2,1,0:T(8,128)S(1)} %copy-done, s32[128,256]{1,0:T(8,128)S(1)} %copy-done.2, f32[80,256]{1,0:T(8,128)S(1)} %collective-permute-done.refs_3_, ...), custom_call_target="tpu_custom_call", output_to_operand_aliasing={{}: (7, {})} | custom-call | flops 24000000 | bytes 9400000 | tf_op jit(solution)/shard_map/advect_rest/pallas_call | solution.py:384
  42.1 1.8 %all-to-all-done.1.got_ref = f32[8,48,256]{2,1,0:T(8,128)} async-done(((f32[8,48,256]{2,1,0:T(8,128)}), f32[8,48,256]{2,1,0:T(8,128)}, u32[]{:S(2)}, u32[]{:S(2)}) %all-to-all-start.1) | async-done | bytes 393248 | tf_op jit(solution)/shard_map/all_to_all | solution.py:540
  43.9 3.2 %chebyshev.1 = f32[16,2048]{1,0:T(8,128)} custom-call(f32[8,48,256]{2,1,0:T(8,128)} %all-to-all-done.1.got_ref), custom_call_target="tpu_custom_call" | custom-call | flops 6000000 | bytes 600000 | tf_op jit(solution)/shard_map/chebyshev/pallas_call | solution.py:508
Async XLA Ops:
  0.6 21.4 %copy-start.2 = (s32[128,256]{1,0:T(8,128)S(1)}, s32[128,256]{1,0:T(8,128)}, u32[]{:S(2)}) copy-start(s32[128,256]{1,0:T(8,128)} %refs_2_.3) | copy-start | bytes 393220
  0.6 21.4 %copy-start = (f32[2,12,128,256]{3,2,1,0:T(8,128)S(1)}, f32[2,12,128,256]{3,2,1,0:T(8,128)}, u32[]{:S(2)}) copy-start(f32[2,12,128,256]{3,2,1,0:T(8,128)} %refs_1_.3) | copy-start | bytes 9437188
  0.7 21.4 %copy-start.3 = (f32[128,256]{1,0:T(8,128)S(1)}, f32[128,256]{1,0:T(8,128)}, u32[]{:S(2)}) copy-start(f32[128,256]{1,0:T(8,128)} %refs_7_.1) | copy-start | bytes 393220
  5.8 16.1 %collective-permute-start = (f32[80,256]{1,0:T(8,128)}, f32[80,256]{1,0:T(8,128)S(1)}, u32[]{:S(2)}, u32[]{:S(2)}) collective-permute-start(f32[80,256]{1,0:T(8,128)} %get-tuple-element.9), channel_id=1, source_target_pairs={{0,8},{8,0},{16,24},{24,16},{32,40},{40,32},{48,56},{56,48},{64,72... | collective-permute-start | bytes 245768 | tf_op jit(solution)/shard_map/ppermute | solution.py:531
  8.0 13.9 %collective-permute-start.1 = (f32[80,256]{1,0:T(8,128)}, f32[80,256]{1,0:T(8,128)}, u32[]{:S(2)}, u32[]{:S(2)}) collective-permute-start(f32[80,256]{1,0:T(8,128)} %get-tuple-element.10), channel_id=1, source_target_pairs={{8,16},{16,8},{24,32},{32,24},{40,48},{48,40},{56,64},{64,56},{72,... | collective-permute-start | bytes 245768 | tf_op jit(solution)/shard_map/ppermute | solution.py:531
  9.3 12.6 %collective-permute-start.2 = (f32[128,128]{1,0:T(8,128)}, f32[128,128]{1,0:T(8,128)S(1)}, u32[]{:S(2)}, u32[]{:S(2)}) collective-permute-start(f32[128,128]{1,0:T(8,128)} %get-tuple-element.11), channel_id=1, source_target_pairs={{0,1},{1,0},{2,3},{3,2},{4,5},{5,4},{6,7},{7,6},{8,9},{9,8},{10,11... | collective-permute-start | bytes 196616 | tf_op jit(solution)/shard_map/ppermute | solution.py:531
  10.3 11.7 %collective-permute-start.3 = (f32[128,128]{1,0:T(8,128)}, f32[128,128]{1,0:T(8,128)}, u32[]{:S(2)}, u32[]{:S(2)}) collective-permute-start(f32[128,128]{1,0:T(8,128)} %get-tuple-element.12), channel_id=1, source_target_pairs={{1,2},{2,1},{3,4},{4,3},{5,6},{6,5},{9,10},{10,9},{11,12},{12,11},... | collective-permute-start | bytes 196616 | tf_op jit(solution)/shard_map/ppermute | solution.py:531
  13.7 15.5 %all-to-all-start = ((f32[16,8,128]{2,1,0:T(8,128)}), f32[16,8,128]{2,1,0:T(8,128)}, u32[]{:S(2)}, u32[]{:S(2)}) async-start(f32[16,8,128]{2,1,0:T(8,128)} %get-tuple-element.15), calls=%async_computation | async-start | bytes 131072 | tf_op jit(solution)/shard_map/all_to_all | solution.py:538
  28.5 0.7 %copy-start.1 = (f32[8,48,256]{2,1,0:T(8,128)}, f32[8,48,256]{2,1,0:T(8,128)S(1)}, u32[]{:S(2)}) copy-start(f32[8,48,256]{2,1,0:T(8,128)S(1)} %get-tuple-element.14._) | copy-start | bytes 1179652
  30.7 13.2 %all-to-all-start.1 = ((f32[8,48,256]{2,1,0:T(8,128)}), f32[8,48,256]{2,1,0:T(8,128)}, u32[]{:S(2)}, u32[]{:S(2)}) async-start(f32[8,48,256]{2,1,0:T(8,128)} %insert_maximum.1), calls=%async_computation.1 | async-start | bytes 786432 | tf_op jit(solution)/shard_map/all_to_all | solution.py:540

commit v12 on v11

--- a/solution.py
+++ b/solution.py
@@ -80,7 +80,7 @@
     return jnp.where(lane == LEVELS, pltpu.roll(upwind * last, LEVELS + 1, 1), terms)
 
 
-def pack_kernel(thick_hbm, t_hbm, v_hbm, ocean_hbm, depth_hbm, row_even, row_odd, col_even, col_odd, top,
+def pack_kernel(thick_hbm, t_hbm, v_hbm, ocean_hbm, depth_hbm, row_odd, col_odd, row_even, col_even, top,
                 t_ref, u_top, u_low, v_top, v_low, v_last, ocean_ref, depth_ref, thick, row_both, col_both, sems):
     odd_x, odd_y = lax.axis_index("bx") % 2, lax.axis_index("by") % 2
     row_hi, row_lo = row_both.at[0], row_both.at[1]
@@ -173,7 +173,7 @@
         pack_kernel,
         in_specs=[HBM] * 5,
         out_specs=[VMEM] * 5,
-        out_shape=[f32(MESSAGE, COLS), f32(MESSAGE, COLS), f32(ROWS, LANE), f32(ROWS, LANE), f32(16, 8, LANE)],
+        out_shape=[f32(MESSAGE, COLS), f32(ROWS, LANE), f32(MESSAGE, COLS), f32(ROWS, LANE), f32(16, 8, LANE)],
         scratch_shapes=[
             pltpu.VMEM((TRACERS, LEVELS, ROWS, COLS), jnp.float32),
             pltpu.VMEM(tile, jnp.float32),
@@ -218,11 +218,11 @@
 
 def advect_kernel(first, *refs):
     if first == 0:
-        (t_hbm, v_hbm, ocean_hbm, row_even, row_odd, col_even, col_odd, depth_hbm, out_hbm, send_ref,
+        (t_hbm, v_hbm, ocean_hbm, row_odd, col_odd, row_even, col_even, depth_hbm, out_hbm, send_ref,
          t_ref, v_ref, out_ref, ocean_ref, rows_in, cols_in, w_x, w_y, before_y, edges, sems, small_sems,
          depth_ref, total, flux, ext, thick) = refs
     else:
-        (t_hbm, v_hbm, ocean_hbm, row_even, row_odd, col_even, col_odd, _, out_hbm,
+        (t_hbm, v_hbm, ocean_hbm, row_odd, col_odd, row_even, col_even, _, out_hbm,
          t_ref, v_ref, out_ref, ocean_ref, rows_in, cols_in, w_x, w_y, before_y, edges, sems, small_sems) = refs
     odd_x, odd_y = lax.axis_index("bx") % 2, lax.axis_index("by") % 2
     row_lo, row_hi = rows_in.at[0], rows_in.at[1]
@@ -343,9 +343,9 @@
         tracers_out(k).wait()
 
 
-def advect(first, tracers, velocity, ocean, row_even, row_odd, col_even, col_odd, extra):
+def advect(first, tracers, velocity, ocean, row_odd, col_odd, row_even, col_even, extra):
     ins = [HBM] * 3 + [ANY] * 4
-    operands = [tracers, velocity, ocean, row_even, row_odd, col_even, col_odd]
+    operands = [tracers, velocity, ocean, row_odd, col_odd, row_even, col_even]
     out_specs = [HBM]
     out_shape = [f32(TRACERS, LEVELS, ROWS, COLS)]
     block = pltpu.VMEM((ROWS, COLS), jnp.float32)
@@ -532,9 +532,8 @@
 
 
 def shards(tracers, velocity, ocean, thickness, depth):
-    row_even, row_odd, col_even, col_odd, top = pack(thickness, tracers, velocity, ocean, depth)
-    from_row_odd, from_col_odd = exchange(row_odd, "bx", 1), exchange(col_odd, "by", 1)
-    halos = (exchange(row_even, "bx", 0), from_row_odd, exchange(col_even, "by", 0), from_col_odd)
+    row_odd, col_odd, row_even, col_even, top = pack(thickness, tracers, velocity, ocean, depth)
+    halos = (exchange(row_odd, "bx", 1), exchange(col_odd, "by", 1), exchange(row_even, "bx", 0), exchange(col_even, "by", 0))
     tops = lax.all_to_all(top, "bx", split_axis=0, concat_axis=0, tiled=True)
     part, parcels = advect(0, tracers, velocity, ocean, *halos, depth)
     got = lax.all_to_all(insert(parcels, tops), "by", split_axis=0, concat_axis=0, tiled=True)

time: 47.4 us -> 48.4 us (1.021)
  starting transfers between devices: 21.1 us -> 22.1 us
    all_to_all x1, starting transfers between devices: 8.22 us -> 5.8 us  [shards(): tops = lax.all_to_all(top, 'bx', split_axis=0, concat_axis=0, tiled=True)]
    ppermute x4, starting transfers between devices: 7.87 us -> 10.1 us  [exchange(): return lax.ppermute(x, axis, pairs)]
    all_to_all x1, starting transfers between devices: 5 us -> 6.14 us  [shards(): lax.all_to_all(insert(parcels, tops), 'by', split_axis=0, concat_axis=0,...]
  transfers between devices with their start and end apart: 6 -> 6, of which waited for: 1 -> 1; matrix products, arithmetic and copies ran while one was open for 0% -> 0% of each run, Pallas kernels for 27% -> 26%
where the time goes in v12:
time: 48.4 us; the launch traced here: 48 us
  Pallas kernels  22.4 us (46%)
  starting transfers between devices  22.1 us (46%)
  waiting for transfers between devices  1.88 us (4%)
  between operations  0.78 us (2%)
  local copies, waits for them, and re-layouts  0.75 us (2%)
    pallas_call x2, Pallas kernels, advect(): pl.pallas_call(functools.partial(advect_kernel, first), in_specs=ins, out...  12.7 us
    ppermute x4, starting transfers between devices, exchange(): return lax.ppermute(x, axis, pairs)  10.1 us
    all_to_all x1, starting transfers between devices, shards(): lax.all_to_all(insert(parcels, tops), 'by', split_axis=0, concat_axis=0,...  6.14 us
    all_to_all x1, starting transfers between devices, shards(): tops = lax.all_to_all(top, 'bx', split_axis=0, concat_axis=0, tiled=True)  5.8 us
    pallas_call x1, Pallas kernels, pack(): pl.pallas_call(pack_kernel, in_specs=[HBM] * 5, out_specs=[VMEM] * 5, out...  5.15 us
    pallas_call x1, Pallas kernels, solve(): pl.pallas_call(solve_kernel, in_specs=[VMEM], out_specs=VMEM, out_shape=f...  3.18 us
    all_to_all x1, waiting for transfers between devices, shards(): lax.all_to_all(insert(parcels, tops), 'by', split_axis=0, concat_axis=0,...  1.87 us
    pallas_call x1, Pallas kernels, insert(): pl.pallas_call(insert_kernel, in_specs=[HBM, VMEM], out_specs=HBM, out_sh...  1.43 us
  transfers between devices with their start and end apart: 6, of which 1 were waited for; matrix products, arithmetic and copies ran while one was open for 0% of the time, Pallas kernels for 26%

profile of v12, /device:TPU:1, one launch (start us, length us, event | category | flops | bytes accessed | tf_op | source)
XLA Modules:
  0.0 48.0 jit_solution(4293220161053346094)
XLA Ops:
  0.6 0.0 copy-start.2
  0.6 0.0 copy-start
  0.7 0.0 copy-start.3
  0.7 5.2 %pack_edges.1 = (f32[80,256]{1,0:T(8,128)}, f32[128,128]{1,0:T(8,128)}, f32[80,256]{1,0:T(8,128)}, f32[128,128]{1,0:T(8,128)}, f32[16,8,128]{2,1,0:T(8,128)}) custom-call(f32[12]{0:T(128)} %thick_hbm.1, f32[4,12,128,256]{3,2,1,0:T(8,128)} %refs_0_.3, f32[2,12,128,256]{3,2,1,0:T(8,128)} %refs_1_.3, s32[128,256]{1,0:T(8,128)} %refs_2_.3, f32[128,256]{1,0:T(8,128)} %refs_7_.1), custom_call_target="tpu_custom_call" | custom-call | flops 4000000 | bytes 7400000 | tf_op jit(solution)/shard_map/pack_edges/pallas_call | solution.py:172
  5.8 0.7 %collective-permute-start = (f32[80,256]{1,0:T(8,128)}, f32[80,256]{1,0:T(8,128)S(1)}, u32[]{:S(2)}, u32[]{:S(2)}) collective-permute-start(f32[80,256]{1,0:T(8,128)} %get-tuple-element.9), channel_id=1, source_target_pairs={{8,16},{16,8},{24,32},{32,24},{40,48},{48,40},{56,64},{64,56},{72,... | collective-permute-start | bytes 245768 | tf_op jit(solution)/shard_map/ppermute | solution.py:531
  6.5 4.7 %collective-permute-start.2 = (f32[80,256]{1,0:T(8,128)}, f32[80,256]{1,0:T(8,128)}, u32[]{:S(2)}, u32[]{:S(2)}) collective-permute-start(f32[80,256]{1,0:T(8,128)} %get-tuple-element.11), channel_id=1, source_target_pairs={{0,8},{8,0},{16,24},{24,16},{32,40},{40,32},{48,56},{56,48},{64,72... | collective-permute-start | bytes 245768 | tf_op jit(solution)/shard_map/ppermute | solution.py:531
  11.2 4.7 %collective-permute-start.1 = (f32[128,128]{1,0:T(8,128)}, f32[128,128]{1,0:T(8,128)S(1)}, u32[]{:S(2)}, u32[]{:S(2)}) collective-permute-start(f32[128,128]{1,0:T(8,128)} %get-tuple-element.10), channel_id=1, source_target_pairs={{1,2},{2,1},{3,4},{4,3},{5,6},{6,5},{9,10},{10,9},{11,12},{12,11},... | collective-permute-start | bytes 196616 | tf_op jit(solution)/shard_map/ppermute | solution.py:531
  15.9 0.1 collective-permute-start.3
  16.0 5.8 %all-to-all-start = ((f32[16,8,128]{2,1,0:T(8,128)}), f32[16,8,128]{2,1,0:T(8,128)}, u32[]{:S(2)}, u32[]{:S(2)}) async-start(f32[16,8,128]{2,1,0:T(8,128)} %get-tuple-element.15), calls=%async_computation | async-start | bytes 131072 | tf_op jit(solution)/shard_map/all_to_all | solution.py:537
  21.8 0.0 collective-permute-done.1.refs_4_
  21.8 0.0 collective-permute-done.3.refs_6_
  21.8 0.0 collective-permute-done.refs_3_
  21.8 0.0 collective-permute-done.2.refs_5_
  21.8 0.0 copy-done.2
  21.9 0.0 copy-done
  21.9 0.0 copy-done.3
  21.9 6.4 %advect_forcing.1 = (f32[4,12,128,256]{3,2,1,0:T(8,128)}, f32[8,48,256]{2,1,0:T(8,128)S(1)}) custom-call(f32[4,12,128,256]{3,2,1,0:T(8,128)} %refs_0_.3, f32[2,12,128,256]{3,2,1,0:T(8,128)S(1)} %copy-done, s32[128,256]{1,0:T(8,128)S(1)} %copy-done.2, f32[80,256]{1,0:T(8,128)S(1)} %collective-permute-done.refs_3_, ...), custom_call_target="tpu_custom_call" | custom-call | flops 24000000 | bytes 9400000 | tf_op jit(solution)/shard_map/advect_forcing/pallas_call | solution.py:384
  28.3 0.0 copy-start.1
  28.3 0.7 %copy-done.1 = f32[8,48,256]{2,1,0:T(8,128)} copy-done((f32[8,48,256]{2,1,0:T(8,128)}, f32[8,48,256]{2,1,0:T(8,128)S(1)}, u32[]{:S(2)}) %copy-start.1) | copy-done | bytes 393240
  29.0 0.0 all-to-all-done.tops
  29.0 1.4 %insert_maximum.1 = f32[8,48,256]{2,1,0:T(8,128)} custom-call(f32[8,48,256]{2,1,0:T(8,128)} %copy-done.1, f32[16,8,128]{2,1,0:T(8,128)} %all-to-all-done.tops), custom_call_target="tpu_custom_call", output_to_operand_aliasing={{}: (0, {})} | custom-call | flops 1000 | bytes 100000 | tf_op jit(solution)/shard_map/insert_maximum/pallas_call | solution.py:405
  30.5 6.1 %all-to-all-start.1 = ((f32[8,48,256]{2,1,0:T(8,128)}), f32[8,48,256]{2,1,0:T(8,128)}, u32[]{:S(2)}, u32[]{:S(2)}) async-start(f32[8,48,256]{2,1,0:T(8,128)} %insert_maximum.1), calls=%async_computation.1 | async-start | bytes 786432 | tf_op jit(solution)/shard_map/all_to_all | solution.py:539
  36.6 6.3 %advect_rest.1 = f32[4,12,128,256]{3,2,1,0:T(8,128)} custom-call(f32[4,12,128,256]{3,2,1,0:T(8,128)} %refs_0_.3, f32[2,12,128,256]{3,2,1,0:T(8,128)S(1)} %copy-done, s32[128,256]{1,0:T(8,128)S(1)} %copy-done.2, f32[80,256]{1,0:T(8,128)S(1)} %collective-permute-done.refs_3_, ...), custom_call_target="tpu_custom_call", output_to_operand_aliasing={{}: (7, {})} | custom-call | flops 24000000 | bytes 9400000 | tf_op jit(solution)/shard_map/advect_rest/pallas_call | solution.py:384
  42.9 1.9 %all-to-all-done.1.got_ref = f32[8,48,256]{2,1,0:T(8,128)} async-done(((f32[8,48,256]{2,1,0:T(8,128)}), f32[8,48,256]{2,1,0:T(8,128)}, u32[]{:S(2)}, u32[]{:S(2)}) %all-to-all-start.1) | async-done | bytes 393248 | tf_op jit(solution)/shard_map/all_to_all | solution.py:539
  44.8 3.2 %chebyshev.1 = f32[16,2048]{1,0:T(8,128)} custom-call(f32[8,48,256]{2,1,0:T(8,128)} %all-to-all-done.1.got_ref), custom_call_target="tpu_custom_call" | custom-call | flops 6000000 | bytes 600000 | tf_op jit(solution)/shard_map/chebyshev/pallas_call | solution.py:508
Async XLA Ops:
  0.6 21.2 %copy-start.2 = (s32[128,256]{1,0:T(8,128)S(1)}, s32[128,256]{1,0:T(8,128)}, u32[]{:S(2)}) copy-start(s32[128,256]{1,0:T(8,128)} %refs_2_.3) | copy-start | bytes 393220
  0.6 21.2 %copy-start = (f32[2,12,128,256]{3,2,1,0:T(8,128)S(1)}, f32[2,12,128,256]{3,2,1,0:T(8,128)}, u32[]{:S(2)}) copy-start(f32[2,12,128,256]{3,2,1,0:T(8,128)} %refs_1_.3) | copy-start | bytes 9437188
  0.7 21.2 %copy-start.3 = (f32[128,256]{1,0:T(8,128)S(1)}, f32[128,256]{1,0:T(8,128)}, u32[]{:S(2)}) copy-start(f32[128,256]{1,0:T(8,128)} %refs_7_.1) | copy-start | bytes 393220
  5.8 16.0 %collective-permute-start = (f32[80,256]{1,0:T(8,128)}, f32[80,256]{1,0:T(8,128)S(1)}, u32[]{:S(2)}, u32[]{:S(2)}) collective-permute-start(f32[80,256]{1,0:T(8,128)} %get-tuple-element.9), channel_id=1, source_target_pairs={{8,16},{16,8},{24,32},{32,24},{40,48},{48,40},{56,64},{64,56},{72,... | collective-permute-start | bytes 245768 | tf_op jit(solution)/shard_map/ppermute | solution.py:531
  6.5 15.3 %collective-permute-start.2 = (f32[80,256]{1,0:T(8,128)}, f32[80,256]{1,0:T(8,128)}, u32[]{:S(2)}, u32[]{:S(2)}) collective-permute-start(f32[80,256]{1,0:T(8,128)} %get-tuple-element.11), channel_id=1, source_target_pairs={{0,8},{8,0},{16,24},{24,16},{32,40},{40,32},{48,56},{56,48},{64,72... | collective-permute-start | bytes 245768 | tf_op jit(solution)/shard_map/ppermute | solution.py:531
  11.2 10.6 %collective-permute-start.1 = (f32[128,128]{1,0:T(8,128)}, f32[128,128]{1,0:T(8,128)S(1)}, u32[]{:S(2)}, u32[]{:S(2)}) collective-permute-start(f32[128,128]{1,0:T(8,128)} %get-tuple-element.10), channel_id=1, source_target_pairs={{1,2},{2,1},{3,4},{4,3},{5,6},{6,5},{9,10},{10,9},{11,12},{12,11},... | collective-permute-start | bytes 196616 | tf_op jit(solution)/shard_map/ppermute | solution.py:531
  15.9 5.9 %collective-permute-start.3 = (f32[128,128]{1,0:T(8,128)}, f32[128,128]{1,0:T(8,128)}, u32[]{:S(2)}, u32[]{:S(2)}) collective-permute-start(f32[128,128]{1,0:T(8,128)} %get-tuple-element.12), channel_id=1, source_target_pairs={{0,1},{1,0},{2,3},{3,2},{4,5},{5,4},{6,7},{7,6},{8,9},{9,8},{10,11... | collective-permute-start | bytes 196616 | tf_op jit(solution)/shard_map/ppermute | solution.py:531
  16.0 13.0 %all-to-all-start = ((f32[16,8,128]{2,1,0:T(8,128)}), f32[16,8,128]{2,1,0:T(8,128)}, u32[]{:S(2)}, u32[]{:S(2)}) async-start(f32[16,8,128]{2,1,0:T(8,128)} %get-tuple-element.15), calls=%async_computation | async-start | bytes 131072 | tf_op jit(solution)/shard_map/all_to_all | solution.py:537
  28.3 0.7 %copy-start.1 = (f32[8,48,256]{2,1,0:T(8,128)}, f32[8,48,256]{2,1,0:T(8,128)S(1)}, u32[]{:S(2)}) copy-start(f32[8,48,256]{2,1,0:T(8,128)S(1)} %get-tuple-element.14._) | copy-start | bytes 1179652
  30.5 14.3 %all-to-all-start.1 = ((f32[8,48,256]{2,1,0:T(8,128)}), f32[8,48,256]{2,1,0:T(8,128)}, u32[]{:S(2)}, u32[]{:S(2)}) async-start(f32[8,48,256]{2,1,0:T(8,128)} %insert_maximum.1), calls=%async_computation.1 | async-start | bytes 786432 | tf_op jit(solution)/shard_map/all_to_all | solution.py:539

commit v13 on v11

--- a/solution.py
+++ b/solution.py
@@ -18,7 +18,7 @@
 EXT = 24
 CHUNK = 32
 TALL = 16
-LIMA, LIMB = 48, 48
+LIMA, LIMB = 852, 768
 
 SPEED, WET, THICK, PART, COEF, EDGE, MESSAGE = 48, 60, 61, 64, 68, 72, 80
 ANY = pl.BlockSpec(memory_space=pl.ANY)
@@ -388,7 +388,7 @@
         out_shape=out_shape,
         scratch_shapes=scratch,
         input_output_aliases=aliases,
-        compiler_params=pltpu.CompilerParams(vmem_limit_bytes=(LIMA if first == 0 else LIMB) * 2**20),
+        compiler_params=pltpu.CompilerParams(vmem_limit_bytes=(LIMA if first == 0 else LIMB) * 2**16),
         cost_estimate=pl.CostEstimate(flops=24_000_000, bytes_accessed=9_400_000, transcendentals=0),
         name="advect_forcing" if first == 0 else "advect_rest",
     )(*operands)

time: 47.4 us -> 47.3 us (level)
  local copies, waits for them, and re-layouts: 0.75 us -> 0.01 us
  Pallas kernels: 22.6 us -> 23.3 us
    pallas_call x2, Pallas kernels: 12.9 us -> 13.6 us  [advect(): pl.pallas_call(functools.partial(advect_kernel, first), in_specs=ins, out...]
    unnamed x8 -> x6, local copies, waits for them, and re-layouts: 0.75 us -> 0.01 us
  transfers between devices with their start and end apart: 6 -> 6, of which waited for: 1 -> 1; matrix products, arithmetic and copies ran while one was open for 0% -> 0% of each run, Pallas kernels for 27% -> 29%
where the time goes in v13:
time: 47.3 us; the launch traced here: 47 us
  Pallas kernels  23.3 us (49%)
  starting transfers between devices  21.1 us (45%)
  waiting for transfers between devices  1.78 us (4%)
  between operations  0.76 us (2%)
    pallas_call x2, Pallas kernels, advect(): pl.pallas_call(functools.partial(advect_kernel, first), in_specs=ins, out...  13.6 us
    all_to_all x1, starting transfers between devices, shards(): tops = lax.all_to_all(top, 'bx', split_axis=0, concat_axis=0, tiled=True)  8.21 us
    ppermute x4, starting transfers between devices, exchange(): return lax.ppermute(x, axis, pairs)  7.87 us
    pallas_call x1, Pallas kernels, pack(): pl.pallas_call(pack_kernel, in_specs=[HBM] * 5, out_specs=[VMEM] * 5, out...  5.06 us
    all_to_all x1, starting transfers between devices, shards(): lax.all_to_all(insert(parcels, tops), 'by', split_axis=0, concat_axis=0,...  5 us
    pallas_call x1, Pallas kernels, solve(): pl.pallas_call(solve_kernel, in_specs=[VMEM], out_specs=VMEM, out_shape=f...  3.18 us
    all_to_all x1, waiting for transfers between devices, shards(): lax.all_to_all(insert(parcels, tops), 'by', split_axis=0, concat_axis=0,...  1.77 us
    pallas_call x1, Pallas kernels, insert(): pl.pallas_call(insert_kernel, in_specs=[HBM, VMEM], out_specs=HBM, out_sh...  1.45 us
  transfers between devices with their start and end apart: 6, of which 1 were waited for; matrix products, arithmetic and copies ran while one was open for 0% of the time, Pallas kernels for 29%

profile of v13, /device:TPU:1, one launch (start us, length us, event | category | flops | bytes accessed | tf_op | source)
XLA Modules:
  0.0 47.0 jit_solution(5392299156691450861)
XLA Ops:
  0.6 0.0 copy-start.1
  0.6 0.0 copy-start.2
  0.7 5.1 %pack_edges.1 = (f32[80,256]{1,0:T(8,128)}, f32[80,256]{1,0:T(8,128)}, f32[128,128]{1,0:T(8,128)}, f32[128,128]{1,0:T(8,128)}, f32[16,8,128]{2,1,0:T(8,128)}) custom-call(f32[12]{0:T(128)} %thick_hbm.1, f32[4,12,128,256]{3,2,1,0:T(8,128)} %refs_0_.3, f32[2,12,128,256]{3,2,1,0:T(8,128)} %refs_1_.3, s32[128,256]{1,0:T(8,128)} %refs_2_.3, f32[128,256]{1,0:T(8,128)} %refs_7_.1), custom_call_target="tpu_custom_call" | custom-call | flops 4000000 | bytes 7400000 | tf_op jit(solution)/shard_map/pack_edges/pallas_call | solution.py:172
  5.7 0.0 copy-start
  5.7 2.2 %collective-permute-start = (f32[80,256]{1,0:T(8,128)}, f32[80,256]{1,0:T(8,128)S(1)}, u32[]{:S(2)}, u32[]{:S(2)}) collective-permute-start(f32[80,256]{1,0:T(8,128)} %get-tuple-element.9), channel_id=1, source_target_pairs={{0,8},{8,0},{16,24},{24,16},{32,40},{40,32},{48,56},{56,48},{64,72... | collective-permute-start | bytes 245768 | tf_op jit(solution)/shard_map/ppermute | solution.py:531
  7.9 1.3 %collective-permute-start.1 = (f32[80,256]{1,0:T(8,128)}, f32[80,256]{1,0:T(8,128)}, u32[]{:S(2)}, u32[]{:S(2)}) collective-permute-start(f32[80,256]{1,0:T(8,128)} %get-tuple-element.10), channel_id=1, source_target_pairs={{8,16},{16,8},{24,32},{32,24},{40,48},{48,40},{56,64},{64,56},{72,... | collective-permute-start | bytes 245768 | tf_op jit(solution)/shard_map/ppermute | solution.py:531
  9.2 1.0 %collective-permute-start.2 = (f32[128,128]{1,0:T(8,128)}, f32[128,128]{1,0:T(8,128)S(1)}, u32[]{:S(2)}, u32[]{:S(2)}) collective-permute-start(f32[128,128]{1,0:T(8,128)} %get-tuple-element.11), channel_id=1, source_target_pairs={{0,1},{1,0},{2,3},{3,2},{4,5},{5,4},{6,7},{7,6},{8,9},{9,8},{10,11... | collective-permute-start | bytes 196616 | tf_op jit(solution)/shard_map/ppermute | solution.py:531
  10.2 3.4 %collective-permute-start.3 = (f32[128,128]{1,0:T(8,128)}, f32[128,128]{1,0:T(8,128)}, u32[]{:S(2)}, u32[]{:S(2)}) collective-permute-start(f32[128,128]{1,0:T(8,128)} %get-tuple-element.12), channel_id=1, source_target_pairs={{1,2},{2,1},{3,4},{4,3},{5,6},{6,5},{9,10},{10,9},{11,12},{12,11},... | collective-permute-start | bytes 196616 | tf_op jit(solution)/shard_map/ppermute | solution.py:531
  13.6 8.2 %all-to-all-start = ((f32[16,8,128]{2,1,0:T(8,128)}), f32[16,8,128]{2,1,0:T(8,128)}, u32[]{:S(2)}, u32[]{:S(2)}) async-start(f32[16,8,128]{2,1,0:T(8,128)} %get-tuple-element.15), calls=%async_computation | async-start | bytes 131072 | tf_op jit(solution)/shard_map/all_to_all | solution.py:538
  21.8 0.0 collective-permute-done.2.refs_5_
  21.8 0.0 collective-permute-done.3.refs_6_
  21.9 0.0 collective-permute-done.refs_3_
  21.9 0.0 collective-permute-done.1.refs_4_
  21.9 0.0 copy-done.1
  21.9 0.0 copy-done.2
  21.9 7.2 %advect_forcing.1 = (f32[4,12,128,256]{3,2,1,0:T(8,128)}, f32[8,48,256]{2,1,0:T(8,128)}) custom-call(f32[4,12,128,256]{3,2,1,0:T(8,128)} %refs_0_.3, f32[2,12,128,256]{3,2,1,0:T(8,128)} %refs_1_.3, s32[128,256]{1,0:T(8,128)S(1)} %copy-done.1, f32[80,256]{1,0:T(8,128)S(1)} %collective-permute-done.refs_3_, f32[80,256]{1,0:T(8,128)} %collective-permute-done.1.refs_4_, ...), custom_call_target="tpu_custom_call" | custom-call | flops 24000000 | bytes 9400000 | tf_op jit(solution)/shard_map/advect_forcing/pallas_call | solution.py:384
  29.1 0.0 all-to-all-done.tops
  29.1 1.5 %insert_maximum.1 = f32[8,48,256]{2,1,0:T(8,128)} custom-call(f32[8,48,256]{2,1,0:T(8,128)} %get-tuple-element.14._, f32[16,8,128]{2,1,0:T(8,128)} %all-to-all-done.tops), custom_call_target="tpu_custom_call", output_to_operand_aliasing={{}: (0, {})} | custom-call | flops 1000 | bytes 100000 | tf_op jit(solution)/shard_map/insert_maximum/pallas_call | solution.py:405
  30.6 5.0 %all-to-all-start.1 = ((f32[8,48,256]{2,1,0:T(8,128)}), f32[8,48,256]{2,1,0:T(8,128)}, u32[]{:S(2)}, u32[]{:S(2)}) async-start(f32[8,48,256]{2,1,0:T(8,128)} %insert_maximum.1), calls=%async_computation.1 | async-start | bytes 786432 | tf_op jit(solution)/shard_map/all_to_all | solution.py:540
  35.6 0.0 copy-done
  35.6 6.4 %advect_rest.1 = f32[4,12,128,256]{3,2,1,0:T(8,128)} custom-call(f32[4,12,128,256]{3,2,1,0:T(8,128)} %refs_0_.3, f32[2,12,128,256]{3,2,1,0:T(8,128)S(1)} %copy-done, s32[128,256]{1,0:T(8,128)S(1)} %copy-done.1, f32[80,256]{1,0:T(8,128)S(1)} %collective-permute-done.refs_3_, ...), custom_call_target="tpu_custom_call", output_to_operand_aliasing={{}: (7, {})} | custom-call | flops 24000000 | bytes 9400000 | tf_op jit(solution)/shard_map/advect_rest/pallas_call | solution.py:384
  42.0 1.8 %all-to-all-done.1.got_ref = f32[8,48,256]{2,1,0:T(8,128)} async-done(((f32[8,48,256]{2,1,0:T(8,128)}), f32[8,48,256]{2,1,0:T(8,128)}, u32[]{:S(2)}, u32[]{:S(2)}) %all-to-all-start.1) | async-done | bytes 393248 | tf_op jit(solution)/shard_map/all_to_all | solution.py:540
  43.8 3.2 %chebyshev.1 = f32[16,2048]{1,0:T(8,128)} custom-call(f32[8,48,256]{2,1,0:T(8,128)} %all-to-all-done.1.got_ref), custom_call_target="tpu_custom_call" | custom-call | flops 6000000 | bytes 600000 | tf_op jit(solution)/shard_map/chebyshev/pallas_call | solution.py:508
Async XLA Ops:
  0.6 21.2 %copy-start.1 = (s32[128,256]{1,0:T(8,128)S(1)}, s32[128,256]{1,0:T(8,128)}, u32[]{:S(2)}) copy-start(s32[128,256]{1,0:T(8,128)} %refs_2_.3) | copy-start | bytes 393220
  0.6 21.2 %copy-start.2 = (f32[128,256]{1,0:T(8,128)S(1)}, f32[128,256]{1,0:T(8,128)}, u32[]{:S(2)}) copy-start(f32[128,256]{1,0:T(8,128)} %refs_7_.1) | copy-start | bytes 393220
  5.7 29.9 %copy-start = (f32[2,12,128,256]{3,2,1,0:T(8,128)S(1)}, f32[2,12,128,256]{3,2,1,0:T(8,128)}, u32[]{:S(2)}) copy-start(f32[2,12,128,256]{3,2,1,0:T(8,128)} %refs_1_.3) | copy-start | bytes 9437188
  5.7 16.1 %collective-permute-start = (f32[80,256]{1,0:T(8,128)}, f32[80,256]{1,0:T(8,128)S(1)}, u32[]{:S(2)}, u32[]{:S(2)}) collective-permute-start(f32[80,256]{1,0:T(8,128)} %get-tuple-element.9), channel_id=1, source_target_pairs={{0,8},{8,0},{16,24},{24,16},{32,40},{40,32},{48,56},{56,48},{64,72... | collective-permute-start | bytes 245768 | tf_op jit(solution)/shard_map/ppermute | solution.py:531
  7.9 13.9 %collective-permute-start.1 = (f32[80,256]{1,0:T(8,128)}, f32[80,256]{1,0:T(8,128)}, u32[]{:S(2)}, u32[]{:S(2)}) collective-permute-start(f32[80,256]{1,0:T(8,128)} %get-tuple-element.10), channel_id=1, source_target_pairs={{8,16},{16,8},{24,32},{32,24},{40,48},{48,40},{56,64},{64,56},{72,... | collective-permute-start | bytes 245768 | tf_op jit(solution)/shard_map/ppermute | solution.py:531
  9.2 12.6 %collective-permute-start.2 = (f32[128,128]{1,0:T(8,128)}, f32[128,128]{1,0:T(8,128)S(1)}, u32[]{:S(2)}, u32[]{:S(2)}) collective-permute-start(f32[128,128]{1,0:T(8,128)} %get-tuple-element.11), channel_id=1, source_target_pairs={{0,1},{1,0},{2,3},{3,2},{4,5},{5,4},{6,7},{7,6},{8,9},{9,8},{10,11... | collective-permute-start | bytes 196616 | tf_op jit(solution)/shard_map/ppermute | solution.py:531
  10.2 11.7 %collective-permute-start.3 = (f32[128,128]{1,0:T(8,128)}, f32[128,128]{1,0:T(8,128)}, u32[]{:S(2)}, u32[]{:S(2)}) collective-permute-start(f32[128,128]{1,0:T(8,128)} %get-tuple-element.12), channel_id=1, source_target_pairs={{1,2},{2,1},{3,4},{4,3},{5,6},{6,5},{9,10},{10,9},{11,12},{12,11},... | collective-permute-start | bytes 196616 | tf_op jit(solution)/shard_map/ppermute | solution.py:531
  13.6 15.5 %all-to-all-start = ((f32[16,8,128]{2,1,0:T(8,128)}), f32[16,8,128]{2,1,0:T(8,128)}, u32[]{:S(2)}, u32[]{:S(2)}) async-start(f32[16,8,128]{2,1,0:T(8,128)} %get-tuple-element.15), calls=%async_computation | async-start | bytes 131072 | tf_op jit(solution)/shard_map/all_to_all | solution.py:538
  30.6 13.2 %all-to-all-start.1 = ((f32[8,48,256]{2,1,0:T(8,128)}), f32[8,48,256]{2,1,0:T(8,128)}, u32[]{:S(2)}, u32[]{:S(2)}) async-start(f32[8,48,256]{2,1,0:T(8,128)} %insert_maximum.1), calls=%async_computation.1 | async-start | bytes 786432 | tf_op jit(solution)/shard_map/all_to_all | solution.py:540

commit v14 on v11

--- a/solution.py
+++ b/solution.py
@@ -173,7 +173,7 @@
         pack_kernel,
         in_specs=[HBM] * 5,
         out_specs=[VMEM] * 5,
-        out_shape=[f32(MESSAGE, COLS), f32(MESSAGE, COLS), f32(ROWS, LANE), f32(ROWS, LANE), f32(16, 8, LANE)],
+        out_shape=[f32(MESSAGE, COLS), f32(MESSAGE, COLS), f32(ROWS, LANE), f32(ROWS, LANE), f32(16, 1, LANE)],
         scratch_shapes=[
             pltpu.VMEM((TRACERS, LEVELS, ROWS, COLS), jnp.float32),
             pltpu.VMEM(tile, jnp.float32),

time: 47.4 us -> 47.2 us (level)
  no operation moved by 1% of the time
where the time goes in v14:
time: 47.2 us; the launch traced here: 46.9 us
  Pallas kernels  22.5 us (48%)
  starting transfers between devices  21.1 us (45%)
  waiting for transfers between devices  1.8 us (4%)
  between operations  0.77 us (2%)
  local copies, waits for them, and re-layouts  0.75 us (2%)
    pallas_call x2, Pallas kernels, advect(): pl.pallas_call(functools.partial(advect_kernel, first), in_specs=ins, out...  12.9 us
    all_to_all x1, starting transfers between devices, shards(): tops = lax.all_to_all(top, 'bx', split_axis=0, concat_axis=0, tiled=True)  8.22 us
    ppermute x4, starting transfers between devices, exchange(): return lax.ppermute(x, axis, pairs)  7.87 us
    pallas_call x1, Pallas kernels, pack(): pl.pallas_call(pack_kernel, in_specs=[HBM] * 5, out_specs=[VMEM] * 5, out...  5.17 us
    all_to_all x1, starting transfers between devices, shards(): lax.all_to_all(insert(parcels, tops), 'by', split_axis=0, concat_axis=0,...  4.98 us
    pallas_call x1, Pallas kernels, solve(): pl.pallas_call(solve_kernel, in_specs=[VMEM], out_specs=VMEM, out_shape=f...  3.18 us
    all_to_all x1, waiting for transfers between devices, shards(): lax.all_to_all(insert(parcels, tops), 'by', split_axis=0, concat_axis=0,...  1.79 us
    pallas_call x1, Pallas kernels, insert(): pl.pallas_call(insert_kernel, in_specs=[HBM, VMEM], out_specs=HBM, out_sh...  1.29 us
  transfers between devices with their start and end apart: 6, of which 1 were waited for; matrix products, arithmetic and copies ran while one was open for 0% of the time, Pallas kernels for 27%

profile of v14, /device:TPU:1, one launch (start us, length us, event | category | flops | bytes accessed | tf_op | source)
XLA Modules:
  0.0 46.9 jit_solution(1265172636376344925)
XLA Ops:
  0.6 0.0 copy-start.2
  0.6 0.0 copy-start
  0.7 0.0 copy-start.3
  0.7 5.2 %pack_edges.1 = (f32[80,256]{1,0:T(8,128)}, f32[80,256]{1,0:T(8,128)}, f32[128,128]{1,0:T(8,128)}, f32[128,128]{1,0:T(8,128)}, f32[16,1,128]{2,1,0:T(1,128)}) custom-call(f32[12]{0:T(128)} %thick_hbm.1, f32[4,12,128,256]{3,2,1,0:T(8,128)} %refs_0_.3, f32[2,12,128,256]{3,2,1,0:T(8,128)} %refs_1_.3, s32[128,256]{1,0:T(8,128)} %refs_2_.3, f32[128,256]{1,0:T(8,128)} %refs_7_.1), custom_call_target="tpu_custom_call" | custom-call | flops 4000000 | bytes 7400000 | tf_op jit(solution)/shard_map/pack_edges/pallas_call | solution.py:172
  5.8 2.2 %collective-permute-start = (f32[80,256]{1,0:T(8,128)}, f32[80,256]{1,0:T(8,128)S(1)}, u32[]{:S(2)}, u32[]{:S(2)}) collective-permute-start(f32[80,256]{1,0:T(8,128)} %get-tuple-element.9), channel_id=1, source_target_pairs={{0,8},{8,0},{16,24},{24,16},{32,40},{40,32},{48,56},{56,48},{64,72... | collective-permute-start | bytes 245768 | tf_op jit(solution)/shard_map/ppermute | solution.py:531
  8.0 1.3 %collective-permute-start.1 = (f32[80,256]{1,0:T(8,128)}, f32[80,256]{1,0:T(8,128)}, u32[]{:S(2)}, u32[]{:S(2)}) collective-permute-start(f32[80,256]{1,0:T(8,128)} %get-tuple-element.10), channel_id=1, source_target_pairs={{8,16},{16,8},{24,32},{32,24},{40,48},{48,40},{56,64},{64,56},{72,... | collective-permute-start | bytes 245768 | tf_op jit(solution)/shard_map/ppermute | solution.py:531
  9.3 1.0 %collective-permute-start.2 = (f32[128,128]{1,0:T(8,128)}, f32[128,128]{1,0:T(8,128)S(1)}, u32[]{:S(2)}, u32[]{:S(2)}) collective-permute-start(f32[128,128]{1,0:T(8,128)} %get-tuple-element.11), channel_id=1, source_target_pairs={{0,1},{1,0},{2,3},{3,2},{4,5},{5,4},{6,7},{7,6},{8,9},{9,8},{10,11... | collective-permute-start | bytes 196616 | tf_op jit(solution)/shard_map/ppermute | solution.py:531
  10.3 3.4 %collective-permute-start.3 = (f32[128,128]{1,0:T(8,128)}, f32[128,128]{1,0:T(8,128)}, u32[]{:S(2)}, u32[]{:S(2)}) collective-permute-start(f32[128,128]{1,0:T(8,128)} %get-tuple-element.12), channel_id=1, source_target_pairs={{1,2},{2,1},{3,4},{4,3},{5,6},{6,5},{9,10},{10,9},{11,12},{12,11},... | collective-permute-start | bytes 196616 | tf_op jit(solution)/shard_map/ppermute | solution.py:531
  13.7 8.2 %all-to-all-start = ((f32[16,1,128]{2,1,0:T(1,128)}), f32[16,1,128]{2,1,0:T(1,128)}, u32[]{:S(2)}, u32[]{:S(2)}) async-start(f32[16,1,128]{2,1,0:T(1,128)} %get-tuple-element.15), calls=%async_computation | async-start | bytes 16384 | tf_op jit(solution)/shard_map/all_to_all | solution.py:538
  21.9 0.0 collective-permute-done.2.refs_5_
  21.9 0.0 collective-permute-done.3.refs_6_
  22.0 0.0 collective-permute-done.refs_3_
  22.0 0.0 collective-permute-done.1.refs_4_
  22.0 0.0 copy-done.2
  22.0 0.0 copy-done
  22.0 0.0 copy-done.3
  22.0 6.5 %advect_forcing.1 = (f32[4,12,128,256]{3,2,1,0:T(8,128)}, f32[8,48,256]{2,1,0:T(8,128)S(1)}) custom-call(f32[4,12,128,256]{3,2,1,0:T(8,128)} %refs_0_.3, f32[2,12,128,256]{3,2,1,0:T(8,128)S(1)} %copy-done, s32[128,256]{1,0:T(8,128)S(1)} %copy-done.2, f32[80,256]{1,0:T(8,128)S(1)} %collective-permute-done.refs_3_, f32[80,256]{1,0:T(8,128)} %collective-permute-done.1.refs_4_, ...), custom_call_target="tpu_custom_call" | custom-call | flops 24000000 | bytes 9400000 | tf_op jit(solution)/shard_map/advect_forcing/pallas_call | solution.py:384
  28.5 0.0 copy-start.1
  28.5 0.7 %copy-done.1 = f32[8,48,256]{2,1,0:T(8,128)} copy-done((f32[8,48,256]{2,1,0:T(8,128)}, f32[8,48,256]{2,1,0:T(8,128)S(1)}, u32[]{:S(2)}) %copy-start.1) | copy-done | bytes 393240
  29.2 0.0 all-to-all-done.tops
  29.2 1.3 %insert_maximum.1 = f32[8,48,256]{2,1,0:T(8,128)} custom-call(f32[8,48,256]{2,1,0:T(8,128)} %copy-done.1, f32[16,1,128]{2,1,0:T(1,128)} %all-to-all-done.tops), custom_call_target="tpu_custom_call", output_to_operand_aliasing={{}: (0, {})} | custom-call | flops 1000 | bytes 100000 | tf_op jit(solution)/shard_map/insert_maximum/pallas_call | solution.py:405
  30.5 5.0 %all-to-all-start.1 = ((f32[8,48,256]{2,1,0:T(8,128)}), f32[8,48,256]{2,1,0:T(8,128)}, u32[]{:S(2)}, u32[]{:S(2)}) async-start(f32[8,48,256]{2,1,0:T(8,128)} %insert_maximum.1), calls=%async_computation.1 | async-start | bytes 786432 | tf_op jit(solution)/shard_map/all_to_all | solution.py:540
  35.5 6.4 %advect_rest.1 = f32[4,12,128,256]{3,2,1,0:T(8,128)} custom-call(f32[4,12,128,256]{3,2,1,0:T(8,128)} %refs_0_.3, f32[2,12,128,256]{3,2,1,0:T(8,128)S(1)} %copy-done, s32[128,256]{1,0:T(8,128)S(1)} %copy-done.2, f32[80,256]{1,0:T(8,128)S(1)} %collective-permute-done.refs_3_, ...), custom_call_target="tpu_custom_call", output_to_operand_aliasing={{}: (7, {})} | custom-call | flops 24000000 | bytes 9400000 | tf_op jit(solution)/shard_map/advect_rest/pallas_call | solution.py:384
  41.9 1.8 %all-to-all-done.1.got_ref = f32[8,48,256]{2,1,0:T(8,128)} async-done(((f32[8,48,256]{2,1,0:T(8,128)}), f32[8,48,256]{2,1,0:T(8,128)}, u32[]{:S(2)}, u32[]{:S(2)}) %all-to-all-start.1) | async-done | bytes 393248 | tf_op jit(solution)/shard_map/all_to_all | solution.py:540
  43.7 3.2 %chebyshev.1 = f32[16,2048]{1,0:T(8,128)} custom-call(f32[8,48,256]{2,1,0:T(8,128)} %all-to-all-done.1.got_ref), custom_call_target="tpu_custom_call" | custom-call | flops 6000000 | bytes 600000 | tf_op jit(solution)/shard_map/chebyshev/pallas_call | solution.py:508
Async XLA Ops:
  0.6 21.4 %copy-start.2 = (s32[128,256]{1,0:T(8,128)S(1)}, s32[128,256]{1,0:T(8,128)}, u32[]{:S(2)}) copy-start(s32[128,256]{1,0:T(8,128)} %refs_2_.3) | copy-start | bytes 393220
  0.6 21.4 %copy-start = (f32[2,12,128,256]{3,2,1,0:T(8,128)S(1)}, f32[2,12,128,256]{3,2,1,0:T(8,128)}, u32[]{:S(2)}) copy-start(f32[2,12,128,256]{3,2,1,0:T(8,128)} %refs_1_.3) | copy-start | bytes 9437188
  0.7 21.4 %copy-start.3 = (f32[128,256]{1,0:T(8,128)S(1)}, f32[128,256]{1,0:T(8,128)}, u32[]{:S(2)}) copy-start(f32[128,256]{1,0:T(8,128)} %refs_7_.1) | copy-start | bytes 393220
  5.8 16.1 %collective-permute-start = (f32[80,256]{1,0:T(8,128)}, f32[80,256]{1,0:T(8,128)S(1)}, u32[]{:S(2)}, u32[]{:S(2)}) collective-permute-start(f32[80,256]{1,0:T(8,128)} %get-tuple-element.9), channel_id=1, source_target_pairs={{0,8},{8,0},{16,24},{24,16},{32,40},{40,32},{48,56},{56,48},{64,72... | collective-permute-start | bytes 245768 | tf_op jit(solution)/shard_map/ppermute | solution.py:531
  8.0 13.9 %collective-permute-start.1 = (f32[80,256]{1,0:T(8,128)}, f32[80,256]{1,0:T(8,128)}, u32[]{:S(2)}, u32[]{:S(2)}) collective-permute-start(f32[80,256]{1,0:T(8,128)} %get-tuple-element.10), channel_id=1, source_target_pairs={{8,16},{16,8},{24,32},{32,24},{40,48},{48,40},{56,64},{64,56},{72,... | collective-permute-start | bytes 245768 | tf_op jit(solution)/shard_map/ppermute | solution.py:531
  9.3 12.6 %collective-permute-start.2 = (f32[128,128]{1,0:T(8,128)}, f32[128,128]{1,0:T(8,128)S(1)}, u32[]{:S(2)}, u32[]{:S(2)}) collective-permute-start(f32[128,128]{1,0:T(8,128)} %get-tuple-element.11), channel_id=1, source_target_pairs={{0,1},{1,0},{2,3},{3,2},{4,5},{5,4},{6,7},{7,6},{8,9},{9,8},{10,11... | collective-permute-start | bytes 196616 | tf_op jit(solution)/shard_map/ppermute | solution.py:531
  10.3 11.7 %collective-permute-start.3 = (f32[128,128]{1,0:T(8,128)}, f32[128,128]{1,0:T(8,128)}, u32[]{:S(2)}, u32[]{:S(2)}) collective-permute-start(f32[128,128]{1,0:T(8,128)} %get-tuple-element.12), channel_id=1, source_target_pairs={{1,2},{2,1},{3,4},{4,3},{5,6},{6,5},{9,10},{10,9},{11,12},{12,11},... | collective-permute-start | bytes 196616 | tf_op jit(solution)/shard_map/ppermute | solution.py:531
  13.7 15.5 %all-to-all-start = ((f32[16,1,128]{2,1,0:T(1,128)}), f32[16,1,128]{2,1,0:T(1,128)}, u32[]{:S(2)}, u32[]{:S(2)}) async-start(f32[16,1,128]{2,1,0:T(1,128)} %get-tuple-element.15), calls=%async_computation | async-start | bytes 16384 | tf_op jit(solution)/shard_map/all_to_all | solution.py:538
  28.5 0.7 %copy-start.1 = (f32[8,48,256]{2,1,0:T(8,128)}, f32[8,48,256]{2,1,0:T(8,128)S(1)}, u32[]{:S(2)}) copy-start(f32[8,48,256]{2,1,0:T(8,128)S(1)} %get-tuple-element.14._) | copy-start | bytes 1179652
  30.5 13.2 %all-to-all-start.1 = ((f32[8,48,256]{2,1,0:T(8,128)}), f32[8,48,256]{2,1,0:T(8,128)}, u32[]{:S(2)}, u32[]{:S(2)}) async-start(f32[8,48,256]{2,1,0:T(8,128)} %insert_maximum.1), calls=%async_computation.1 | async-start | bytes 786432 | tf_op jit(solution)/shard_map/all_to_all | solution.py:540
